TPU v7x, 32 devices: a whole 2x2x4 slice. The times are simulated.
32 devices in a mesh: fsdp: 8 (over y, x, core), seq: 4 (over z).
Axes of the slice: x: 2, y: 2, z: 4, core: 2. Of those that a mesh axis runs over, the one named last changes fastest.
Arguments:
- streams: bfloat16 [3, 2048, 4096], P(None, 'seq', 'fsdp'), may hold values from -6 to 6
- record_blocks: int32 [3], replicated, may hold values from 1 to 8, as said below
- tail_rows: int32 [3], replicated, may hold values from 1 to 128
- unit_dest: int32 [128], replicated, may hold values from 0 to 127, as said below
- mixer_filter: float32 [128, 4096], P(None, ('fsdp', 'seq')), may hold values from -0.5 to 0.5
- feat_filter: float32 [7, 3, 4096], P(None, None, ('fsdp', 'seq')), may hold values from -2 to 2
- norm_gain: float32 [4096], P(('fsdp', 'seq')), may hold values from 0.25 to 1.75
- out_grad: bfloat16 [2048, 4096], P('seq', 'fsdp'), may hold values from -6 to 6
Outputs:
- out: bfloat16 [2048, 4096], P('seq', 'fsdp')
- stream_grad: bfloat16 [3, 2048, 4096], P(None, 'seq', 'fsdp')
- mixer_grad: float32 [128, 4096], P(None, ('fsdp', 'seq'))
- feat_grad: float32 [7, 3, 4096], P(None, None, ('fsdp', 'seq'))
- gain_grad: float32 [4096], P(('fsdp', 'seq'))
Inputs may be any that keep to these rules, and one draw needn't show every extreme that they name: unit_dest is a permutation; the 32 units of each shard of 512 rows go to exactly half of the shards, 16 units to each of them, so each shard receives 16 units from each of half of the shards. record_blocks sums to 16; the second record is the longest, exactly 8 blocks.
All inputs are finite; a program needn't handle non-finite values.
Results may differ from a plain program's by a relative error of at most 0.0085.
Values may be sent and summed in bfloat16 or wider, within the bound.
No kernel may reach another device: no remote copies, remote signals or barrier semaphores. Data moves between devices by JAX's collectives and lax.ppermute only.
A program may use at most 128 MiB of HBM per device.

v0:
```python
import jax
import jax.numpy as jnp
import numpy as np
from jax import lax
from jax.sharding import PartitionSpec as P

C = 4096
KM = 128
KF = 7
UNIT = 16


EPSILON = 1e-06


def from_behind(array, axis, by):
    length = lax.axis_size(axis)
    pairs = [(i, i + by) for i in range(length) if 0 <= i + by < length]
    return lax.ppermute(array, axis, pairs)


def lag_table(length):
    row_index = np.arange(length)[:, None]
    col_index = np.arange(2 * length)[None, :]
    lagged = length + row_index - col_index
    return np.where((lagged >= 0) & (lagged < length), lagged, length).astype(np.int32)


def toeplitz(filter_bf):
    padded = jnp.concatenate(
        [filter_bf.T, jnp.zeros((filter_bf.shape[1], 1), filter_bf.dtype)], axis=1
    )
    return jnp.take(padded, jnp.asarray(lag_table(filter_bf.shape[0])), axis=1)


def record_masks(record_blocks, tail_rows, first_block, block_count):
    starts = jnp.cumsum(record_blocks) - record_blocks
    record_ends = starts + record_blocks - 1
    block_ids = first_block + jnp.arange(block_count, dtype=jnp.int32)
    starts_here = jnp.any(starts[None, :] == block_ids[:, None], axis=1)
    starts_next = jnp.any(starts[None, :] == block_ids[:, None] + 1, axis=1)
    closing = record_ends[None, :] == block_ids[:, None]
    filled_rows = jnp.where(
        jnp.any(closing, axis=1), jnp.sum(jnp.where(closing, tail_rows[None, :], 0), axis=1), KM
    )
    live_rows = (jnp.arange(KM, dtype=jnp.int32)[None, :] < filled_rows[:, None]).astype(
        jnp.float32
    )
    carry_on = 1.0 - starts_here.astype(jnp.float32)
    carry_next = 1.0 - starts_next.astype(jnp.float32)
    return (carry_on, carry_next, live_rows)


def routing(unit_dest, position, shards, per_shard, capacity):
    target_shard = (unit_dest // per_shard).reshape(shards, per_shard)
    unit_ids = jnp.arange(per_shard, dtype=jnp.int32)
    earlier = unit_ids[None, :] < unit_ids[:, None]
    same_target = target_shard[:, :, None] == target_shard[:, None, :]
    rank_within = jnp.sum(jnp.where(same_target & earlier[None], 1, 0), axis=2).astype(jnp.int32)
    own_target = lax.dynamic_index_in_dim(target_shard, position, 0, keepdims=False)
    own_rank = lax.dynamic_index_in_dim(rank_within, position, 0, keepdims=False)
    own_slot = own_target * capacity + own_rank
    slot_ids = jnp.arange(shards * capacity, dtype=jnp.int32)
    send_match = own_slot[None, :] == slot_ids[:, None]
    send_source = jnp.sum(jnp.where(send_match, unit_ids[None, :], 0), axis=1)
    send_filled = jnp.any(send_match, axis=1)
    arrive_slot = (jnp.arange(shards, dtype=jnp.int32)[:, None] * capacity + rank_within).reshape(
        -1
    )
    wanted = position * per_shard + unit_ids
    arrive_match = unit_dest[None, :] == wanted[:, None]
    packed_slot = jnp.sum(jnp.where(arrive_match, arrive_slot[None, :], 0), axis=1)
    back_match = packed_slot[None, :] == slot_ids[:, None]
    back_source = jnp.sum(jnp.where(back_match, unit_ids[None, :], 0), axis=1)
    back_filled = jnp.any(back_match, axis=1)
    return (send_source, send_filled, packed_slot, back_source, back_filled, own_slot)


def move_units(values, source, filled, shards):
    unit_rows = values.reshape(values.shape[0], -1, UNIT, values.shape[2])
    picked = jnp.take(unit_rows, source, axis=1)
    picked = jnp.where(filled[None, :, None, None], picked, jnp.zeros_like(picked))
    return picked.reshape(values.shape[0], shards, -1, values.shape[2])


def featurize(extended, feat_taps, live_rows):
    accumulated = jnp.zeros(extended.shape[:2] + (KM, extended.shape[3]), jnp.float32)
    for tap_index in range(KF):
        window = extended[:, :, 8 - tap_index : 8 - tap_index + KM].astype(jnp.float32)
        accumulated = accumulated + feat_taps[tap_index][:, None, None, :] * window
    return (accumulated * live_rows[None, :, :, None]).astype(jnp.bfloat16)


def spread(d_extended, feat_taps):
    accumulated = jnp.zeros(d_extended.shape[:2] + (KM, d_extended.shape[3]), jnp.float32)
    for tap_index in range(KF):
        window = d_extended[:, :, tap_index : tap_index + KM].astype(jnp.float32)
        accumulated = accumulated + feat_taps[tap_index][:, None, None, :] * window
    return accumulated.astype(jnp.bfloat16)


def tap_sums(d_feature, extended):
    d_float = d_feature.astype(jnp.float32)
    collected = []
    for tap_index in range(KF):
        window = extended[:, :, 8 - tap_index : 8 - tap_index + KM].astype(jnp.float32)
        collected.append(jnp.sum(d_float * window, axis=(1, 2)))
    return jnp.stack(collected)


def lag_sums(d_response, both_parts):
    channels = d_response.shape[2]
    group_width = min(32, channels)
    collected = []
    for start_col in range(0, channels, group_width):
        products = jnp.einsum(
            "bic,bkc->cik",
            d_response[:, :, start_col : start_col + group_width],
            both_parts[:, :, start_col : start_col + group_width],
            preferred_element_type=jnp.float32,
        )
        flattened = jnp.pad(products.reshape(group_width, 2 * KM * KM), ((0, 0), (0, KM)))
        skewed = flattened.reshape(group_width, KM, 2 * KM + 1)
        summed = jnp.sum(skewed[:, :, 1 : KM + 1], axis=1)
        collected.append(summed[:, ::-1].T)
    return jnp.concatenate(collected, axis=1)


def body(
    streams, record_blocks, tail_rows, unit_dest, mixer_filter, feat_filter, norm_gain, out_grad
):
    rows_dev = streams.shape[1]
    channels = streams.shape[2]
    shards = lax.axis_size("seq")
    position = lax.axis_index("seq")
    per_shard = rows_dev // UNIT
    capacity = 2 * per_shard // shards
    blocks_dev = rows_dev // KM
    send_source, send_filled, packed_slot, back_source, back_filled, own_slot = routing(
        unit_dest, position, shards, per_shard, capacity
    )
    outgoing = move_units(streams, send_source, send_filled, shards)
    arrived = lax.all_to_all(outgoing, "seq", split_axis=1, concat_axis=1, tiled=True)
    packed = jnp.take(arrived.reshape(3, -1, UNIT, channels), packed_slot, axis=1).reshape(
        3, blocks_dev, KM, channels
    )
    carry_on, carry_next, live_rows = record_masks(
        record_blocks, tail_rows, position * blocks_dev, blocks_dev
    )
    mixer_panel, feat_panel, gain_panel = (
        lax.all_gather(mixer_filter, "seq", axis=1, tiled=True),
        lax.all_gather(feat_filter, "seq", axis=2, tiled=True),
        lax.all_gather(norm_gain, "seq", axis=0, tiled=True),
    )
    rim_rows = from_behind(packed[:, blocks_dev - 1, KM - 8 :, :], "seq", 1)
    tail_part = jnp.concatenate([rim_rows[:, None], packed[:, : blocks_dev - 1, KM - 8 :]], axis=1)
    tail_part = jnp.where(carry_on[None, :, None, None] > 0, tail_part, jnp.zeros_like(tail_part))
    extended = jnp.concatenate([tail_part, packed], axis=2)
    feature = featurize(extended, feat_panel, live_rows)
    mixed_in = (feature[1].astype(jnp.float32) * feature[2].astype(jnp.float32)).astype(
        jnp.bfloat16
    )
    matrix = toeplitz(mixer_panel.astype(jnp.bfloat16))
    rim_mixed = from_behind(mixed_in[blocks_dev - 1], "seq", 1)
    previous = jnp.concatenate([rim_mixed[None], mixed_in[: blocks_dev - 1]], axis=0)
    previous = jnp.where(carry_on[:, None, None] > 0, previous, jnp.zeros_like(previous))
    response = jnp.einsum(
        "cik,bkc->bic", matrix[:, :, KM:], mixed_in, preferred_element_type=jnp.float32
    )
    response = response + jnp.einsum(
        "cik,bkc->bic", matrix[:, :, :KM], previous, preferred_element_type=jnp.float32
    )
    gated_out = (feature[0].astype(jnp.float32) * response).astype(jnp.bfloat16)
    gated_float = gated_out.astype(jnp.float32)
    squares = lax.psum(jnp.sum(gated_float * gated_float, axis=-1), "fsdp")
    row_scale = live_rows * lax.rsqrt(squares / C + EPSILON)
    normed = gated_float * row_scale[..., None]
    out = (normed * gain_panel).astype(jnp.bfloat16).reshape(rows_dev, channels)
    mixer_back, feat_back, gain_back = (
        lax.all_gather(mixer_filter, "seq", axis=1, tiled=True),
        lax.all_gather(feat_filter, "seq", axis=2, tiled=True),
        lax.all_gather(norm_gain, "seq", axis=0, tiled=True),
    )
    matrix_back = toeplitz(mixer_back.astype(jnp.bfloat16))
    grad_rows = out_grad.reshape(blocks_dev, KM, channels).astype(jnp.float32)
    gain_term = jnp.sum(grad_rows * normed, axis=(0, 1))
    weighted = grad_rows * gain_back
    inner_sum = lax.psum(jnp.sum(weighted * normed, axis=-1), "fsdp") / C
    d_gated = (row_scale[..., None] * (weighted - normed * inner_sum[..., None])).astype(
        jnp.bfloat16
    )
    d_gated_float = d_gated.astype(jnp.float32)
    d_query = d_gated_float * response
    d_response = (d_gated_float * feature[0].astype(jnp.float32)).astype(jnp.bfloat16)
    response_rim = from_behind(d_response[0], "seq", -1)
    following = jnp.concatenate([d_response[1:], response_rim[None]], axis=0)
    following = jnp.where(carry_next[:, None, None] > 0, following, jnp.zeros_like(following))
    d_mixed = jnp.einsum(
        "cik,bic->bkc", matrix_back[:, :, KM:], d_response, preferred_element_type=jnp.float32
    )
    d_mixed = d_mixed + jnp.einsum(
        "cik,bic->bkc", matrix_back[:, :, :KM], following, preferred_element_type=jnp.float32
    )
    d_feature = jnp.stack(
        [
            d_query,
            d_mixed * feature[2].astype(jnp.float32),
            d_mixed * feature[1].astype(jnp.float32),
        ]
    ).astype(jnp.bfloat16)
    mixer_term = lag_sums(d_response, jnp.concatenate([previous, mixed_in], axis=1))
    feat_term = tap_sums(d_feature, extended)
    feature_rim = from_behind(d_feature[:, 0, :8, :], "seq", -1)
    head_rows = jnp.concatenate([d_feature[:, 1:, :8], feature_rim[:, None]], axis=1)
    head_rows = jnp.where(carry_next[None, :, None, None] > 0, head_rows, jnp.zeros_like(head_rows))
    d_extended = jnp.concatenate([d_feature, head_rows], axis=2)
    d_packed = spread(d_extended, feat_back).reshape(3, rows_dev, channels)
    returning = move_units(d_packed, back_source, back_filled, shards)
    returned = lax.all_to_all(returning, "seq", split_axis=1, concat_axis=1, tiled=True)
    stream_grad = jnp.take(returned.reshape(3, -1, UNIT, channels), own_slot, axis=1).reshape(
        3, rows_dev, channels
    )
    mixer_whole, feat_whole, gain_whole = lax.psum((mixer_term, feat_term, gain_term), "seq")
    piece_width = channels // shards
    first_col = position * piece_width
    mixer_grad = lax.dynamic_slice_in_dim(mixer_whole, first_col, piece_width, 1)
    feat_grad = lax.dynamic_slice_in_dim(feat_whole, first_col, piece_width, 2)
    gain_grad = lax.dynamic_slice_in_dim(gain_whole, first_col, piece_width, 0)
    return (out, stream_grad, mixer_grad, feat_grad, gain_grad)


def solution(mesh):
    placed = (
        P(None, "seq", "fsdp"),
        P(),
        P(),
        P(),
        P(None, ("fsdp", "seq")),
        P(None, None, ("fsdp", "seq")),
        P(("fsdp", "seq")),
        P("seq", "fsdp"),
    )
    return jax.shard_map(
        body,
        mesh=mesh,
        in_specs=placed,
        out_specs=(
            P("seq", "fsdp"),
            P(None, "seq", "fsdp"),
            P(None, ("fsdp", "seq")),
            P(None, None, ("fsdp", "seq")),
            P(("fsdp", "seq")),
        ),
        check_vma=False,
    )
```

profile of v0, /device:TPU:0, one launch (start us, length us, event | category | flops | bytes accessed | tf_op | source)
XLA Modules:
  0.0 894.1 jit_solution(3491635460898840194)
XLA Ops:
  24.5 76.1 %all_gather.12 = f32[7,3,512]{2,0,1:T(8,128)S(1)} all-gather(f32[7,3,128]{2,0,1:T(8,128)S(1)} %copy-done.64), channel_id=1, replica_groups=mesh['fsdp'=8,'seq'=4] {'seq'}, dimensions={2}, use_global_device_ids=true | all-gather | bytes 53760 | tf_op jit(solution)/shard_map/all_gather | solution.py:152
  117.4 22.6 %fusion.28 = bf16[3,4,128,512]{2,1,3,0:T(4,128)(2,1)S(1)} fusion(bf16[3,4,128,512]{2,1,3,0:T(4,128)(2,1)S(1)} %copy.169, f32[4,128]{1,0:T(4,128)S(1)} %fusion.117, f32[3,512]{1,0:T(4,128)S(1)} %get-tuple-element.72, f32[3,512]{1,0:T(4,128)S(1)} %get-tuple-element.73, f32[3,512]{1,0:T(4,128)S(1)} %get-tuple-element.74, f32[3,512]{1,0:T(4,128)S(1)} %get-tuple-element.75, ...), kind=kLoop, calls=%fused_computation.60 | loop fusion | flops 31457280 | bytes 3289088 | tf_op jit(solution)/shard_map/convert_element_type | solution.py:91
  145.9 12.3 %all_gather.13 = bf16[128,512]{1,0:T(8,128)(2,1)S(1)} all-gather(bf16[128,128]{1,0:T(8,128)(2,1)S(1)} %convert.55), channel_id=1, replica_groups=mesh['fsdp'=8,'seq'=4] {'seq'}, dimensions={1}, use_global_device_ids=true | all-gather | bytes 163840 | tf_op jit(solution)/shard_map/all_gather | solution.py:151
  158.2 131.2 %gather_fusion.2 = bf16[32768,512]{1,0:T(8,128)(2,1)} fusion(bf16[512,129]{0,1:T(8,128)(2,1)S(1)} %concatenate.32, s32[32768]{0:T(1024)S(1)} %broadcast_clamp_fusion), kind=kCustom, calls=%fused_computation.2.clone | custom fusion | bytes 67239936 | tf_op jit(solution)/shard_map/jit(_take)/gather | solution.py:33
  289.4 45.4 %copy.198 = bf16[128,256,512]{1,0,2:T(8,128)(2,1)} copy(bf16[128,256,512]{2,1,0:T(8,128)(2,1)} %bitcast.233) | data formatting | bytes 67108864 | tf_op jit(solution)/shard_map/jit(_take)/gather | solution.py:33
  335.1 8.3 all-gather
  344.8 12.2 %fusion.2 = f32[512,4,128]{2,1,0:T(4,128)S(1)} fusion(bf16[4,128,512]{1,0,2:T(4,128)(2,1)S(1)} %maximum_select_fusion, bf16[512,128,256]{2,1,0:T(8,128)(2,1)} %bitcast.234), kind=kOutput, calls=%fused_computation.7 | convolution fusion | flops 67108864 | bytes 18350080 | tf_op jit(solution)/shard_map/cik,bkc->bic/dot_general | solution.py:170
  357.0 13.1 %fusion.56 = (f32[4,128]{1,0:T(4,128)S(1)}, bf16[4,128,512]{1,0,2:T(4,128)(2,1)S(1)}, f32[4,128,512]{1,0,2:T(4,128)}) fusion(bf16[3,4,128,512]{2,1,3,0:T(4,128)(2,1)} %copy-done.8, f32[512,4,128]{2,1,0:T(4,128)S(1)} %fusion.2, bf16[4,128,512]{1,0,2:T(4,128)(2,1)S(1)} %fusion.61, bf16[512,128,256]{2,1,0:T(8,128)(2,1)} %bitcast.235), kind=kOutput, calls=%fused_computation.138 | convolution fusion | flops 68943360 | bytes 20449280 | tf_op jit(solution)/shard_map/cik,bkc->bic/dot_general | solution.py:167
  370.2 12.3 %psum.35 = f32[4,128]{1,0:T(4,128)S(1)} all-reduce(f32[4,128]{1,0:T(4,128)S(1)} %get-tuple-element.51), channel_id=1, replica_groups=mesh['fsdp'=8,'seq'=4] {'fsdp'}, use_global_device_ids=true, to_apply=%region_9.13 | all-reduce | flops 512 | bytes 4096 | tf_op jit(solution)/shard_map/psum | solution.py:175
  387.1 11.9 %psum.36 = f32[4,128]{1,0:T(4,128)S(1)} all-reduce(f32[4,128]{1,0:T(4,128)S(1)} %get-tuple-element.40), channel_id=1, replica_groups=mesh['fsdp'=8,'seq'=4] {'fsdp'}, use_global_device_ids=true, to_apply=%region_12.16 | all-reduce | flops 512 | bytes 4096 | tf_op jit(solution)/shard_map/psum | solution.py:188
  419.9 8.1 reshape.315
  453.9 8.1 reshape.317
  487.9 8.4 reshape.321
  522.1 8.1 reshape.325
  539.1 8.0 reshape.327
  556.0 8.2 reshape.329
  590.0 8.4 reshape.333
  624.1 8.1 reshape.337
  668.8 8.4 fusion
  677.2 8.2 fusion.60
  685.5 31.5 %fusion.26 = (f32[3,512]{1,0:T(4,128)}, f32[3,512]{1,0:T(4,128)}, f32[3,512]{1,0:T(4,128)}, f32[3,512]{1,0:T(4,128)}, f32[3,512]{1,0:T(4,128)}, /*index=5*/f32[3,512]{1,0:T(4,128)}, bf16[3,4,128,512]{2,1,3,0:T(4,128)(2,1)S(1)}) fusion(bf16[3,4,128,512]{2,1,3,0:T(4,128)(2,1)S(1)} %copy-done.3, bf16[3,4,8,512]{2,1,3,0:T(4,128)(2,1)S(1)} %copy-done.5, ...), kind=kLoop, calls=%fused_computation.54 | loop fusion | flops 33807360 | bytes 4853760 | tf_op jit(solution)/shard_map/reduce_sum | solution.py:107
  732.1 8.2 reshape.343
  752.7 18.4 %fusion.27 = bf16[3,4,128,512]{2,1,3,0:T(4,128)(2,1)} fusion(bf16[3,4,128,512]{2,1,3,0:T(4,128)(2,1)S(1)} %get-tuple-element.46, bf16[3,4,136,512]{2,1,3,0:T(4,128)(2,1)S(1)} %pad_maximum_fusion, f32[3,512]{1,0:T(4,128)S(1)} %copy-done.20, f32[3,512]{1,0:T(4,128)S(1)} %copy-done.22, f32[3,512]{1,0:T(4,128)S(1)} %copy-done.24, f32[3,512]{1,0:T(4,128)S(1)} %copy-done.26, ...), kind=kLoop, calls=%fused_computation.59 | loop fusion | flops 16515072 | bytes 12625920 | tf_op jit(solution)/shard_map/convert_element_type | solution.py:99
  807.8 68.3 %all-reduce.17 = (f32[7,3,512]{2,1,0:T(4,128)S(1)}, f32[512]{0:T(512)S(1)}) all-reduce(f32[7,3,512]{2,1,0:T(4,128)S(1)} %constant_dynamic-update-slice_fusion.16, f32[512]{0:T(512)S(1)} %copy-done.65), channel_id=1, replica_groups=mesh['fsdp'=8,'seq'=4] {'seq'}, use_global_device_ids=true, to_apply=%region_39.43 | all-reduce | flops 11264 | bytes 90112 | tf_op jit(solution)/shard_map/psum | solution.py:223
  (387 shorter events, 324.4 us)
Async XLA Ops:
  17.8 83.4 %copy-start.74 = (s32[3]{0:T(128)S(1)}, s32[3]{0:T(128)}, u32[]{:S(2)}) copy-start(s32[3]{0:T(128)} %param.18) | copy-start | bytes 40
  17.8 84.5 %copy-start.18 = (s32[32768]{0:T(1024)S(1)}, s32[32768]{0:T(1024)}, u32[]{:S(2)}) copy-start(s32[32768]{0:T(1024)} %constant.141) | copy-start | bytes 393220
  17.8 84.6 %all-to-all-start = ((bf16[3,4,256,512]{3,2,0,1:T(8,128)(2,1)}), bf16[3,4,256,512]{3,2,0,1:T(8,128)(2,1)}, u32[]{:S(2)}, u32[]{:S(2)}) async-start(bf16[3,4,256,512]{3,2,0,1:T(8,128)(2,1)} %copy.166), calls=%async_computation | async-start | bytes 6291456 | tf_op jit(solution)/shard_map/all_to_all | solution.py:143
  102.2 15.1 %copy-start.19 = (f32[3,512]{1,0:T(4,128)}, f32[3,512]{1,0:T(4,128)S(1)}, u32[]{:S(2)}) copy-start(f32[3,512]{1,0:T(4,128)S(1)} %get-tuple-element.72) | copy-start | bytes 18436
  102.3 15.1 %copy-start.21 = (f32[3,512]{1,0:T(4,128)}, f32[3,512]{1,0:T(4,128)S(1)}, u32[]{:S(2)}) copy-start(f32[3,512]{1,0:T(4,128)S(1)} %get-tuple-element.73) | copy-start | bytes 18436
  102.3 15.1 %copy-start.23 = (f32[3,512]{1,0:T(4,128)}, f32[3,512]{1,0:T(4,128)S(1)}, u32[]{:S(2)}) copy-start(f32[3,512]{1,0:T(4,128)S(1)} %get-tuple-element.74) | copy-start | bytes 18436
  102.3 15.1 %copy-start.25 = (f32[3,512]{1,0:T(4,128)}, f32[3,512]{1,0:T(4,128)S(1)}, u32[]{:S(2)}) copy-start(f32[3,512]{1,0:T(4,128)S(1)} %get-tuple-element.75) | copy-start | bytes 18436
  102.3 15.0 %copy-start.27 = (f32[3,512]{1,0:T(4,128)}, f32[3,512]{1,0:T(4,128)S(1)}, u32[]{:S(2)}) copy-start(f32[3,512]{1,0:T(4,128)S(1)} %get-tuple-element.76) | copy-start | bytes 18436
  102.3 15.0 %copy-start.29 = (f32[3,512]{1,0:T(4,128)}, f32[3,512]{1,0:T(4,128)S(1)}, u32[]{:S(2)}) copy-start(f32[3,512]{1,0:T(4,128)S(1)} %get-tuple-element.77) | copy-start | bytes 18436
  110.5 4.3 collective-permute-start
  113.6 26.3 %copy-start.31 = (f32[1,3,512]{2,1,0:T(4,128)}, f32[1,3,512]{2,1,0:T(4,128)S(1)}, u32[]{:S(2)}) copy-start(f32[1,3,512]{2,1,0:T(4,128)S(1)} %copy.229) | copy-start | bytes 18436
  117.3 24.1 %copy-start.4 = (bf16[3,4,8,512]{2,1,3,0:T(4,128)(2,1)}, bf16[3,4,8,512]{2,1,3,0:T(4,128)(2,1)S(1)}, u32[]{:S(2)}) copy-start(bf16[3,4,8,512]{2,1,3,0:T(4,128)(2,1)S(1)} %copy.171) | copy-start | bytes 294916
  141.8 202.2 %collective-permute-start.1 = (bf16[128,512]{1,0:T(8,128)(2,1)S(1)}, bf16[128,512]{1,0:T(8,128)(2,1)S(1)}, u32[]{:S(2)}, u32[]{:S(2)}) collective-permute-start(bf16[128,512]{1,0:T(8,128)(2,1)S(1)} %bitcast.291), channel_id=1, source_target_pairs={{0,1},{1,2},{2,3},{4,5},{5,6},{6,7},{8,9},{9,10},{10,11},{12,13},{... | collective-permute-start | bytes 393224 | tf_op jit(solution)/shard_map/ppermute | solution.py:19
  289.4 45.4 %copy-start.14 = (bf16[512,512]{1,0:T(8,128)(2,1)S(1)}, bf16[512,512]{1,0:T(8,128)(2,1)}, u32[]{:S(2)}) copy-start(bf16[512,512]{1,0:T(8,128)(2,1)} %param.23) | copy-start | bytes 1572868
  289.4 45.7 %copy-start.72 = (f32[128]{0:T(128)S(1)}, f32[128]{0:T(128)}, u32[]{:S(2)}) copy-start(f32[128]{0:T(128)} %param.22) | copy-start | bytes 1540
  403.7 258.3 %copy-start.11 = (bf16[4,128,512]{1,0,2:T(4,128)(2,1)}, bf16[4,128,512]{1,0,2:T(4,128)(2,1)S(1)}, u32[]{:S(2)}) copy-start(bf16[4,128,512]{1,0,2:T(4,128)(2,1)S(1)} %fusion.59) | copy-start | bytes 1572868
  413.2 254.5 %collective-permute-start.2 = (bf16[128,512]{1,0:T(8,128)(2,1)}, bf16[128,512]{1,0:T(8,128)(2,1)}, u32[]{:S(2)}, u32[]{:S(2)}) collective-permute-start(bf16[128,512]{1,0:T(8,128)(2,1)} %bitcast.27), channel_id=1, source_target_pairs={{1,0},{2,1},{3,2},{5,4},{6,5},{7,6},{9,8},{10,9},{11,10},{13,12},{... | collective-permute-start | bytes 393224 | tf_op jit(solution)/shard_map/ppermute | solution.py:19
  487.9 11.8 %copy-start.50 = (bf16[4,256,32]{1,0,2:T(4,128)(2,1)S(1)}, bf16[4,256,32]{1,0,2:T(4,128)(2,1)}, u32[]{:S(2)}) copy-start(bf16[4,256,32]{1,0,2:T(4,128)(2,1)} %fusion.220) | copy-start | bytes 196612
  589.9 11.8 %copy-start.44 = (bf16[4,256,32]{1,0,2:T(4,128)(2,1)S(1)}, bf16[4,256,32]{1,0,2:T(4,128)(2,1)}, u32[]{:S(2)}) copy-start(bf16[4,256,32]{1,0,2:T(4,128)(2,1)} %fusion.232) | copy-start | bytes 196612
  720.5 24.9 %collective-permute-start.3 = (bf16[3,8,512]{2,1,0:T(8,128)(2,1)S(1)}, bf16[3,8,512]{2,1,0:T(8,128)(2,1)S(1)}, u32[]{:S(2)}, u32[]{:S(2)}) collective-permute-start(bf16[3,8,512]{2,1,0:T(8,128)(2,1)S(1)} %bitcast.295), channel_id=1, source_target_pairs={{1,0},{2,1},{3,2},{5,4},{6,5},{7,6},{9,8},{10,9},{11,10},{13,12},{... | collective-permute-start | bytes 73736 | tf_op jit(solution)/shard_map/ppermute | solution.py:19
  780.9 97.9 %all-to-all-start.1 = ((bf16[3,4,256,512]{3,2,0,1:T(8,128)(2,1)}), bf16[3,4,256,512]{3,2,0,1:T(8,128)(2,1)}, u32[]{:S(2)}, u32[]{:S(2)}) async-start(bf16[3,4,256,512]{3,2,0,1:T(8,128)(2,1)} %copy.186), calls=%async_computation.1 | async-start | bytes 6291456 | tf_op jit(solution)/shard_map/all_to_all | solution.py:219
  787.6 18.0 %copy-start.7 = (bf16[32,3,16,512]{3,2,1,0:T(8,128)(2,1)S(1)}, bf16[32,3,16,512]{3,2,1,0:T(8,128)(2,1)}, u32[]{:S(2)}) copy-start(bf16[32,3,16,512]{3,2,1,0:T(8,128)(2,1)} %copy-done.6) | copy-start | bytes 4718596
  787.6 89.6 %all-reduce.20.cloned.1.call-start = ((), (), s32[]{:S(2)}) async-start(), calls=%async_computation.2 | async-start | bytes 524288 | tf_op jit(solution)/shard_map/psum | solution.py:223
  792.3 13.3 %copy-start.13 = (bf16[4,128,512]{2,1,0:T(8,128)(2,1)S(1)}, bf16[4,128,512]{2,1,0:T(8,128)(2,1)}, u32[]{:S(2)}) copy-start(bf16[4,128,512]{2,1,0:T(8,128)(2,1)} %copy.189) | copy-start | bytes 1572868
  (59 other events, 336.4 us)
Sparse Core Ops, SparseCore 0:
  802.1 66.7 all-reduce.19
where the time goes:
time: 907 us; the launch traced here: 894 us
  local copies, waits for them, and re-layouts  451 us (50%)
  blocking collectives  189 us (21%)
  other arithmetic  159 us (18%)
  matrix products  56.3 us (6%)
  starting transfers between devices  22.3 us (2%)
  between operations  16 us (2%)
    gather x2, local copies, waits for them, and re-layouts, toeplitz(): return jnp.take(padded, jnp.asarray(lag_table(filter_bf.shape[0])), axis=1)  177 us
    reshape x16, local copies, waits for them, and re-layouts, lag_sums(): skewed = flattened.reshape(group_width, KM, 2 * KM + 1)  129 us
    all_gather x1, blocking collectives, body(): lax.all_gather(feat_filter, 'seq', axis=2, tiled=True)  76.1 us
    psum x1, blocking collectives, body(): lax.psum((mixer_term, feat_term, gain_term), 'seq')  68.3 us
    unnamed x195, local copies, waits for them, and re-layouts  51 us
    reduce_sum x16, other arithmetic, lag_sums(): summed = jnp.sum(skewed[:, :, 1:KM + 1], axis=1)  50.4 us
    pad x16, local copies, waits for them, and re-layouts, lag_sums(): jnp.pad(products.reshape(group_width, 2 * KM * KM), ((0, 0), (0, KM)))  36.3 us
    reduce_sum x2, other arithmetic, tap_sums(): collected.append(jnp.sum(d_float * window, axis=(1, 2)))  33.5 us
  transfers between devices with their start and end apart: 7, of which 0 were waited for; matrix products, arithmetic and copies ran while one was open for 54% of the time, Pallas kernels for 0%

commit v1 on v0

v1 whole, which is shorter than its diff:
```python
import jax
import jax.numpy as jnp
import numpy as np
from jax import lax
from jax.experimental import pallas as pl
from jax.experimental.pallas import tpu as pltpu
from jax.sharding import PartitionSpec as P

KM = 128
KF = 7
UNIT = 16
HALO = 8
LANES = 128
PER_BLOCK = KM // UNIT


EPSILON = 1e-06

bf16 = jnp.bfloat16
f32 = jnp.float32


def split_bf16(matrix):
    high = matrix.astype(bf16)
    low = (matrix - high.astype(np.float64)).astype(bf16)
    return high, low


def transform_matrices():
    angle = 2.0 * np.pi * (np.arange(KM) + 0.5)[:, None] / (2 * KM)
    ahead = np.arange(KM)[None, :] * angle
    analysis = np.concatenate([np.cos(ahead), -np.sin(ahead)], axis=0)
    high, low = split_bf16(analysis)
    analysis_pair = np.concatenate([high, low], axis=1)

    def synthesis(first):
        turn = (first + np.arange(KM))[:, None] * angle.T
        matrix = np.concatenate([np.cos(turn), -np.sin(turn)], axis=1) / KM
        high, low = split_bf16(matrix)
        return np.concatenate([high, low, high], axis=1)

    return analysis_pair, synthesis(KM), synthesis(0)


def record_layout(record_blocks, tail_rows, block_count):
    starts = jnp.cumsum(record_blocks) - record_blocks
    record_ends = starts + record_blocks - 1
    block_ids = jnp.arange(block_count, dtype=jnp.int32)
    starts_here = jnp.any(starts[None, :] == block_ids[:, None], axis=1)
    starts_next = jnp.any(starts[None, :] == block_ids[:, None] + 1, axis=1)
    starts_next = starts_next | (block_ids == block_count - 1)
    closing = record_ends[None, :] == block_ids[:, None]
    filled_rows = jnp.where(
        jnp.any(closing, axis=1), jnp.sum(jnp.where(closing, tail_rows[None, :], 0), axis=1), KM
    )
    carry_on = 1 - starts_here.astype(jnp.int32)
    carry_next = 1 - starts_next.astype(jnp.int32)
    return jnp.stack([carry_on, carry_next, filled_rows.astype(jnp.int32)])


def analyse(analysis_ref, block):
    twice = jnp.concatenate([block, block], axis=0)
    return jnp.dot(analysis_ref[...], twice, preferred_element_type=f32)


def synthesise(synthesis_ref, real, imag):
    spectrum = jnp.concatenate([real, imag], axis=0)
    high = spectrum.astype(bf16)
    low = (spectrum - high.astype(f32)).astype(bf16)
    stacked = jnp.concatenate([high, high, low], axis=0)
    return jnp.dot(synthesis_ref[...], stacked, preferred_element_type=f32)


def alternate(shape):
    rows = lax.broadcasted_iota(jnp.int32, shape, 0)
    return (1 - 2 * (rows & 1)).astype(f32)


def fetch_block(source_ref, extended_ref, unit_ref, layout_ref, block):
    for unit in range(PER_BLOCK):
        first = pl.multiple_of(unit_ref[block * PER_BLOCK + unit] * UNIT, UNIT)
        extended_ref[HALO + unit * UNIT : HALO + (unit + 1) * UNIT, :] = source_ref[
            pl.ds(first, UNIT), :
        ].astype(f32)
    before = jnp.maximum(block * PER_BLOCK - 1, 0)
    first = pl.multiple_of(unit_ref[before] * UNIT, UNIT)
    rim = source_ref[pl.ds(first, UNIT), :].astype(f32)[UNIT - HALO :]
    extended_ref[0:HALO, :] = jnp.where(layout_ref[0, block] > 0, rim, 0.0)


def store_units(target_ref, unit_ref, block, rows):
    for unit in range(PER_BLOCK):
        first = pl.multiple_of(unit_ref[block * PER_BLOCK + unit] * UNIT, UNIT)
        target_ref[pl.ds(first, UNIT), :] = rows[unit * UNIT : (unit + 1) * UNIT]


def featurize(extended_ref, taps_ref, stream, filled):
    total = None
    for lag in range(KF):
        tap = taps_ref[3 * lag + stream : 3 * lag + stream + 1, :]
        term = tap * extended_ref[HALO - lag : HALO - lag + KM, :]
        total = term if total is None else total + term
    rows = lax.broadcasted_iota(jnp.int32, total.shape, 0)
    return jnp.where(rows < filled, total, 0.0).astype(bf16)


def spread(ahead_ref, taps_ref, stream):
    total = None
    for lag in range(KF):
        tap = taps_ref[3 * lag + stream : 3 * lag + stream + 1, :]
        term = tap * ahead_ref[lag : lag + KM, :]
        total = term if total is None else total + term
    return total.astype(bf16)


def fold(rows):
    return jnp.sum(rows.reshape(-1, 8, rows.shape[1]), axis=0)


def add_tap_sums(sums_ref, d_float, extended_ref):
    for lag in range(KF):
        window = extended_ref[HALO - lag : HALO - lag + KM, :]
        sums_ref[8 * lag : 8 * (lag + 1), :] += fold(d_float * window)


def set_ahead(ahead_ref, d_feature, going_on):
    head = ahead_ref[0:HALO, :]
    ahead_ref[KM : KM + HALO, :] = jnp.where(going_on > 0, head, 0.0)
    ahead_ref[0:KM, :] = d_feature.astype(f32)


def block_rows(block):
    return pl.ds(pl.multiple_of(block * KM, KM), KM)


def forward_kernel(shards, rows, *refs):
    unit_ref, layout_ref, position_ref = refs[:3]
    pieces = refs[3 : 3 + shards]
    taps_ref, mixer_ref, gain_ref, analysis_ref, synthesis_ref = refs[3 + shards : 8 + shards]
    staged_ref, feature_ref, response_ref, spectra_ref, filter_ref, gated_ref, squares_ref = refs[
        8 + shards : 15 + shards
    ]
    leaving = refs[15 + shards : 15 + 2 * shards]
    query_ext, key_ext, value_ext, last_ref, gain_rows_ref, sems = refs[15 + 2 * shards :]
    width = staged_ref.shape[2]
    pairs = staged_ref.shape[1] // (2 * KM)
    arrivals = [
        pltpu.make_async_copy(
            pieces[slot], staged_ref.at[:, pl.ds(slot * rows, rows)], sems.at[slot]
        )
        for slot in range(shards)
    ]
    for copy in arrivals:
        copy.start()
    filter_ref[...] = analyse(analysis_ref, mixer_ref[...].astype(bf16))
    last_ref[...] = jnp.zeros_like(last_ref)
    terms = [term.astype(f32) for term in three_terms(gain_ref[...])]
    rest = jnp.zeros((UNIT - 3, width), f32)
    gain_rows_ref[...] = jnp.concatenate(terms + [rest], axis=0).astype(bf16)
    for copy in arrivals:
        copy.wait()

    def pair_step(pair, carry):
        mixed, queries = [], []
        for half in range(2):
            block = 2 * pair + half
            filled = layout_ref[2, block]
            features = []
            for stream, extended_ref in enumerate((query_ext, key_ext, value_ext)):
                fetch_block(staged_ref.at[stream], extended_ref, unit_ref, layout_ref, block)
                feature = featurize(extended_ref, taps_ref, stream, filled)
                feature_ref[stream, block_rows(block), :] = feature
                features.append(feature.astype(f32))
            queries.append(features[0])
            mixed.append((features[1] * features[2]).astype(bf16))
        own = analyse(analysis_ref, jnp.concatenate(mixed, axis=1))
        first_on = (layout_ref[0, 2 * pair] > 0).astype(f32)
        second_on = (layout_ref[0, 2 * pair + 1] > 0).astype(f32)
        earlier = jnp.concatenate([last_ref[...] * first_on, own[:, :width] * second_on], axis=1)
        last_ref[...] = own[:, width:]
        sign = alternate((KM, 2 * width))
        real = earlier[:KM] + sign * own[KM:]
        imag = earlier[KM:] - sign * own[:KM]
        spectra_ref[pair, 0:KM, :] = real
        spectra_ref[pair, KM:, :] = imag
        filter_real = jnp.concatenate([filter_ref[0:KM, :]] * 2, axis=1)
        filter_imag = jnp.concatenate([filter_ref[KM:, :]] * 2, axis=1)
        response = synthesise(
            synthesis_ref,
            real * filter_real - imag * filter_imag,
            real * filter_imag + imag * filter_real,
        )
        for half in range(2):
            block = 2 * pair + half
            own_response = response[:, half * width : (half + 1) * width]
            response_ref[block_rows(block), :] = own_response
            gated = (queries[half] * own_response).astype(bf16)
            gated_ref[block_rows(block), :] = gated
            gated = gated.astype(f32)
            squares_ref[pl.ds(block, 1), :] = jnp.sum((gated * gated).T, axis=0, keepdims=True)
        return carry

    lax.fori_loop(0, pairs, pair_step, 0)
    departures = send_rows(gated_ref, leaving, position_ref[0], rows, sems)
    for slot, target in enumerate(leaving):
        departures.append(
            pltpu.make_async_copy(
                gain_rows_ref, target.at[pl.ds(rows, UNIT)], sems.at[shards + slot]
            )
        )
    for copy in departures:
        copy.start()
    for copy in departures:
        copy.wait()


def send_rows(source_ref, leaving, position, rows, sems):
    departures = []
    for slot, target in enumerate(leaving):
        first = pl.multiple_of((position ^ slot) * rows, rows)
        departures.append(
            pltpu.make_async_copy(
                source_ref.at[pl.ds(first, rows)], target.at[pl.ds(0, rows)], sems.at[slot]
            )
        )
    return departures


def send_slots(source_ref, leaving, rows, sems):
    departures = [
        pltpu.make_async_copy(source_ref.at[pl.ds(slot * rows, rows)], target, sems.at[slot])
        for slot, target in enumerate(leaving)
    ]
    for copy in departures:
        copy.start()
    for copy in departures:
        copy.wait()


def three_terms(values):
    terms = []
    for _ in range(3):
        terms.append(values.astype(bf16))
        values = values - terms[-1].astype(f32)
    return terms


def sum_lanes(values):
    terms = jnp.concatenate(three_terms(values), axis=1)
    ones = jnp.ones((8, terms.shape[1]), bf16)
    return lax.dot_general(
        ones, terms, (((1,), (1,)), ((), ())), preferred_element_type=f32
    )[0:1]


def product_kernel(shards, rows, *refs):
    position_ref = refs[0]
    pieces = refs[1 : 1 + shards]
    gated_ref, squares_ref, gain_ref, staged_ref, sums_ref, sems = refs[1 + shards :]
    blocks = gated_ref.shape[0] // KM
    arrivals = []
    for slot in range(shards):
        first = pl.multiple_of((position_ref[0] ^ slot) * rows, rows)
        arrivals.append(
            pltpu.make_async_copy(pieces[slot], staged_ref.at[pl.ds(first, rows)], sems.at[slot])
        )
    for copy in arrivals:
        copy.start()
    sums_ref[0:blocks, :] = squares_ref[...]
    for slot in range(shards):
        first_block = (position_ref[0] ^ slot) * (rows // KM)
        for step in range(rows // KM):
            gated = gated_ref[block_rows(first_block + step), :].astype(f32)
            weighted = pieces[slot][step * KM : (step + 1) * KM, :].astype(f32) * gain_ref[...]
            sums_ref[pl.ds(blocks + first_block + step, 1), :] = sum_lanes(weighted * gated)
    for copy in arrivals:
        copy.wait()


def scale_of(sums_ref, block, filled, total_channels):
    lanes = lax.broadcasted_iota(jnp.int32, (1, KM), 1)
    squares = sums_ref[pl.ds(block, 1), :]
    return jnp.where(lanes < filled, lax.rsqrt(squares / total_channels + EPSILON), 0.0)


def down_rows(rows, width):
    count = len(rows)
    terms = [term.astype(f32) for row in rows for term in three_terms(row)]
    rest = jnp.zeros((16 - 3 * count, KM), f32)
    stacked = jnp.concatenate(terms + [rest], axis=0).astype(bf16)
    shape = (16, count * width)
    source = lax.broadcasted_iota(jnp.int32, shape, 0)
    lanes = lax.broadcasted_iota(jnp.int32, shape, 1)
    first = 3 * (lanes // width)
    chosen = ((source >= first) & (source < first + 3)).astype(f32).astype(bf16)
    columns = lax.dot_general(
        stacked, chosen, (((0,), (0,)), ((), ())), preferred_element_type=f32
    )
    return [columns[:, i * width : (i + 1) * width] for i in range(count)]


def norm_kernel(total_channels, shards, rows, *refs):
    (
        unit_ref, layout_ref, cotangent_ref, response_ref, taps_ref, gain_ref, feature_ref,
        gated_ref, sums_ref, d_query_ref, d_response_ref,
    ) = refs[:11]
    leaving = refs[11 : 11 + shards]
    grad_ref, ahead_ref, sems = refs[11 + shards :]
    blocks = gated_ref.shape[0] // KM
    width = gated_ref.shape[1]
    ahead_ref[...] = jnp.zeros_like(ahead_ref)

    def block_step(step, carry):
        block = blocks - 1 - step
        scale_row = scale_of(sums_ref, block, layout_ref[2, block], total_channels)
        products = sums_ref[pl.ds(blocks + block, 1), :]
        inner_row = scale_row * products / total_channels
        scale, pull = down_rows([scale_row, scale_row * scale_row * inner_row], width)
        gated = gated_ref[block_rows(block), :].astype(f32)
        weighted = cotangent_ref[block_rows(block), :].astype(f32) * gain_ref[...]
        d_gated = (scale * weighted - pull * gated).astype(bf16).astype(f32)
        feature = feature_ref[0, block_rows(block), :].astype(f32)
        d_response_ref[block_rows(block), :] = (d_gated * feature).astype(bf16)
        d_query = (d_gated * response_ref[block_rows(block), :]).astype(bf16)
        d_query_ref[block_rows(block), :] = d_query
        set_ahead(ahead_ref, d_query, layout_ref[1, block])
        store_units(grad_ref, unit_ref, block, spread(ahead_ref, taps_ref, 0))
        return carry

    lax.fori_loop(0, blocks, block_step, 0)
    send_slots(grad_ref, leaving, rows, sems)


def mix_back_kernel(shards, rows, *refs):
    (
        unit_ref, layout_ref, taps_ref, analysis_ref, synthesis_ref, feature_ref,
        spectra_ref, filter_ref, d_response_ref, query_piece_ref, mixer_grad_ref, d_others_ref,
    ) = refs[:12]
    leaving = refs[12 : 12 + shards]
    grad_ref, key_ahead, value_ahead, next_ref, cross_ref, sems = refs[12 + shards :]
    width = feature_ref.shape[2]
    pairs = feature_ref.shape[1] // (2 * KM)
    for scratch in (key_ahead, value_ahead, next_ref, cross_ref):
        scratch[...] = jnp.zeros_like(scratch)
    query_copy = pltpu.make_async_copy(query_piece_ref, leaving[1].at[0], sems.at[shards])
    query_copy.start()

    def pair_step(step, carry):
        pair = pairs - 1 - step
        d_response = jnp.concatenate(
            [d_response_ref[block_rows(2 * pair), :], d_response_ref[block_rows(2 * pair + 1), :]],
            axis=1,
        )
        own = analyse(analysis_ref, d_response)
        first_on = (layout_ref[1, 2 * pair] > 0).astype(f32)
        second_on = (layout_ref[1, 2 * pair + 1] > 0).astype(f32)
        later = jnp.concatenate([own[:, width:] * first_on, next_ref[...] * second_on], axis=1)
        next_ref[...] = own[:, :width]
        own_real, own_imag = own[:KM], own[KM:]
        real_x, imag_x = spectra_ref[pair, 0:KM, :], spectra_ref[pair, KM:, :]
        cross_real = own_real * real_x + own_imag * imag_x
        cross_imag = own_imag * real_x - own_real * imag_x
        cross_ref[0:KM, :] += cross_real[:, :width] + cross_real[:, width:]
        cross_ref[KM:, :] += cross_imag[:, :width] + cross_imag[:, width:]
        sign = alternate((KM, 2 * width))
        real = own_real + sign * later[KM:]
        imag = own_imag - sign * later[:KM]
        filter_real = jnp.concatenate([filter_ref[0:KM, :]] * 2, axis=1)
        filter_imag = jnp.concatenate([filter_ref[KM:, :]] * 2, axis=1)
        d_mixed = synthesise(
            synthesis_ref,
            real * filter_real + imag * filter_imag,
            imag * filter_real - real * filter_imag,
        )
        for half in (1, 0):
            block = 2 * pair + half
            d_mixed_block = d_mixed[:, half * width : (half + 1) * width]
            for stream, ahead_ref in ((1, key_ahead), (2, value_ahead)):
                factor = feature_ref[3 - stream, block_rows(block), :].astype(f32)
                d_feature = (d_mixed_block * factor).astype(bf16)
                d_others_ref[stream - 1, block_rows(block), :] = d_feature
                set_ahead(ahead_ref, d_feature, layout_ref[1, block])
                spread_rows = spread(ahead_ref, taps_ref, stream)
                store_units(grad_ref.at[stream - 1], unit_ref, block, spread_rows)
        return carry

    lax.fori_loop(0, pairs, pair_step, 0)
    departures = [
        pltpu.make_async_copy(
            grad_ref.at[:, pl.ds(slot * rows, rows)],
            target.at[1:3] if slot == 1 else target,
            sems.at[slot],
        )
        for slot, target in enumerate(leaving)
    ]
    for copy in departures:
        copy.start()
    sign = alternate((KM, width))
    mixer_grad_ref[...] = synthesise(
        synthesis_ref, sign * cross_ref[KM:, :], -(sign * cross_ref[0:KM, :])
    )
    for copy in departures + [query_copy]:
        copy.wait()


def tap_grad_kernel(
    total_channels,
    unit_ref, layout_ref, staged_ref, d_query_ref, d_others_ref, gated_ref, cotangent_ref,
    sums_ref, taps_grad_ref, gain_grad_ref, extended_ref, tap_sums_ref, gain_sums_ref,
):
    blocks = gated_ref.shape[0] // KM
    width = gated_ref.shape[1]
    tap_sums_ref[...] = jnp.zeros_like(tap_sums_ref)
    gain_sums_ref[...] = jnp.zeros_like(gain_sums_ref)

    def block_step(block, carry):
        scale_row = scale_of(sums_ref, block, layout_ref[2, block], total_channels)
        (scale,) = down_rows([scale_row], width)
        normed = gated_ref[block_rows(block), :].astype(f32) * scale
        cotangent = cotangent_ref[block_rows(block), :].astype(f32)
        gain_sums_ref[...] += fold(cotangent * normed)
        for stream in range(3):
            extended = extended_ref.at[stream]
            fetch_block(staged_ref.at[stream], extended, unit_ref, layout_ref, block)
            if stream == 0:
                d_feature = d_query_ref[block_rows(block), :]
            else:
                d_feature = d_others_ref[stream - 1, block_rows(block), :]
            add_tap_sums(tap_sums_ref.at[stream], d_feature.astype(f32), extended)
        return carry

    lax.fori_loop(0, blocks, block_step, 0)
    gain_grad_ref[...] = jnp.sum(gain_sums_ref[...], axis=0, keepdims=True)
    for stream in range(3):
        for lag in range(KF):
            taps_grad_ref[3 * lag + stream : 3 * lag + stream + 1, :] = jnp.sum(
                tap_sums_ref[stream, 8 * lag : 8 * (lag + 1), :], axis=0, keepdims=True
            )


def scale_out_kernel(total_channels, shards, rows, *refs):
    layout_ref, position_ref, sums_ref = refs[:3]
    pieces = refs[3 : 3 + shards]
    scaled = refs[3 + shards :]

    def block_step(step, carry):
        block = position_ref[0] * (rows // KM) + step
        scale_row = scale_of(sums_ref, block, layout_ref[2, block], total_channels)
        (scale,) = down_rows([scale_row], pieces[0].shape[1])
        for piece, target in zip(pieces, scaled):
            terms = piece[rows : rows + UNIT, :].astype(f32)
            gain = terms[0:1] + terms[1:2] + terms[2:3]
            normed = piece[block_rows(step), :].astype(f32) * scale
            target[block_rows(step), :] = (normed * gain).astype(bf16)
        return carry

    lax.fori_loop(0, rows // KM, block_step, 0)


def lane_place(position, slot, width):
    return pl.ds(pl.multiple_of((position ^ slot) * width, width), width)


def assemble_out_kernel(shards, width, position_ref, *refs):
    pieces, target, sems = refs[:shards], refs[shards], refs[shards + 1]
    copies = []
    for slot, piece in enumerate(pieces):
        lanes = lane_place(position_ref[0], slot, width)
        copies.append(pltpu.make_async_copy(piece, target.at[:, lanes], sems.at[slot]))
    for copy in copies:
        copy.start()
    for copy in copies:
        copy.wait()


def assemble_grad_kernel(shards, width, position_ref, *refs):
    queries, others, target, sems = refs[: shards - 1], refs[shards - 1 : -2], refs[-2], refs[-1]
    copies = []
    for slot in range(shards):
        lanes = lane_place(position_ref[0], slot, width)
        first = 0 if slot == 1 else 1
        copies.append((others[slot], target.at[first:3, :, lanes]))
        if slot != 1:
            copies.append((queries[min(slot, 1) + max(slot - 2, 0)], target.at[0, :, lanes]))
    copies = [
        pltpu.make_async_copy(source, view, sems.at[i]) for i, (source, view) in enumerate(copies)
    ]
    for copy in copies:
        copy.start()
    for copy in copies:
        copy.wait()


NEAR = pltpu.VMEM
FAR = pl.ANY


def run_kernel(kernel, scalars, arrays, outs, scratch, microseconds, name, sems=0):
    in_specs = [pl.BlockSpec(memory_space=pltpu.SMEM)] * len(scalars)
    operands = list(scalars)
    for array, space in arrays:
        operands.append(array)
        in_specs.append(pl.BlockSpec(memory_space=space))
    scratch_shapes = [pltpu.VMEM(s, d) for s, d in scratch]
    if sems:
        scratch_shapes.append(pltpu.SemaphoreType.DMA((sems,)))
    return pl.pallas_call(
        kernel,
        out_shape=[jax.ShapeDtypeStruct(s, d) for s, d, _ in outs],
        in_specs=in_specs,
        out_specs=[pl.BlockSpec(memory_space=space) for _, _, space in outs],
        scratch_shapes=scratch_shapes,
        compiler_params=pltpu.CompilerParams(vmem_limit_bytes=20 * 1024 * 1024),
        cost_estimate=pl.CostEstimate(
            flops=int(microseconds * 1e9), bytes_accessed=0, transcendentals=0
        ),
        name=name,
    )(*operands)


def exchange(array, axis, bits):
    return lax.ppermute(array, axis, [(i, i ^ bits) for i in range(lax.axis_size(axis))])


def butterfly(sums, axis):
    bit = 1
    while bit < lax.axis_size(axis):
        sums = sums + exchange(sums, axis, bit)
        bit *= 2
    return sums


def body(
    streams, record_blocks, tail_rows, unit_dest, mixer_filter, feat_filter, norm_gain, out_grad
):
    rows = streams.shape[1]
    channels = streams.shape[2]
    shards = lax.axis_size("seq")
    position = lax.axis_index("seq")
    total_channels = channels * lax.axis_size("fsdp")
    tokens = rows * shards
    blocks = tokens // KM
    units = tokens // UNIT
    units_dev = rows // UNIT
    narrow = channels // shards
    width = -(-narrow // LANES) * LANES

    def widen(array):
        if width == narrow:
            return array
        return jnp.pad(array, ((0, 0),) * (array.ndim - 1) + ((0, width - narrow),))

    def to_channels(array):
        pieces = []
        for slot in range(shards):
            first = (position ^ slot) * narrow
            part = lax.dynamic_slice_in_dim(array, first, narrow, array.ndim - 1)
            pieces.append(widen(exchange(part, "seq", slot) if slot else part))
        return pieces

    def to_tokens(pieces, slots):
        return [
            exchange(part[..., :narrow], "seq", slot) if slot else part[..., :narrow]
            for slot, part in zip(slots, pieces)
        ]

    every_slot = range(shards)

    position_word = position.astype(jnp.int32).reshape(1)
    layout = record_layout(record_blocks, tail_rows, blocks)
    unit_ids = jnp.arange(units, dtype=jnp.int32)
    loaded_unit = jnp.sum(
        jnp.where(unit_dest[None, :] == unit_ids[:, None], unit_ids[None, :], 0), axis=1
    ).astype(jnp.int32)
    slot = position ^ (loaded_unit // units_dev)
    unit_table = slot * units_dev + loaded_unit % units_dev
    analysis, synthesis_on, synthesis_back = (jnp.asarray(m) for m in transform_matrices())
    taps = widen(feat_filter.reshape(3 * KF, narrow))
    own_gain = norm_gain.reshape(1, narrow)
    gain = widen(own_gain)
    mixer = widen(mixer_filter)

    arrived = to_channels(streams)
    arrived[1], late_grad = lax.optimization_barrier((arrived[1], out_grad))
    cotangent_pieces = to_channels(late_grad)

    whole = (tokens, width)
    spectra_shape = (blocks // 2, 2 * KM, 2 * width)
    extended_shape = (KM + HALO, width)
    extended = (extended_shape, f32)
    scalars = (unit_table, layout)
    forward = run_kernel(
        lambda *refs: forward_kernel(shards, rows, *refs),
        scalars + (position_word,),
        [(part, FAR) for part in arrived]
        + [(a, NEAR) for a in (taps, mixer, gain, analysis, synthesis_on)],
        (
            ((3,) + whole, bf16, NEAR), ((3,) + whole, bf16, NEAR), (whole, f32, NEAR),
            (spectra_shape, f32, NEAR), ((2 * KM, width), f32, NEAR), (whole, bf16, NEAR),
            ((blocks, KM), f32, NEAR),
        ) + (((rows + UNIT, width), bf16, FAR),) * shards,
        (extended,) * 3 + (((2 * KM, width), f32), ((UNIT, width), bf16)),
        9,
        "forward",
        sems=2 * shards,
    )
    staged, features, response, spectra, filter_spectrum, gated, squares = forward[:7]
    gated_back = to_tokens(forward[7:], every_slot)
    cotangent, sums = run_kernel(
        lambda *refs: product_kernel(shards, rows, *refs),
        (position_word,),
        [(a, NEAR) for a in cotangent_pieces] + [(a, NEAR) for a in (gated, squares, gain)],
        ((whole, bf16, NEAR), ((2 * blocks, KM), f32, NEAR)),
        (),
        2,
        "product",
        sems=shards,
    )
    sums = butterfly(sums, "fsdp")
    sums, gated_back = lax.optimization_barrier((sums, gated_back))
    sums = butterfly(sums, "seq")
    norm = run_kernel(
        lambda *refs: norm_kernel(total_channels, shards, rows, *refs),
        scalars,
        [(a, NEAR) for a in (cotangent, response, taps, gain, features, gated, sums)],
        ((whole, bf16, NEAR),) * 2 + (((rows, width), bf16, FAR),) * shards,
        ((whole, bf16), extended),
        3,
        "norm",
        sems=shards,
    )
    d_query, d_response = norm[:2]
    query_back = to_tokens(norm[2:3] + norm[4:], [slot for slot in every_slot if slot != 1])
    back = run_kernel(
        lambda *refs: mix_back_kernel(shards, rows, *refs),
        scalars,
        [
            (a, NEAR)
            for a in (
                taps, analysis, synthesis_back, features, spectra, filter_spectrum, d_response
            )
        ]
        + [(norm[3], FAR)],
        (((KM, width), f32, NEAR), ((2,) + whole, bf16, NEAR))
        + tuple(((3 if slot == 1 else 2, rows, width), bf16, FAR) for slot in every_slot),
        (((2,) + whole, bf16),) + (extended,) * 2 + (((2 * KM, width), f32),) * 2,
        7,
        "mix_back",
        sems=shards + 1,
    )
    mixer_grad, d_others = back[:2]
    others_back = to_tokens(back[2:], every_slot)
    taps_grad, gain_grad = run_kernel(
        lambda *refs: tap_grad_kernel(total_channels, *refs),
        scalars,
        [(a, NEAR) for a in (staged, d_query, d_others, gated, cotangent, sums)],
        (((3 * KF, width), f32, NEAR), ((1, width), f32, NEAR)),
        (((3,) + extended_shape, f32), ((3, 8 * KF, width), f32), ((8, width), f32)),
        4,
        "tap_grad",
    )
    scaled = run_kernel(
        lambda *refs: scale_out_kernel(total_channels, shards, rows, *refs),
        (layout, position_word),
        [(sums, NEAR)] + [(a, NEAR) for a in gated_back],
        (((rows, narrow), bf16, NEAR),) * shards,
        (),
        1,
        "scale_out",
    )
    if width == narrow:
        (out,) = run_kernel(
            lambda *refs: assemble_out_kernel(shards, width, *refs),
            (position_word,),
            [(a, FAR) for a in scaled],
            (((rows, channels), bf16, FAR),),
            (),
            1,
            "assemble_out",
            sems=shards,
        )
        (stream_grad,) = run_kernel(
            lambda *refs: assemble_grad_kernel(shards, width, *refs),
            (position_word,),
            [(a, FAR) for a in query_back] + [(a, FAR) for a in others_back],
            (((3, rows, channels), bf16, FAR),),
            (),
            1,
            "assemble_grad",
            sems=2 * shards,
        )
    else:
        def assemble(pieces):
            stacked = jnp.stack(pieces)
            in_place = jnp.take(stacked, position ^ jnp.arange(shards), axis=0)
            return jnp.moveaxis(in_place, 0, -2).reshape(pieces[0].shape[:-1] + (channels,))

        out = assemble(scaled)
        queries = query_back[:1] + [others_back[1][0]] + query_back[1:]
        others_back[1] = others_back[1][1:]
        stream_grad = jnp.concatenate([assemble(queries)[None], assemble(others_back)])
    feat_grad = taps_grad[:, :narrow].reshape(KF, 3, narrow)
    return (out, stream_grad, mixer_grad[:, :narrow], feat_grad, gain_grad[0, :narrow])


def solution(mesh):
    placed = (
        P(None, "seq", "fsdp"),
        P(),
        P(),
        P(),
        P(None, ("fsdp", "seq")),
        P(None, None, ("fsdp", "seq")),
        P(("fsdp", "seq")),
        P("seq", "fsdp"),
    )
    return jax.shard_map(
        body,
        mesh=mesh,
        in_specs=placed,
        out_specs=(
            P("seq", "fsdp"),
            P(None, "seq", "fsdp"),
            P(None, ("fsdp", "seq")),
            P(None, None, ("fsdp", "seq")),
            P(("fsdp", "seq")),
        ),
        check_vma=False,
    )
```

time: 907 us -> 117 us (0.13); the launches traced: 894 us -> 117 us
  local copies, waits for them, and re-layouts: 451 us -> 3.09 us
  blocking collectives: 189 us -> 0 us
  other arithmetic: 159 us -> 0.53 us
  waiting for transfers between devices: 0.03 us -> 56.4 us
  matrix products: 56.3 us -> 0 us
  Pallas kernels: 0 us -> 30.7 us
  between operations: 16 us -> 0.94 us
    gather x6 -> x0, local copies, waits for them, and re-layouts: 187 us -> none  [the longest x2 177 us: toeplitz(): return jnp.take(padded, jnp.asarray(lag_table(filter_bf.shape[0])), axis=1)]
    reshape x20 -> x2, local copies, waits for them, and re-layouts: 134 us -> 0.02 us  [the longest x1 0.01 us: body(): taps = widen(feat_filter.reshape(3 * KF, narrow))]
    all_gather x3 -> x0, blocking collectives: 96.7 us -> none  [the longest x1 76.1 us: body(): lax.all_gather(feat_filter, 'seq', axis=2, tiled=True)]
    psum x3 -> x0, blocking collectives: 92.4 us -> none  [the longest x1 68.3 us: body(): lax.psum((mixer_term, feat_term, gain_term), 'seq')]
    reduce_sum x24 -> x2, other arithmetic: 89.9 us -> 0.19 us  [the longest x1 0.1 us: body(): jnp.sum(jnp.where(unit_dest[None, :] == unit_ids[:, None], unit_ids[None,...]
    ppermute x4 -> x19, waiting for transfers between devices: 0.01 us -> 56.4 us  [exchange(): lax.ppermute(array, axis, [(i, i ^ bits) for i in range(lax.axis_size(axi...]
    dot_general x20 -> x0, matrix products: 56.3 us -> none  [the longest x16 14.3 us: lag_sums(): jnp.einsum('bic,bkc->cik', d_response[:, :, start_col:start_col + group_w...]
    unnamed x195 -> x22, local copies, waits for them, and re-layouts: 51 us -> 0.65 us
  transfers between devices with their start and end apart: 7 -> 19, of which waited for: 0 -> 9; matrix products, arithmetic and copies ran while one was open for 54% -> 1% of each run, Pallas kernels for 0% -> 20%
where the time goes in v1:
time: 117 us
  waiting for transfers between devices  56.4 us (48%)
  Pallas kernels  30.7 us (26%)
  starting transfers between devices  25.2 us (22%)
  local copies, waits for them, and re-layouts  3.09 us (3%)
    ppermute x19, waiting for transfers between devices, exchange(): lax.ppermute(array, axis, [(i, i ^ bits) for i in range(lax.axis_size(axi...  56.4 us
    pallas_call x8, Pallas kernels, run_kernel(): pl.pallas_call(kernel, out_shape=[jax.ShapeDtypeStruct(s, d) for s, d, _...  30.7 us
    ppermute x19, starting transfers between devices, exchange(): lax.ppermute(array, axis, [(i, i ^ bits) for i in range(lax.axis_size(axi...  25.2 us
    dynamic_slice x2, local copies, waits for them, and re-layouts, to_channels(): part = lax.dynamic_slice_in_dim(array, first, narrow, array.ndim - 1)  2.41 us
  transfers between devices with their start and end apart: 19, of which 9 were waited for; matrix products, arithmetic and copies ran while one was open for 1% of the time, Pallas kernels for 20%

profile of v1, /device:TPU:0, one launch (start us, length us, event | category | flops | bytes accessed | tf_op | source)
XLA Modules:
  0.0 116.8 jit_solution(13166581294898476260)
XLA Ops:
  0.8 2.3 %constant_dynamic-slice_fusion = (bf16[3,512,128]{2,1,0:T(8,128)(2,1)S(1)}, bf16[3,512,128]{2,1,0:T(8,128)(2,1)S(1)}, bf16[3,512,128]{2,1,0:T(8,128)(2,1)}, bf16[3,512,128]{2,1,0:T(8,128)(2,1)S(1)}) fusion(bf16[3,512,512]{2,1,0:T(8,128)(2,1)} %param.11, s32[]{:T(128)S(6)} %select_n.56, s32[]{:T(128)S(6)} %select_n.54, s32[]{:T(128)S(6)} %select_n.53, ...), kind=kLoop, calls=%fused_computation.7 | loop fusion | bytes 3145744 | tf_op jit(solution)/shard_map/dynamic_slice | solution.py:557
  3.1 5.0 %collective-permute-start.5 = (bf16[3,512,128]{2,1,0:T(8,128)(2,1)S(1)}, bf16[3,512,128]{2,1,0:T(8,128)(2,1)S(1)}, u32[]{:S(2)}, u32[]{:S(2)}) collective-permute-start(bf16[3,512,128]{2,1,0:T(8,128)(2,1)S(1)} %get-tuple-element.98), channel_id=1, source_target_pairs={{0,3},{1,2},{2,1},{3,0},{4,7},{5,6},{6,5},{7,4},{8,11},{9,10},{10,... | collective-permute-start | bytes 1179656 | tf_op jit(solution)/shard_map/ppermute | solution.py:522
  9.3 17.5 %collective-permute-done.refs_4_ = bf16[3,512,128]{2,1,0:T(8,128)(2,1)S(1)} collective-permute-done((bf16[3,512,128]{2,1,0:T(8,128)(2,1)}, bf16[3,512,128]{2,1,0:T(8,128)(2,1)S(1)}, u32[]{:S(2)}, u32[]{:S(2)}) %collective-permute-start) | collective-permute-done | bytes 393248 | tf_op jit(solution)/shard_map/ppermute | solution.py:522
  26.9 2.1 %collective-permute-start.3 = (bf16[512,128]{1,0:T(8,128)(2,1)S(1)}, bf16[512,128]{1,0:T(8,128)(2,1)S(1)}, u32[]{:S(2)}, u32[]{:S(2)}) collective-permute-start(bf16[512,128]{1,0:T(8,128)(2,1)S(1)} %get-tuple-element.102), channel_id=1, source_target_pairs={{0,3},{1,2},{2,1},{3,0},{4,7},{5,6},{6,5},{7,4},{8,11},{9,10},{10,... | collective-permute-start | bytes 393224 | tf_op jit(solution)/shard_map/ppermute | solution.py:522
  29.0 1.2 %collective-permute-start.2 = (bf16[512,128]{1,0:T(8,128)(2,1)S(1)}, bf16[512,128]{1,0:T(8,128)(2,1)S(1)}, u32[]{:S(2)}, u32[]{:S(2)}) collective-permute-start(bf16[512,128]{1,0:T(8,128)(2,1)S(1)} %get-tuple-element.103), channel_id=1, source_target_pairs={{0,2},{1,3},{2,0},{3,1},{4,6},{5,7},{6,4},{7,5},{8,10},{9,11},{10,... | collective-permute-start | bytes 393224 | tf_op jit(solution)/shard_map/ppermute | solution.py:522
  31.4 16.9 %collective-permute-done.4.refs_5_ = bf16[3,512,128]{2,1,0:T(8,128)(2,1)S(1)} collective-permute-done((bf16[3,512,128]{2,1,0:T(8,128)(2,1)S(1)}, bf16[3,512,128]{2,1,0:T(8,128)(2,1)S(1)}, u32[]{:S(2)}, u32[]{:S(2)}) %collective-permute-start.4) | collective-permute-done | bytes 393248 | tf_op jit(solution)/shard_map/ppermute | solution.py:522
  48.3 8.2 %forward.1 = (bf16[3,2048,128]{2,1,0:T(8,128)(2,1)S(1)}, bf16[3,2048,128]{2,1,0:T(8,128)(2,1)S(1)}, f32[2048,128]{1,0:T(8,128)S(1)}, f32[8,256,256]{2,1,0:T(8,12...) custom-call(s32[128]{0:T(128)S(1)} %fusion.3.refs_0_, ...), custom_call_target="tpu_custom_call" | custom-call | flops 8999999488 | tf_op jit(solution)/shard_map/forward/pallas_call | solution.py:507
  56.6 3.2 %collective-permute-start.10 = (bf16[528,128]{1,0:T(8,128)(2,1)S(1)}, bf16[528,128]{1,0:T(8,128)(2,1)S(1)}, u32[]{:S(2)}, u32[]{:S(2)}) collective-permute-start(bf16[528,128]{1,0:T(8,128)(2,1)S(1)} %get-tuple-element.50), channel_id=1, source_target_pairs={{0,2},{1,3},{2,0},{3,1},{4,6},{5,7},{6,4},{7,5},{8,10},{9,11},{10,... | collective-permute-start | bytes 405512 | tf_op jit(solution)/shard_map/ppermute | solution.py:522
  61.0 1.4 %product.1 = (bf16[2048,128]{1,0:T(8,128)(2,1)S(1)}, f32[32,128]{1,0:T(8,128)S(1)}) custom-call(s32[1]{0:T(128)} %bitcast.refs_2_.refs_0_.refs_1_, bf16[512,128]{1,0:T(8,128)(2,1)S(1)} %get-tuple-element.105.refs_1_, bf16[512,128]{1,0:T(8,128)(2,1)S(1)} %collective-permute-done.1.refs_2_, bf16[512,128]{1,0:T(8,128)(2,1)S(1)} %collective-permute-done.2.refs_3_, ...), custom_call_target="tpu_custom_call" | custom-call | flops 2000000000 | tf_op jit(solution)/shard_map/product/pallas_call | solution.py:507
  63.7 1.4 %collective-permute-start.7 = (f32[32,128]{1,0:T(8,128)S(1)}, f32[32,128]{1,0:T(8,128)S(1)}, u32[]{:S(2)}, u32[]{:S(2)}) collective-permute-start(f32[32,128]{1,0:T(8,128)S(1)} %add.62), channel_id=1, source_target_pairs={{0,8},{4,12},{8,0},{12,4},{16,24},{20,28},{24,16},{28,20},{1,9},{5... | collective-permute-start | bytes 49160 | tf_op jit(solution)/shard_map/ppermute | solution.py:522
  65.1 2.3 %collective-permute-done.7 = f32[32,128]{1,0:T(8,128)S(1)} collective-permute-done((f32[32,128]{1,0:T(8,128)S(1)}, f32[32,128]{1,0:T(8,128)S(1)}, u32[]{:S(2)}, u32[]{:S(2)}) %collective-permute-start.7) | collective-permute-done | bytes 16416 | tf_op jit(solution)/shard_map/ppermute | solution.py:522
  67.4 1.5 %collective-permute-start.8 = (f32[32,128]{1,0:T(8,128)S(1)}, f32[32,128]{1,0:T(8,128)S(1)}, u32[]{:S(2)}, u32[]{:S(2)}) collective-permute-start(f32[32,128]{1,0:T(8,128)S(1)} %add.63), channel_id=1, source_target_pairs={{0,16},{4,20},{8,24},{12,28},{16,0},{20,4},{24,8},{28,12},{1,17},{... | collective-permute-start | bytes 49160 | tf_op jit(solution)/shard_map/ppermute | solution.py:522
  68.9 2.3 %collective-permute-done.8 = f32[32,128]{1,0:T(8,128)S(1)} collective-permute-done((f32[32,128]{1,0:T(8,128)S(1)}, f32[32,128]{1,0:T(8,128)S(1)}, u32[]{:S(2)}, u32[]{:S(2)}) %collective-permute-start.8) | collective-permute-done | bytes 16416 | tf_op jit(solution)/shard_map/ppermute | solution.py:522
  71.3 3.7 %collective-permute-done.12 = f32[32,128]{1,0:T(8,128)S(1)} collective-permute-done((f32[32,128]{1,0:T(8,128)S(1)}, f32[32,128]{1,0:T(8,128)S(1)}, u32[]{:S(2)}, u32[]{:S(2)}) %collective-permute-start.12) | collective-permute-done | bytes 16416 | tf_op jit(solution)/shard_map/ppermute | solution.py:522
  75.0 1.3 %collective-permute-start.13 = (f32[32,128]{1,0:T(8,128)S(1)}, f32[32,128]{1,0:T(8,128)S(1)}, u32[]{:S(2)}, u32[]{:S(2)}) collective-permute-start(f32[32,128]{1,0:T(8,128)S(1)} %add.65), channel_id=1, source_target_pairs={{0,2},{1,3},{2,0},{3,1},{4,6},{5,7},{6,4},{7,5},{8,10},{9,11},{10,... | collective-permute-start | bytes 49160 | tf_op jit(solution)/shard_map/ppermute | solution.py:522
  76.3 3.4 %collective-permute-done.13 = f32[32,128]{1,0:T(8,128)S(1)} collective-permute-done((f32[32,128]{1,0:T(8,128)S(1)}, f32[32,128]{1,0:T(8,128)S(1)}, u32[]{:S(2)}, u32[]{:S(2)}) %collective-permute-start.13) | collective-permute-done | bytes 16416 | tf_op jit(solution)/shard_map/ppermute | solution.py:522
  79.6 5.6 %norm.1 = (bf16[2048,128]{1,0:T(8,128)(2,1)S(1)}, bf16[2048,128]{1,0:T(8,128)(2,1)S(1)}, bf16[512,128]{1,0:T(8,128)(2,1)S(1)}, bf16[512,128]{1,0:T(8,128)(2,1)S(...) custom-call(s32[128]{0:T(128)S(1)} %fusion.3.refs_0_, s32[3,16]{1,0:T(4,128)S(1)} %pad_add_fusion.refs_1_.refs_0_, ...), custom_call_target="tpu_custom_call" | custom-call | flops 3000000000 | tf_op jit(solution)/shard_map/norm/pallas_call | solution.py:507
  85.2 1.3 %collective-permute-start.14 = (bf16[512,128]{1,0:T(8,128)(2,1)S(1)}, bf16[512,128]{1,0:T(8,128)(2,1)S(1)}, u32[]{:S(2)}, u32[]{:S(2)}) collective-permute-start(bf16[512,128]{1,0:T(8,128)(2,1)S(1)} %get-tuple-element.65), channel_id=1, source_target_pairs={{0,2},{1,3},{2,0},{3,1},{4,6},{5,7},{6,4},{7,5},{8,10},{9,11},{10,... | collective-permute-start | bytes 393224 | tf_op jit(solution)/shard_map/ppermute | solution.py:522
  86.6 1.4 %collective-permute-start.15 = (bf16[512,128]{1,0:T(8,128)(2,1)S(1)}, bf16[512,128]{1,0:T(8,128)(2,1)S(1)}, u32[]{:S(2)}, u32[]{:S(2)}) collective-permute-start(bf16[512,128]{1,0:T(8,128)(2,1)S(1)} %get-tuple-element.66), channel_id=1, source_target_pairs={{0,3},{1,2},{2,1},{3,0},{4,7},{5,6},{6,5},{7,4},{8,11},{9,10},{10,... | collective-permute-start | bytes 393224 | tf_op jit(solution)/shard_map/ppermute | solution.py:522
  88.0 7.0 %mix_back.1 = (f32[128,128]{1,0:T(8,128)}, bf16[2,2048,128]{2,1,0:T(8,128)(2,1)S(1)}, bf16[2,512,128]{2,1,0:T(8,128)(2,1)S(1)}, bf16[3,512,128]{2,1,0:T(8,128)(2...) custom-call(s32[128]{0:T(128)S(1)} %fusion.3.refs_0_, ...), custom_call_target="tpu_custom_call" | custom-call | flops 7000000000 | tf_op jit(solution)/shard_map/mix_back/pallas_call | solution.py:507
  95.1 2.0 %collective-permute-start.17 = (bf16[2,512,128]{2,1,0:T(8,128)(2,1)S(1)}, bf16[2,512,128]{2,1,0:T(8,128)(2,1)S(1)}, u32[]{:S(2)}, u32[]{:S(2)}) collective-permute-start(bf16[2,512,128]{2,1,0:T(8,128)(2,1)S(1)} %get-tuple-element.73), channel_id=1, source_target_pairs={{0,2},{1,3},{2,0},{3,1},{4,6},{5,7},{6,4},{7,5},{8,10},{9,11},{10,... | collective-permute-start | bytes 786440 | tf_op jit(solution)/shard_map/ppermute | solution.py:522
  98.6 5.0 %tap_grad.1 = (f32[21,128]{1,0:T(8,128)S(1)}, f32[1,128]{1,0:T(1,128)}) custom-call(s32[128]{0:T(128)S(1)} %fusion.3.refs_0_, s32[3,16]{1,0:T(4,128)S(1)} %pad_add_fusion.refs_1_.refs_0_, bf16[3,2048,128]{2,1,0:T(8,128)(2,1)S(1)} %get-tuple-element.76.refs_2_, bf16[2048,128]{1,0:T(8,128)(2,1)S(1)} %get-tuple-element.77.refs_3_, ...), custom_call_target="tpu_custom_call" | custom-call | flops 4000000000 | tf_op jit(solution)/shard_map/tap_grad/pallas_call | solution.py:507
  103.6 1.5 %scale_out.1 = (bf16[512,128]{1,0:T(8,128)(2,1)S(1)}, bf16[512,128]{1,0:T(8,128)(2,1)S(1)}, bf16[512,128]{1,0:T(8,128)(2,1)S(1)}, bf16[512,128]{1,0:T(8,128)(2,1)S(1)}) custom-call(s32[3,16]{1,0:T(4,128)S(1)} %pad_add_fusion.refs_1_.refs_0_, s32[1]{0:T(128)} %bitcast.refs_2_.refs_0_.refs_1_, f32[32,128]{1,0:T(8,128)S(1)} %add.66.refs_2_.refs_8_.refs_7_, ...), custom_call_target="tpu_custom_call" | custom-call | flops 1000000000 | tf_op jit(solution)/shard_map/scale_out/pallas_call | solution.py:507
  106.5 8.0 %collective-permute-done.17.refs_6_ = bf16[2,512,128]{2,1,0:T(8,128)(2,1)S(1)} collective-permute-done((bf16[2,512,128]{2,1,0:T(8,128)(2,1)S(1)}, bf16[2,512,128]{2,1,0:T(8,128)(2,1)S(1)}, u32[]{:S(2)}, u32[]{:S(2)}) %collective-permute-start.17) | collective-permute-done | bytes 262176 | tf_op jit(solution)/shard_map/ppermute | solution.py:522
  (64 shorter events, 10.3 us)
Async XLA Ops:
  0.7 26.1 %copy-start.5 = (bf16[512,512]{1,0:T(8,128)(2,1)S(1)}, bf16[512,512]{1,0:T(8,128)(2,1)}, u32[]{:S(2)}) copy-start(bf16[512,512]{1,0:T(8,128)(2,1)} %param.18) | copy-start | bytes 1572868
  0.7 47.6 %copy-start = (f32[128,128]{1,0:T(8,128)S(1)}, f32[128,128]{1,0:T(8,128)}, u32[]{:S(2)}) copy-start(f32[128,128]{1,0:T(8,128)} %refs_8_.1) | copy-start | bytes 196612
  0.7 47.6 %copy-start.1 = (f32[128]{0:T(128)S(1)}, f32[128]{0:T(128)}, u32[]{:S(2)}) copy-start(f32[128]{0:T(128)} %param.17) | copy-start | bytes 1540
  0.7 47.6 %copy-start.3 = (bf16[128,768]{1,0:T(8,128)(2,1)S(1)}, bf16[128,768]{1,0:T(8,128)(2,1)}, u32[]{:S(2)}) copy-start(bf16[128,768]{1,0:T(8,128)(2,1)} %constant.61.clone.refs_11_) | copy-start | bytes 589828
  0.7 47.6 %copy-start.4 = (bf16[256,256]{1,0:T(8,128)(2,1)S(1)}, bf16[256,256]{1,0:T(8,128)(2,1)}, u32[]{:S(2)}) copy-start(bf16[256,256]{1,0:T(8,128)(2,1)} %constant.60.clone.refs_10_.refs_3_) | copy-start | bytes 393220
  3.1 28.3 %collective-permute-start.5 = (bf16[3,512,128]{2,1,0:T(8,128)(2,1)S(1)}, bf16[3,512,128]{2,1,0:T(8,128)(2,1)S(1)}, u32[]{:S(2)}, u32[]{:S(2)}) collective-permute-start(bf16[3,512,128]{2,1,0:T(8,128)(2,1)S(1)} %get-tuple-element.98), channel_id=1, source_target_pairs={{0,3},{1,2},{2,1},{3,0},{4,7},{5,6},{6,5},{7,4},{8,11},{9,10},{10,... | collective-permute-start | bytes 1179656 | tf_op jit(solution)/shard_map/ppermute | solution.py:522
  8.1 18.7 %collective-permute-start = (bf16[3,512,128]{2,1,0:T(8,128)(2,1)}, bf16[3,512,128]{2,1,0:T(8,128)(2,1)S(1)}, u32[]{:S(2)}, u32[]{:S(2)}) collective-permute-start(bf16[3,512,128]{2,1,0:T(8,128)(2,1)} %get-tuple-element.100), channel_id=1, source_target_pairs={{0,1},{1,0},{2,3},{3,2},{4,5},{5,4},{6,7},{7,6},{8,9},{9,8},{10,11... | collective-permute-start | bytes 1179656 | tf_op jit(solution)/shard_map/ppermute | solution.py:522
  8.1 40.2 %collective-permute-start.4 = (bf16[3,512,128]{2,1,0:T(8,128)(2,1)S(1)}, bf16[3,512,128]{2,1,0:T(8,128)(2,1)S(1)}, u32[]{:S(2)}, u32[]{:S(2)}) collective-permute-start(bf16[3,512,128]{2,1,0:T(8,128)(2,1)S(1)} %get-tuple-element.101), channel_id=1, source_target_pairs={{0,2},{1,3},{2,0},{3,1},{4,6},{5,7},{6,4},{7,5},{8,10},{9,11},{10,... | collective-permute-start | bytes 1179656 | tf_op jit(solution)/shard_map/ppermute | solution.py:522
  26.9 32.9 %collective-permute-start.3 = (bf16[512,128]{1,0:T(8,128)(2,1)S(1)}, bf16[512,128]{1,0:T(8,128)(2,1)S(1)}, u32[]{:S(2)}, u32[]{:S(2)}) collective-permute-start(bf16[512,128]{1,0:T(8,128)(2,1)S(1)} %get-tuple-element.102), channel_id=1, source_target_pairs={{0,3},{1,2},{2,1},{3,0},{4,7},{5,6},{6,5},{7,4},{8,11},{9,10},{10,... | collective-permute-start | bytes 393224 | tf_op jit(solution)/shard_map/ppermute | solution.py:522
  29.0 32.1 %collective-permute-start.2 = (bf16[512,128]{1,0:T(8,128)(2,1)S(1)}, bf16[512,128]{1,0:T(8,128)(2,1)S(1)}, u32[]{:S(2)}, u32[]{:S(2)}) collective-permute-start(bf16[512,128]{1,0:T(8,128)(2,1)S(1)} %get-tuple-element.103), channel_id=1, source_target_pairs={{0,2},{1,3},{2,0},{3,1},{4,6},{5,7},{6,4},{7,5},{8,10},{9,11},{10,... | collective-permute-start | bytes 393224 | tf_op jit(solution)/shard_map/ppermute | solution.py:522
  30.2 30.9 %collective-permute-start.1 = (bf16[512,128]{1,0:T(8,128)(2,1)S(1)}, bf16[512,128]{1,0:T(8,128)(2,1)S(1)}, u32[]{:S(2)}, u32[]{:S(2)}) collective-permute-start(bf16[512,128]{1,0:T(8,128)(2,1)S(1)} %get-tuple-element.104), channel_id=1, source_target_pairs={{0,1},{1,0},{2,3},{3,2},{4,5},{5,4},{6,7},{7,6},{8,9},{9,8},{10,11... | collective-permute-start | bytes 393224 | tf_op jit(solution)/shard_map/ppermute | solution.py:522
  56.6 14.6 %collective-permute-start.9 = (bf16[528,128]{1,0:T(8,128)(2,1)S(1)}, bf16[528,128]{1,0:T(8,128)(2,1)S(1)}, u32[]{:S(2)}, u32[]{:S(2)}) collective-permute-start(bf16[528,128]{1,0:T(8,128)(2,1)S(1)} %get-tuple-element.49), channel_id=1, source_target_pairs={{0,1},{1,0},{2,3},{3,2},{4,5},{5,4},{6,7},{7,6},{8,9},{9,8},{10,11... | collective-permute-start | bytes 405512 | tf_op jit(solution)/shard_map/ppermute | solution.py:522
  56.6 14.5 %collective-permute-start.10 = (bf16[528,128]{1,0:T(8,128)(2,1)S(1)}, bf16[528,128]{1,0:T(8,128)(2,1)S(1)}, u32[]{:S(2)}, u32[]{:S(2)}) collective-permute-start(bf16[528,128]{1,0:T(8,128)(2,1)S(1)} %get-tuple-element.50), channel_id=1, source_target_pairs={{0,2},{1,3},{2,0},{3,1},{4,6},{5,7},{6,4},{7,5},{8,10},{9,11},{10,... | collective-permute-start | bytes 405512 | tf_op jit(solution)/shard_map/ppermute | solution.py:522
  59.8 11.4 %collective-permute-start.11 = (bf16[528,128]{1,0:T(8,128)(2,1)S(1)}, bf16[528,128]{1,0:T(8,128)(2,1)S(1)}, u32[]{:S(2)}, u32[]{:S(2)}) collective-permute-start(bf16[528,128]{1,0:T(8,128)(2,1)S(1)} %get-tuple-element.51), channel_id=1, source_target_pairs={{0,3},{1,2},{2,1},{3,0},{4,7},{5,6},{6,5},{7,4},{8,11},{9,10},{10,... | collective-permute-start | bytes 405512 | tf_op jit(solution)/shard_map/ppermute | solution.py:522
  62.4 1.2 %collective-permute-start.6 = (f32[32,128]{1,0:T(8,128)S(1)}, f32[32,128]{1,0:T(8,128)S(1)}, u32[]{:S(2)}, u32[]{:S(2)}) collective-permute-start(f32[32,128]{1,0:T(8,128)S(1)} %get-tuple-element.47), channel_id=1, source_target_pairs={{0,4},{4,0},{8,12},{12,8},{16,20},{20,16},{24,28},{28,24},{1,5},{5... | collective-permute-start | bytes 49160 | tf_op jit(solution)/shard_map/ppermute | solution.py:522
  63.7 3.7 %collective-permute-start.7 = (f32[32,128]{1,0:T(8,128)S(1)}, f32[32,128]{1,0:T(8,128)S(1)}, u32[]{:S(2)}, u32[]{:S(2)}) collective-permute-start(f32[32,128]{1,0:T(8,128)S(1)} %add.62), channel_id=1, source_target_pairs={{0,8},{4,12},{8,0},{12,4},{16,24},{20,28},{24,16},{28,20},{1,9},{5... | collective-permute-start | bytes 49160 | tf_op jit(solution)/shard_map/ppermute | solution.py:522
  67.4 3.7 %collective-permute-start.8 = (f32[32,128]{1,0:T(8,128)S(1)}, f32[32,128]{1,0:T(8,128)S(1)}, u32[]{:S(2)}, u32[]{:S(2)}) collective-permute-start(f32[32,128]{1,0:T(8,128)S(1)} %add.63), channel_id=1, source_target_pairs={{0,16},{4,20},{8,24},{12,28},{16,0},{20,4},{24,8},{28,12},{1,17},{... | collective-permute-start | bytes 49160 | tf_op jit(solution)/shard_map/ppermute | solution.py:522
  71.2 3.8 %collective-permute-start.12 = (f32[32,128]{1,0:T(8,128)S(1)}, f32[32,128]{1,0:T(8,128)S(1)}, u32[]{:S(2)}, u32[]{:S(2)}) collective-permute-start(f32[32,128]{1,0:T(8,128)S(1)} %add.64), channel_id=1, source_target_pairs={{0,1},{1,0},{2,3},{3,2},{4,5},{5,4},{6,7},{7,6},{8,9},{9,8},{10,11... | collective-permute-start | bytes 49160 | tf_op jit(solution)/shard_map/ppermute | solution.py:522
  75.0 4.6 %collective-permute-start.13 = (f32[32,128]{1,0:T(8,128)S(1)}, f32[32,128]{1,0:T(8,128)S(1)}, u32[]{:S(2)}, u32[]{:S(2)}) collective-permute-start(f32[32,128]{1,0:T(8,128)S(1)} %add.65), channel_id=1, source_target_pairs={{0,2},{1,3},{2,0},{3,1},{4,6},{5,7},{6,4},{7,5},{8,10},{9,11},{10,... | collective-permute-start | bytes 49160 | tf_op jit(solution)/shard_map/ppermute | solution.py:522
  85.2 21.3 %collective-permute-start.14 = (bf16[512,128]{1,0:T(8,128)(2,1)S(1)}, bf16[512,128]{1,0:T(8,128)(2,1)S(1)}, u32[]{:S(2)}, u32[]{:S(2)}) collective-permute-start(bf16[512,128]{1,0:T(8,128)(2,1)S(1)} %get-tuple-element.65), channel_id=1, source_target_pairs={{0,2},{1,3},{2,0},{3,1},{4,6},{5,7},{6,4},{7,5},{8,10},{9,11},{10,... | collective-permute-start | bytes 393224 | tf_op jit(solution)/shard_map/ppermute | solution.py:522
  86.6 19.9 %collective-permute-start.15 = (bf16[512,128]{1,0:T(8,128)(2,1)S(1)}, bf16[512,128]{1,0:T(8,128)(2,1)S(1)}, u32[]{:S(2)}, u32[]{:S(2)}) collective-permute-start(bf16[512,128]{1,0:T(8,128)(2,1)S(1)} %get-tuple-element.66), channel_id=1, source_target_pairs={{0,3},{1,2},{2,1},{3,0},{4,7},{5,6},{6,5},{7,4},{8,11},{9,10},{10,... | collective-permute-start | bytes 393224 | tf_op jit(solution)/shard_map/ppermute | solution.py:522
  95.1 19.5 %collective-permute-start.17 = (bf16[2,512,128]{2,1,0:T(8,128)(2,1)S(1)}, bf16[2,512,128]{2,1,0:T(8,128)(2,1)S(1)}, u32[]{:S(2)}, u32[]{:S(2)}) collective-permute-start(bf16[2,512,128]{2,1,0:T(8,128)(2,1)S(1)} %get-tuple-element.73), channel_id=1, source_target_pairs={{0,2},{1,3},{2,0},{3,1},{4,6},{5,7},{6,4},{7,5},{8,10},{9,11},{10,... | collective-permute-start | bytes 786440 | tf_op jit(solution)/shard_map/ppermute | solution.py:522
  97.1 17.5 %collective-permute-start.18 = (bf16[2,512,128]{2,1,0:T(8,128)(2,1)S(1)}, bf16[2,512,128]{2,1,0:T(8,128)(2,1)S(1)}, u32[]{:S(2)}, u32[]{:S(2)}) collective-permute-start(bf16[2,512,128]{2,1,0:T(8,128)(2,1)S(1)} %get-tuple-element.74), channel_id=1, source_target_pairs={{0,3},{1,2},{2,1},{3,0},{4,7},{5,6},{6,5},{7,4},{8,11},{9,10},{10,... | collective-permute-start | bytes 786440 | tf_op jit(solution)/shard_map/ppermute | solution.py:522
  98.3 17.3 %collective-permute-start.16 = (bf16[3,512,128]{2,1,0:T(8,128)(2,1)S(1)}, bf16[3,512,128]{2,1,0:T(8,128)(2,1)S(1)}, u32[]{:S(2)}, u32[]{:S(2)}) collective-permute-start(bf16[3,512,128]{2,1,0:T(8,128)(2,1)S(1)} %get-tuple-element.72), channel_id=1, source_target_pairs={{0,1},{1,0},{2,3},{3,2},{4,5},{5,4},{6,7},{7,6},{8,9},{9,8},{10,11... | collective-permute-start | bytes 1179656 | tf_op jit(solution)/shard_map/ppermute | solution.py:522
  (5 other events, 41.6 us)

commit v2 on v1

v2 whole, which is shorter than its diff:
```python
import jax
import jax.numpy as jnp
import numpy as np
from jax import lax
from jax.experimental import pallas as pl
from jax.experimental.pallas import tpu as pltpu
from jax.sharding import PartitionSpec as P

KM = 128
KF = 7
UNIT = 16
HALO = 8
LANES = 128
PER_BLOCK = KM // UNIT


EPSILON = 1e-06

bf16 = jnp.bfloat16
f32 = jnp.float32


def split_bf16(matrix):
    high = matrix.astype(bf16)
    low = (matrix - high.astype(np.float64)).astype(bf16)
    return high, low


def transform_matrices():
    angle = 2.0 * np.pi * (np.arange(KM) + 0.5)[:, None] / (2 * KM)
    ahead = np.arange(KM)[None, :] * angle
    analysis = np.concatenate([np.cos(ahead), -np.sin(ahead)], axis=0)
    high, low = split_bf16(analysis)
    analysis_pair = np.concatenate([high, low], axis=1)

    def synthesis(first):
        turn = (first + np.arange(KM))[:, None] * angle.T
        matrix = np.concatenate([np.cos(turn), -np.sin(turn)], axis=1) / KM
        high, low = split_bf16(matrix)
        return np.concatenate([high, low], axis=0)

    return analysis_pair, synthesis(KM), synthesis(0)


def record_layout(record_blocks, tail_rows, block_count):
    starts = jnp.cumsum(record_blocks) - record_blocks
    record_ends = starts + record_blocks - 1
    block_ids = jnp.arange(block_count, dtype=jnp.int32)
    starts_here = jnp.any(starts[None, :] == block_ids[:, None], axis=1)
    starts_next = jnp.any(starts[None, :] == block_ids[:, None] + 1, axis=1)
    starts_next = starts_next | (block_ids == block_count - 1)
    closing = record_ends[None, :] == block_ids[:, None]
    filled_rows = jnp.where(
        jnp.any(closing, axis=1), jnp.sum(jnp.where(closing, tail_rows[None, :], 0), axis=1), KM
    )
    carry_on = 1 - starts_here.astype(jnp.int32)
    carry_next = 1 - starts_next.astype(jnp.int32)
    return jnp.stack([carry_on, carry_next, filled_rows.astype(jnp.int32)])


def analyse(analysis_ref, block):
    twice = jnp.concatenate([block, block], axis=0)
    return jnp.dot(analysis_ref[...], twice, preferred_element_type=f32)


def synthesise(synthesis_ref, real, imag):
    spectrum = jnp.concatenate([real, imag], axis=0)
    high = spectrum.astype(bf16)
    low = (spectrum - high.astype(f32)).astype(bf16)
    both = jnp.dot(synthesis_ref[...], high, preferred_element_type=f32)
    rest = jnp.dot(synthesis_ref[0:KM, :], low, preferred_element_type=f32)
    return both[:KM] + (both[KM:] + rest)


def alternate(shape):
    rows = lax.broadcasted_iota(jnp.int32, shape, 0)
    return (1 - 2 * (rows & 1)).astype(f32)


def fetch_block(source_ref, extended_ref, unit_ref, layout_ref, block):
    for unit in range(PER_BLOCK):
        first = pl.multiple_of(unit_ref[block * PER_BLOCK + unit] * UNIT, UNIT)
        extended_ref[HALO + unit * UNIT : HALO + (unit + 1) * UNIT, :] = source_ref[
            pl.ds(first, UNIT), :
        ].astype(f32)
    before = jnp.maximum(block * PER_BLOCK - 1, 0)
    first = pl.multiple_of(unit_ref[before] * UNIT, UNIT)
    rim = source_ref[pl.ds(first, UNIT), :].astype(f32)[UNIT - HALO :]
    extended_ref[0:HALO, :] = jnp.where(layout_ref[0, block] > 0, rim, 0.0)


def store_units(target_ref, unit_ref, block, rows):
    for unit in range(PER_BLOCK):
        first = pl.multiple_of(unit_ref[block * PER_BLOCK + unit] * UNIT, UNIT)
        target_ref[pl.ds(first, UNIT), :] = rows[unit * UNIT : (unit + 1) * UNIT]


def featurize(extended_ref, taps_ref, stream, filled):
    total = None
    for lag in range(KF):
        tap = taps_ref[3 * lag + stream : 3 * lag + stream + 1, :]
        term = tap * extended_ref[HALO - lag : HALO - lag + KM, :]
        total = term if total is None else total + term
    rows = lax.broadcasted_iota(jnp.int32, total.shape, 0)
    return jnp.where(rows < filled, total, 0.0).astype(bf16)


def spread(ahead_ref, taps_ref, stream):
    total = None
    for lag in range(KF):
        tap = taps_ref[3 * lag + stream : 3 * lag + stream + 1, :]
        term = tap * ahead_ref[lag : lag + KM, :]
        total = term if total is None else total + term
    return total.astype(bf16)


def fold(rows):
    return jnp.sum(rows.reshape(-1, 8, rows.shape[1]), axis=0)


def add_tap_sums(sums_ref, d_float, extended_ref):
    for lag in range(KF):
        window = extended_ref[HALO - lag : HALO - lag + KM, :]
        sums_ref[8 * lag : 8 * (lag + 1), :] += fold(d_float * window)


def set_ahead(ahead_ref, layout_ref, block, d_feature):
    ahead_ref[block + 1, 0:KM, :] = d_feature
    going_on = layout_ref[1, jnp.maximum(block - 1, 0)]
    ahead_ref[block, KM:, :] = jnp.where(going_on > 0, d_feature[:HALO], 0.0)


def repeat(count, per_step, work):
    def step(index, carry):
        for offset in range(per_step):
            work(per_step * index + offset, offset)
        return carry

    lax.fori_loop(0, count // per_step, step, 0)


def block_rows(block):
    return pl.ds(pl.multiple_of(block * KM, KM), KM)


def twice(array):
    return jnp.concatenate([array, array], axis=1)


def respond_kernel(shards, rows, *refs):
    unit_ref, layout_ref = refs[:2]
    pieces = refs[2 : 2 + shards]
    taps_ref, mixer_ref, analysis_ref, synthesis_ref = refs[2 + shards : 6 + shards]
    staged_ref, feature_ref, response_ref, filter_ref = refs[6 + shards : 10 + shards]
    extended_ref, mixed_ref, spectra_ref, sems = refs[10 + shards :]
    width = staged_ref.shape[2]
    pairs = staged_ref.shape[1] // (2 * KM)
    arrivals = [
        pltpu.make_async_copy(
            pieces[slot], staged_ref.at[:, pl.ds(slot * rows, rows)], sems.at[slot]
        )
        for slot in range(shards)
    ]
    for copy in arrivals:
        copy.start()
    filter_ref[...] = analyse(analysis_ref, mixer_ref[...].astype(bf16))
    spectra_ref[0, ...] = jnp.zeros(spectra_ref.shape[1:], f32)
    for copy in arrivals:
        copy.wait()

    def feature_pair(pair, offset):
        mixed = []
        for half in range(2):
            block = 2 * pair + half
            filled = layout_ref[2, block]
            features = []
            for stream in range(2):
                extended = extended_ref.at[2 * half + stream]
                fetch_block(staged_ref.at[stream], extended, unit_ref, layout_ref, block)
                feature = featurize(extended, taps_ref, stream + 1, filled)
                feature_ref[stream, block_rows(block), :] = feature
                features.append(feature.astype(f32))
            mixed.append((features[0] * features[1]).astype(bf16))
        mixed_ref[pair, ...] = jnp.concatenate(mixed, axis=1)

    def analyse_pair(pair, offset):
        spectra_ref[pair + 1, ...] = analyse(analysis_ref, mixed_ref[pair, ...])

    def respond_pair(pair, offset):
        own = spectra_ref[pair + 1, ...]
        first_on = (layout_ref[0, 2 * pair] > 0).astype(f32)
        second_on = (layout_ref[0, 2 * pair + 1] > 0).astype(f32)
        earlier = jnp.concatenate(
            [spectra_ref[pair, :, width:] * first_on, own[:, :width] * second_on], axis=1
        )
        sign = alternate((KM, 2 * width))
        real = earlier[:KM] + sign * own[KM:]
        imag = earlier[KM:] - sign * own[:KM]
        filter_real, filter_imag = twice(filter_ref[0:KM, :]), twice(filter_ref[KM:, :])
        response = synthesise(
            synthesis_ref,
            real * filter_real - imag * filter_imag,
            real * filter_imag + imag * filter_real,
        )
        response_ref[block_rows(2 * pair), :] = response[:, :width]
        response_ref[block_rows(2 * pair + 1), :] = response[:, width:]

    repeat(pairs, 1, feature_pair)
    repeat(pairs, 2, analyse_pair)
    repeat(pairs, 2, respond_pair)


def gate_kernel(shards, rows, *refs):
    unit_ref, layout_ref, position_ref = refs[:3]
    pieces = refs[3 : 3 + shards]
    response_ref, taps_ref, gain_ref = refs[3 + shards : 6 + shards]
    staged_ref, feature_ref, gated_ref, squares_ref = refs[6 + shards : 10 + shards]
    leaving = refs[10 + shards : 10 + 2 * shards]
    extended_ref, sems = refs[10 + 2 * shards :]
    width = staged_ref.shape[1]
    blocks = staged_ref.shape[0] // KM
    arrivals = [
        pltpu.make_async_copy(piece, staged_ref.at[pl.ds(slot * rows, rows)], sems.at[slot])
        for slot, piece in enumerate(pieces)
    ]
    for copy in arrivals:
        copy.start()
    terms = [term.astype(f32) for term in bf16_terms(gain_ref[...], 3)]
    rest = jnp.zeros((UNIT - 3, width), f32)
    gain_rows = jnp.concatenate(terms + [rest], axis=0).astype(bf16)
    for shard in range(shards):
        gated_ref[shard, rows:, :] = gain_rows
    for copy in arrivals:
        copy.wait()

    def gate_block(block, offset):
        extended = extended_ref.at[offset]
        fetch_block(staged_ref, extended, unit_ref, layout_ref, block)
        feature = featurize(extended, taps_ref, 0, layout_ref[2, block])
        feature_ref[block_rows(block), :] = feature
        gated = (feature.astype(f32) * response_ref[block_rows(block), :]).astype(bf16)
        set_gated(gated_ref, block, gated)
        gated = gated.astype(f32)
        squares_ref[pl.ds(block, 1), :] = sum_lanes(gated * gated)

    repeat(blocks, 4, gate_block)
    departures = [
        pltpu.make_async_copy(gated_ref.at[position_ref[0] ^ slot], target, sems.at[slot])
        for slot, target in enumerate(leaving)
    ]
    for copy in departures:
        copy.start()
    for copy in departures:
        copy.wait()


def product_kernel(shards, rows, *refs):
    position_ref = refs[0]
    pieces = refs[1 : 1 + shards]
    gated_ref, squares_ref, gain_ref, staged_ref, sums_ref, sems = refs[1 + shards :]
    blocks = squares_ref.shape[0]
    arrivals = []
    for slot in range(shards):
        first = pl.multiple_of((position_ref[0] ^ slot) * rows, rows)
        arrivals.append(
            pltpu.make_async_copy(pieces[slot], staged_ref.at[pl.ds(first, rows)], sems.at[slot])
        )
    for copy in arrivals:
        copy.start()
    sums_ref[0:blocks, :] = squares_ref[...]
    for slot in range(shards):
        shard = position_ref[0] ^ slot
        for step in range(rows // KM):
            here = slice(step * KM, (step + 1) * KM)
            gated = gated_ref[shard, here, :].astype(f32)
            weighted = pieces[slot][here, :].astype(f32) * gain_ref[...]
            block = shard * (rows // KM) + step
            sums_ref[pl.ds(blocks + block, 1), :] = sum_lanes(weighted * gated)
    for copy in arrivals:
        copy.wait()


def gated_place(gated_ref, block):
    per_shard = (gated_ref.shape[1] - UNIT) // KM
    return block // per_shard, block_rows(block % per_shard)


def set_gated(gated_ref, block, gated):
    shard, place = gated_place(gated_ref, block)
    gated_ref[shard, place, :] = gated


def get_gated(gated_ref, block):
    shard, place = gated_place(gated_ref, block)
    return gated_ref[shard, place, :].astype(f32)


def send_slots(source_ref, leaving, rows, sems):
    departures = [
        pltpu.make_async_copy(source_ref.at[pl.ds(slot * rows, rows)], target, sems.at[slot])
        for slot, target in enumerate(leaving)
    ]
    for copy in departures:
        copy.start()
    for copy in departures:
        copy.wait()


def bf16_terms(values, count):
    terms = []
    for _ in range(count):
        terms.append(values.astype(bf16))
        values = values - terms[-1].astype(f32)
    return terms


def sum_lanes(values):
    terms = jnp.concatenate(bf16_terms(values, 2), axis=1)
    ones = jnp.ones((8, terms.shape[1]), bf16)
    return lax.dot_general(
        ones, terms, (((1,), (1,)), ((), ())), preferred_element_type=f32
    )[0:1]


def scale_of(sums_ref, block, filled, total_channels):
    lanes = lax.broadcasted_iota(jnp.int32, (1, KM), 1)
    squares = sums_ref[pl.ds(block, 1), :]
    return jnp.where(lanes < filled, lax.rsqrt(squares / total_channels + EPSILON), 0.0)


def down_rows(row, width):
    return jnp.broadcast_to(row, (width, KM)).T


def norm_kernel(total_channels, shards, rows, *refs):
    (
        unit_ref, layout_ref, cotangent_ref, response_ref, taps_ref, gain_ref, feature_ref,
        gated_ref, sums_ref, d_query_ref, d_response_ref,
    ) = refs[:11]
    leaving = refs[11 : 11 + shards]
    grad_ref, ahead_ref, sems = refs[11 + shards :]
    blocks = cotangent_ref.shape[0] // KM
    width = cotangent_ref.shape[1]
    ahead_ref[blocks, KM:, :] = jnp.zeros((HALO, width), f32)

    def scale_block(block, offset):
        scale_row = scale_of(sums_ref, block, layout_ref[2, block], total_channels)
        products = sums_ref[pl.ds(blocks + block, 1), :]
        inner_row = scale_row * products / total_channels
        scale = down_rows(scale_row, width)
        pull = down_rows(scale_row * scale_row * inner_row, width)
        gated = get_gated(gated_ref, block)
        weighted = cotangent_ref[block_rows(block), :].astype(f32) * gain_ref[...]
        d_gated = (scale * weighted - pull * gated).astype(bf16).astype(f32)
        feature = feature_ref[block_rows(block), :].astype(f32)
        d_response_ref[block_rows(block), :] = (d_gated * feature).astype(bf16)
        d_query = (d_gated * response_ref[block_rows(block), :]).astype(bf16)
        d_query_ref[block_rows(block), :] = d_query
        set_ahead(ahead_ref, layout_ref, block, d_query.astype(f32))

    def spread_block(block, offset):
        spread_rows = spread(ahead_ref.at[block + 1], taps_ref, 0)
        store_units(grad_ref, unit_ref, block, spread_rows)

    repeat(blocks, 2, scale_block)
    repeat(blocks, 2, spread_block)
    send_slots(grad_ref, leaving, rows, sems)


def mix_back_kernel(shards, rows, *refs):
    (
        unit_ref, layout_ref, taps_ref, analysis_ref, synthesis_ref, feature_ref, filter_ref,
        d_response_ref, query_piece_ref, mixer_grad_ref, d_others_ref,
    ) = refs[:11]
    leaving = refs[11 : 11 + shards]
    grad_ref, ahead_ref, spectra_ref, cross_ref, sems = refs[11 + shards :]
    width = feature_ref.shape[2]
    blocks = feature_ref.shape[1] // KM
    pairs = blocks // 2
    query_copy = pltpu.make_async_copy(query_piece_ref, leaving[1].at[0], sems.at[shards])
    query_copy.start()
    cross_ref[...] = jnp.zeros_like(cross_ref)
    spectra_ref[pairs, ...] = jnp.zeros(spectra_ref.shape[1:], f32)
    for stream in range(2):
        ahead_ref[stream, blocks, KM:, :] = jnp.zeros((HALO, width), f32)

    def analyse_pair(pair, offset):
        d_response = jnp.concatenate(
            [d_response_ref[block_rows(2 * pair), :], d_response_ref[block_rows(2 * pair + 1), :]],
            axis=1,
        )
        spectra_ref[pair, ...] = analyse(analysis_ref, d_response)

    def mix_pair(pair, offset):
        own = spectra_ref[pair, ...]
        first_on = (layout_ref[1, 2 * pair] > 0).astype(f32)
        second_on = (layout_ref[1, 2 * pair + 1] > 0).astype(f32)
        later = jnp.concatenate(
            [own[:, width:] * first_on, spectra_ref[pair + 1, :, :width] * second_on], axis=1
        )
        sign = alternate((KM, 2 * width))
        real = own[:KM] + sign * later[KM:]
        imag = own[KM:] - sign * later[:KM]
        mixed = []
        for block in (2 * pair, 2 * pair + 1):
            key_feature = feature_ref[0, block_rows(block), :].astype(f32)
            value_feature = feature_ref[1, block_rows(block), :].astype(f32)
            mixed.append((key_feature * value_feature).astype(bf16))
        source = analyse(analysis_ref, jnp.concatenate(mixed, axis=1))
        cross_real = real * source[:KM] + imag * source[KM:]
        cross_imag = imag * source[:KM] - real * source[KM:]
        cross_ref[0:KM, :] += cross_real[:, :width] + cross_real[:, width:]
        cross_ref[KM:, :] += cross_imag[:, :width] + cross_imag[:, width:]
        filter_real, filter_imag = twice(filter_ref[0:KM, :]), twice(filter_ref[KM:, :])
        d_mixed = synthesise(
            synthesis_ref,
            real * filter_real + imag * filter_imag,
            imag * filter_real - real * filter_imag,
        )
        for half in range(2):
            block = 2 * pair + half
            d_mixed_block = d_mixed[:, half * width : (half + 1) * width]
            for stream in (1, 2):
                factor = feature_ref[2 - stream, block_rows(block), :].astype(f32)
                d_feature = (d_mixed_block * factor).astype(bf16)
                d_others_ref[stream - 1, block_rows(block), :] = d_feature
                set_ahead(ahead_ref.at[stream - 1], layout_ref, block, d_feature.astype(f32))

    def spread_block(block, offset):
        for stream in (1, 2):
            spread_rows = spread(ahead_ref.at[stream - 1, block + 1], taps_ref, stream)
            store_units(grad_ref.at[stream - 1], unit_ref, block, spread_rows)

    repeat(pairs, 2, analyse_pair)
    repeat(pairs, 2, mix_pair)
    repeat(blocks, 1, spread_block)
    departures = [
        pltpu.make_async_copy(
            grad_ref.at[:, pl.ds(slot * rows, rows)],
            target.at[1:3] if slot == 1 else target,
            sems.at[slot],
        )
        for slot, target in enumerate(leaving)
    ]
    for copy in departures:
        copy.start()
    mixer_grad_ref[...] = synthesise(synthesis_ref, cross_ref[0:KM, :], cross_ref[KM:, :])
    for copy in departures + [query_copy]:
        copy.wait()


def tap_grad_kernel(
    total_channels,
    unit_ref, layout_ref, query_ref, others_ref, d_query_ref, d_others_ref, gated_ref,
    cotangent_ref, sums_ref, taps_grad_ref, gain_grad_ref, extended_ref, tap_sums_ref,
    gain_sums_ref,
):
    blocks = cotangent_ref.shape[0] // KM
    width = cotangent_ref.shape[1]
    tap_sums_ref[...] = jnp.zeros_like(tap_sums_ref)
    gain_sums_ref[...] = jnp.zeros_like(gain_sums_ref)

    def block_step(block, carry):
        scale_row = scale_of(sums_ref, block, layout_ref[2, block], total_channels)
        scale = down_rows(scale_row, width)
        normed = get_gated(gated_ref, block) * scale
        cotangent = cotangent_ref[block_rows(block), :].astype(f32)
        gain_sums_ref[...] += fold(cotangent * normed)
        for stream in range(3):
            extended = extended_ref.at[stream]
            if stream == 0:
                source_ref = query_ref
                d_feature = d_query_ref[block_rows(block), :]
            else:
                source_ref = others_ref.at[stream - 1]
                d_feature = d_others_ref[stream - 1, block_rows(block), :]
            fetch_block(source_ref, extended, unit_ref, layout_ref, block)
            add_tap_sums(tap_sums_ref.at[stream], d_feature.astype(f32), extended)
        return carry

    lax.fori_loop(0, blocks, block_step, 0)
    gain_grad_ref[...] = jnp.sum(gain_sums_ref[...], axis=0, keepdims=True)
    for stream in range(3):
        for lag in range(KF):
            taps_grad_ref[3 * lag + stream : 3 * lag + stream + 1, :] = jnp.sum(
                tap_sums_ref[stream, 8 * lag : 8 * (lag + 1), :], axis=0, keepdims=True
            )


def scale_out_kernel(total_channels, shards, rows, *refs):
    layout_ref, position_ref, sums_ref = refs[:3]
    pieces = refs[3 : 3 + shards]
    out_ref, scaled_ref, sems = refs[3 + shards :]
    narrow = pieces[0].shape[1]

    def scale_block(step, offset):
        block = position_ref[0] * (rows // KM) + step
        scale_row = scale_of(sums_ref, block, layout_ref[2, block], total_channels)
        scale = down_rows(scale_row, narrow)
        for slot, piece in enumerate(pieces):
            terms = piece[rows : rows + UNIT, :].astype(f32)
            gain = terms[0:1] + terms[1:2] + terms[2:3]
            normed = piece[block_rows(step), :].astype(f32) * scale
            scaled_ref[slot, block_rows(step), :] = (normed * gain).astype(bf16)

    repeat(rows // KM, 1, scale_block)
    copies = []
    for slot in range(shards):
        if len(out_ref.shape) == 2:
            target = out_ref.at[:, lane_place(position_ref[0], slot, narrow)]
        else:
            target = out_ref.at[position_ref[0] ^ slot]
        copies.append(pltpu.make_async_copy(scaled_ref.at[slot], target, sems.at[slot]))
    for copy in copies:
        copy.start()
    for copy in copies:
        copy.wait()


def lane_place(position, slot, width):
    return pl.ds(pl.multiple_of((position ^ slot) * width, width), width)


def assemble_grad_kernel(shards, width, position_ref, *refs):
    queries, others, target, sems = refs[: shards - 1], refs[shards - 1 : -2], refs[-2], refs[-1]
    copies = []
    for slot in range(shards):
        lanes = lane_place(position_ref[0], slot, width)
        first = 0 if slot == 1 else 1
        copies.append((others[slot], target.at[first:3, :, lanes]))
        if slot != 1:
            copies.append((queries[min(slot, 1) + max(slot - 2, 0)], target.at[0, :, lanes]))
    copies = [
        pltpu.make_async_copy(source, view, sems.at[i]) for i, (source, view) in enumerate(copies)
    ]
    for copy in copies:
        copy.start()
    for copy in copies:
        copy.wait()


NEAR = pltpu.VMEM
FAR = pl.ANY


def run_kernel(kernel, scalars, arrays, outs, scratch, microseconds, name, sems=0):
    in_specs = [pl.BlockSpec(memory_space=pltpu.SMEM)] * len(scalars)
    operands = list(scalars)
    for array, space in arrays:
        operands.append(array)
        in_specs.append(pl.BlockSpec(memory_space=space))
    scratch_shapes = [pltpu.VMEM(s, d) for s, d in scratch]
    memory = 8 * 1024 * 1024 + sum(
        int(np.prod(s)) * jnp.dtype(d).itemsize for s, d in scratch
    )
    if sems:
        scratch_shapes.append(pltpu.SemaphoreType.DMA((sems,)))
    return pl.pallas_call(
        kernel,
        out_shape=[jax.ShapeDtypeStruct(s, d) for s, d, _ in outs],
        in_specs=in_specs,
        out_specs=[pl.BlockSpec(memory_space=space) for _, _, space in outs],
        scratch_shapes=scratch_shapes,
        compiler_params=pltpu.CompilerParams(vmem_limit_bytes=memory),
        cost_estimate=pl.CostEstimate(
            flops=int(microseconds * 1e9), bytes_accessed=0, transcendentals=0
        ),
        name=name,
    )(*operands)


def exchange(array, axis, bits):
    return lax.ppermute(array, axis, [(i, i ^ bits) for i in range(lax.axis_size(axis))])


def butterfly(sums, axis, radix):
    step = 1
    while step < lax.axis_size(axis):
        radix = min(radix, lax.axis_size(axis) // step)
        others = [exchange(sums, axis, step * k) for k in range(1, radix)]
        for other in others:
            sums = sums + other
        step *= radix
    return sums


def body(
    streams, record_blocks, tail_rows, unit_dest, mixer_filter, feat_filter, norm_gain, out_grad
):
    rows = streams.shape[1]
    channels = streams.shape[2]
    shards = lax.axis_size("seq")
    position = lax.axis_index("seq")
    total_channels = channels * lax.axis_size("fsdp")
    tokens = rows * shards
    blocks = tokens // KM
    units = tokens // UNIT
    units_dev = rows // UNIT
    narrow = channels // shards
    width = -(-narrow // LANES) * LANES

    def widen(array):
        if width == narrow:
            return array
        return jnp.pad(array, ((0, 0),) * (array.ndim - 1) + ((0, width - narrow),))

    def lane_parts(array):
        return [
            lax.dynamic_slice_in_dim(array, (position ^ slot) * narrow, narrow, array.ndim - 1)
            for slot in range(shards)
        ]

    def exchange_parts(parts):
        return [
            widen(exchange(part, "seq", slot) if slot else part)
            for slot, part in enumerate(parts)
        ]

    def to_tokens(pieces, slots):
        return [
            exchange(part[..., :narrow], "seq", slot) if slot else part[..., :narrow]
            for slot, part in zip(slots, pieces)
        ]

    every_slot = range(shards)

    position_word = position.astype(jnp.int32).reshape(1)
    layout = record_layout(record_blocks, tail_rows, blocks)
    unit_ids = jnp.arange(units, dtype=jnp.int32)
    loaded_unit = jnp.sum(
        jnp.where(unit_dest[None, :] == unit_ids[:, None], unit_ids[None, :], 0), axis=1
    ).astype(jnp.int32)
    slot = position ^ (loaded_unit // units_dev)
    unit_table = slot * units_dev + loaded_unit % units_dev
    analysis, synthesis_on, synthesis_back = (jnp.asarray(m) for m in transform_matrices())
    taps = widen(feat_filter.reshape(3 * KF, narrow))
    own_gain = norm_gain.reshape(1, narrow)
    gain = widen(own_gain)
    mixer = widen(mixer_filter)

    others = exchange_parts(lane_parts(streams[1:]))
    query_parts = lane_parts(streams[0])
    others[1], query_parts = lax.optimization_barrier((others[1], query_parts))
    queries = exchange_parts(query_parts)
    grad_parts = lane_parts(out_grad)
    queries[1], grad_parts = lax.optimization_barrier((queries[1], grad_parts))
    cotangents = exchange_parts(grad_parts)

    whole = (tokens, width)
    spectra = ((blocks // 2 + 1, 2 * KM, 2 * width), f32)
    extended_shape = (KM + HALO, width)
    scalars = (unit_table, layout)
    staged, features, response, filter_spectrum = run_kernel(
        lambda *refs: respond_kernel(shards, rows, *refs),
        scalars,
        [(part, FAR) for part in others]
        + [(a, NEAR) for a in (taps, mixer, analysis, synthesis_on)],
        (
            ((2,) + whole, bf16, NEAR), ((2,) + whole, bf16, NEAR), (whole, f32, NEAR),
            ((2 * KM, width), f32, NEAR),
        ),
        (((4,) + extended_shape, f32), ((blocks // 2, KM, 2 * width), bf16), spectra),
        6,
        "respond",
        sems=shards,
    )
    gate = run_kernel(
        lambda *refs: gate_kernel(shards, rows, *refs),
        scalars + (position_word,),
        [(part, FAR) for part in queries] + [(a, NEAR) for a in (response, taps, gain)],
        (
            (whole, bf16, NEAR), (whole, bf16, NEAR),
            ((shards, rows + UNIT, width), bf16, NEAR), ((blocks, KM), f32, NEAR),
        ) + (((rows + UNIT, width), bf16, FAR),) * shards,
        (((4,) + extended_shape, f32),),
        0.5,
        "gate",
        sems=shards,
    )
    staged_query, query_feature, gated, squares = gate[:4]
    gated_back = to_tokens(gate[4:], every_slot)
    cotangent, sums = run_kernel(
        lambda *refs: product_kernel(shards, rows, *refs),
        (position_word,),
        [(part, NEAR) for part in cotangents] + [(a, NEAR) for a in (gated, squares, gain)],
        ((whole, bf16, NEAR), ((2 * blocks, KM), f32, NEAR)),
        (),
        2,
        "product",
        sems=shards,
    )
    sums = butterfly(sums, "fsdp", 2)
    sums, gated_back = lax.optimization_barrier((sums, gated_back))
    sums = butterfly(sums, "seq", 4)
    norm = run_kernel(
        lambda *refs: norm_kernel(total_channels, shards, rows, *refs),
        scalars,
        [(a, NEAR) for a in (cotangent, response, taps, gain, query_feature, gated, sums)],
        ((whole, bf16, NEAR),) * 2 + (((rows, width), bf16, FAR),) * shards,
        ((whole, bf16), ((blocks + 1,) + extended_shape, f32)),
        3,
        "norm",
        sems=shards,
    )
    d_query, d_response = norm[:2]
    query_back = to_tokens(norm[2:3] + norm[4:], [slot for slot in every_slot if slot != 1])
    back = run_kernel(
        lambda *refs: mix_back_kernel(shards, rows, *refs),
        scalars,
        [
            (a, NEAR)
            for a in (
                taps, analysis, synthesis_back, features, filter_spectrum, d_response
            )
        ]
        + [(norm[3], FAR)],
        (((KM, width), f32, NEAR), ((2,) + whole, bf16, NEAR))
        + tuple(((3 if slot == 1 else 2, rows, width), bf16, FAR) for slot in every_slot),
        (
            ((2,) + whole, bf16), ((2, blocks + 1) + extended_shape, f32), spectra,
            ((2 * KM, width), f32),
        ),
        7,
        "mix_back",
        sems=shards + 1,
    )
    mixer_grad, d_others = back[:2]
    others_back = to_tokens(back[2:], every_slot)
    d_others, query_back = lax.optimization_barrier((d_others, query_back))
    taps_grad, gain_grad = run_kernel(
        lambda *refs: tap_grad_kernel(total_channels, *refs),
        scalars,
        [
            (a, NEAR)
            for a in (staged_query, staged, d_query, d_others, gated, cotangent, sums)
        ],
        (((3 * KF, width), f32, NEAR), ((1, width), f32, NEAR)),
        (((3,) + extended_shape, f32), ((3, 8 * KF, width), f32), ((8, width), f32)),
        4,
        "tap_grad",
    )
    aligned = width == narrow
    (out,) = run_kernel(
        lambda *refs: scale_out_kernel(total_channels, shards, rows, *refs),
        (layout, position_word),
        [(sums, NEAR)] + [(a, NEAR) for a in gated_back],
        (((rows, channels) if aligned else (shards, rows, narrow), bf16, FAR),),
        (((shards, rows, narrow), bf16),),
        2,
        "scale_out",
        sems=shards,
    )
    if aligned:
        (stream_grad,) = run_kernel(
            lambda *refs: assemble_grad_kernel(shards, width, *refs),
            (position_word,),
            [(a, NEAR) for a in query_back] + [(a, NEAR) for a in others_back],
            (((3, rows, channels), bf16, FAR),),
            (),
            1,
            "assemble_grad",
            sems=2 * shards,
        )
    else:
        def assemble(pieces):
            stacked = jnp.stack(pieces)
            in_place = jnp.take(stacked, position ^ jnp.arange(shards), axis=0)
            return jnp.moveaxis(in_place, 0, -2).reshape(pieces[0].shape[:-1] + (channels,))

        out = out.transpose(1, 0, 2).reshape(rows, channels)
        queries = query_back[:1] + [others_back[1][0]] + query_back[1:]
        others_back[1] = others_back[1][1:]
        stream_grad = jnp.concatenate([assemble(queries)[None], assemble(others_back)])
    feat_grad = taps_grad[:, :narrow].reshape(KF, 3, narrow)
    return (out, stream_grad, mixer_grad[:, :narrow], feat_grad, gain_grad[0, :narrow])


def solution(mesh):
    placed = (
        P(None, "seq", "fsdp"),
        P(),
        P(),
        P(),
        P(None, ("fsdp", "seq")),
        P(None, None, ("fsdp", "seq")),
        P(("fsdp", "seq")),
        P("seq", "fsdp"),
    )
    return jax.shard_map(
        body,
        mesh=mesh,
        in_specs=placed,
        out_specs=(
            P("seq", "fsdp"),
            P(None, "seq", "fsdp"),
            P(None, ("fsdp", "seq")),
            P(None, None, ("fsdp", "seq")),
            P(("fsdp", "seq")),
        ),
        check_vma=False,
    )
```

time: 117 us -> 108 us (0.923); the launches traced: 117 us -> 106 us
  waiting for transfers between devices: 56.4 us -> 38.6 us
  starting transfers between devices: 25.2 us -> 37 us
  Pallas kernels: 30.7 us -> 25.1 us
    ppermute x19 -> x23, waiting for transfers between devices: 56.4 us -> 38.6 us  [exchange(): lax.ppermute(array, axis, [(i, i ^ bits) for i in range(lax.axis_size(axi...]
    ppermute x19 -> x23, starting transfers between devices: 25.2 us -> 37 us  [exchange(): lax.ppermute(array, axis, [(i, i ^ bits) for i in range(lax.axis_size(axi...]
    pallas_call x8, Pallas kernels: 30.7 us -> 25.1 us  [run_kernel(): pl.pallas_call(kernel, out_shape=[jax.ShapeDtypeStruct(s, d) for s, d, _...]
    slice x0 -> x3, local copies, waits for them, and re-layouts: none -> 2.32 us  [the longest x2 1.2 us: body(): others = exchange_parts(lane_parts(streams[1:]))]
    dynamic_slice x2 -> x3, local copies, waits for them, and re-layouts: 2.41 us -> 1.09 us  [lane_parts(): lax.dynamic_slice_in_dim(array, (position ^ slot) * narrow, narrow, array...]
  transfers between devices with their start and end apart: 19 -> 23, of which waited for: 9 -> 10; matrix products, arithmetic and copies ran while one was open for 1% -> 3% of each run, Pallas kernels for 20% -> 20%
where the time goes in v2:
time: 108 us; the launch traced here: 106 us
  waiting for transfers between devices  38.6 us (36%)
  starting transfers between devices  37 us (34%)
  Pallas kernels  25.1 us (23%)
  local copies, waits for them, and re-layouts  4.09 us (4%)
    ppermute x23, waiting for transfers between devices, exchange(): lax.ppermute(array, axis, [(i, i ^ bits) for i in range(lax.axis_size(axi...  38.6 us
    ppermute x23, starting transfers between devices, exchange(): lax.ppermute(array, axis, [(i, i ^ bits) for i in range(lax.axis_size(axi...  37 us
    pallas_call x8, Pallas kernels, run_kernel(): pl.pallas_call(kernel, out_shape=[jax.ShapeDtypeStruct(s, d) for s, d, _...  25.1 us
  transfers between devices with their start and end apart: 23, of which 10 were waited for; matrix products, arithmetic and copies ran while one was open for 3% of the time, Pallas kernels for 20%

profile of v2, /device:TPU:0, one launch (start us, length us, event | category | flops | bytes accessed | tf_op | source)
XLA Modules:
  0.0 106.3 jit_solution(6557803044516733943)
XLA Ops:
  2.1 5.1 %collective-permute-start.8 = (bf16[2,512,128]{2,1,0:T(8,128)(2,1)S(1)}, bf16[2,512,128]{2,1,0:T(8,128)(2,1)S(1)}, u32[]{:S(2)}, u32[]{:S(2)}) collective-permute-start(bf16[2,512,128]{2,1,0:T(8,128)(2,1)S(1)} %get-tuple-element.116), channel_id=1, source_target_pairs={{0,3},{1,2},{2,1},{3,0},{4,7},{5,6},{6,5},{7,4},{8,11},{9,10},{10,... | collective-permute-start | bytes 786440 | tf_op jit(solution)/shard_map/ppermute | solution.py:573
  10.3 13.8 %collective-permute-done.refs_3_ = bf16[2,512,128]{2,1,0:T(8,128)(2,1)S(1)} collective-permute-done((bf16[2,512,128]{2,1,0:T(8,128)(2,1)S(1)}, bf16[2,512,128]{2,1,0:T(8,128)(2,1)S(1)}, u32[]{:S(2)}, u32[]{:S(2)}) %collective-permute-start) | collective-permute-done | bytes 262176 | tf_op jit(solution)/shard_map/ppermute | solution.py:573
  24.1 2.5 %collective-permute-start.1 = (bf16[512,128]{1,0:T(8,128)(2,1)}, bf16[512,128]{1,0:T(8,128)(2,1)S(1)}, u32[]{:S(2)}, u32[]{:S(2)}) collective-permute-start(bf16[512,128]{1,0:T(8,128)(2,1)} %get-tuple-element.52), channel_id=1, source_target_pairs={{0,1},{1,0},{2,3},{3,2},{4,5},{5,4},{6,7},{7,6},{8,9},{9,8},{10,11... | collective-permute-start | bytes 393224 | tf_op jit(solution)/shard_map/ppermute | solution.py:573
  26.8 2.4 %collective-permute-start.6 = (bf16[512,128]{1,0:T(8,128)(2,1)S(1)}, bf16[512,128]{1,0:T(8,128)(2,1)S(1)}, u32[]{:S(2)}, u32[]{:S(2)}) collective-permute-start(bf16[512,128]{1,0:T(8,128)(2,1)S(1)} %get-tuple-element.60), channel_id=1, source_target_pairs={{0,3},{1,2},{2,1},{3,0},{4,7},{5,6},{6,5},{7,4},{8,11},{9,10},{10,... | collective-permute-start | bytes 393224 | tf_op jit(solution)/shard_map/ppermute | solution.py:573
  29.2 4.7 %collective-permute-done.1.refs_4_ = bf16[512,128]{1,0:T(8,128)(2,1)S(1)} collective-permute-done((bf16[512,128]{1,0:T(8,128)(2,1)}, bf16[512,128]{1,0:T(8,128)(2,1)S(1)}, u32[]{:S(2)}, u32[]{:S(2)}) %collective-permute-start.1) | collective-permute-done | bytes 131104 | tf_op jit(solution)/shard_map/ppermute | solution.py:573
  33.9 3.7 %collective-permute-start.3 = (bf16[512,128]{1,0:T(8,128)(2,1)S(1)}, bf16[512,128]{1,0:T(8,128)(2,1)S(1)}, u32[]{:S(2)}, u32[]{:S(2)}) collective-permute-start(bf16[512,128]{1,0:T(8,128)(2,1)S(1)} %get-tuple-element.55), channel_id=1, source_target_pairs={{0,2},{1,3},{2,0},{3,1},{4,6},{5,7},{6,4},{7,5},{8,10},{9,11},{10,... | collective-permute-start | bytes 393224 | tf_op jit(solution)/shard_map/ppermute | solution.py:573
  38.9 4.9 %respond.1 = (bf16[2,2048,128]{2,1,0:T(8,128)(2,1)S(1)}, bf16[2,2048,128]{2,1,0:T(8,128)(2,1)S(1)}, f32[2048,128]{1,0:T(8,128)S(1)}, f32[256,128]{1,0:T(8,128)S(1)}) custom-call(s32[128]{0:T(128)S(1)} %fusion.3.refs_0_, s32[3,16]{1,0:T(4,128)S(1)} %pad_add_fusion.refs_1_.refs_0_, bf16[2,512,128]{2,1,0:T(8,128)(2,1)S(1)} %get-tuple-element.118.refs_2_, ...), custom_call_target="tpu_custom_call" | custom-call | flops 6000000000 | tf_op jit(solution)/shard_map/respond/pallas_call | solution.py:558
  43.8 3.8 %gate.1 = (bf16[2048,128]{1,0:T(8,128)(2,1)S(1)}, bf16[2048,128]{1,0:T(8,128)(2,1)S(1)}, bf16[4,528,128]{2,1,0:T(8,128)(2,1)S(1)}, f32[16,128]{1,0:T(8,128)S(1)}...) custom-call(s32[128]{0:T(128)S(1)} %fusion.3.refs_0_, ...), custom_call_target="tpu_custom_call" | custom-call | flops 500000000 | tf_op jit(solution)/shard_map/gate/pallas_call | solution.py:558
  47.6 3.7 %collective-permute-start.12 = (bf16[528,128]{1,0:T(8,128)(2,1)S(1)}, bf16[528,128]{1,0:T(8,128)(2,1)S(1)}, u32[]{:S(2)}, u32[]{:S(2)}) collective-permute-start(bf16[528,128]{1,0:T(8,128)(2,1)S(1)} %get-tuple-element.67), channel_id=1, source_target_pairs={{0,1},{1,0},{2,3},{3,2},{4,5},{5,4},{6,7},{7,6},{8,9},{9,8},{10,11... | collective-permute-start | bytes 405512 | tf_op jit(solution)/shard_map/ppermute | solution.py:573
  51.3 1.8 %collective-permute-start.13 = (bf16[528,128]{1,0:T(8,128)(2,1)S(1)}, bf16[528,128]{1,0:T(8,128)(2,1)S(1)}, u32[]{:S(2)}, u32[]{:S(2)}) collective-permute-start(bf16[528,128]{1,0:T(8,128)(2,1)S(1)} %get-tuple-element.68), channel_id=1, source_target_pairs={{0,2},{1,3},{2,0},{3,1},{4,6},{5,7},{6,4},{7,5},{8,10},{9,11},{10,... | collective-permute-start | bytes 405512 | tf_op jit(solution)/shard_map/ppermute | solution.py:573
  56.8 1.5 %collective-permute-start.10 = (f32[32,128]{1,0:T(8,128)S(1)}, f32[32,128]{1,0:T(8,128)S(1)}, u32[]{:S(2)}, u32[]{:S(2)}) collective-permute-start(f32[32,128]{1,0:T(8,128)S(1)} %add.69), channel_id=1, source_target_pairs={{0,8},{4,12},{8,0},{12,4},{16,24},{20,28},{24,16},{28,20},{1,9},{5... | collective-permute-start | bytes 49160 | tf_op jit(solution)/shard_map/ppermute | solution.py:573
  58.3 2.2 %collective-permute-done.10 = f32[32,128]{1,0:T(8,128)S(1)} collective-permute-done((f32[32,128]{1,0:T(8,128)S(1)}, f32[32,128]{1,0:T(8,128)S(1)}, u32[]{:S(2)}, u32[]{:S(2)}) %collective-permute-start.10) | collective-permute-done | bytes 16416 | tf_op jit(solution)/shard_map/ppermute | solution.py:573
  60.6 1.5 %collective-permute-start.11 = (f32[32,128]{1,0:T(8,128)S(1)}, f32[32,128]{1,0:T(8,128)S(1)}, u32[]{:S(2)}, u32[]{:S(2)}) collective-permute-start(f32[32,128]{1,0:T(8,128)S(1)} %add.70), channel_id=1, source_target_pairs={{0,16},{4,20},{8,24},{12,28},{16,0},{20,4},{24,8},{28,12},{1,17},{... | collective-permute-start | bytes 49160 | tf_op jit(solution)/shard_map/ppermute | solution.py:573
  62.1 2.2 %collective-permute-done.11 = f32[32,128]{1,0:T(8,128)S(1)} collective-permute-done((f32[32,128]{1,0:T(8,128)S(1)}, f32[32,128]{1,0:T(8,128)S(1)}, u32[]{:S(2)}, u32[]{:S(2)}) %collective-permute-start.11) | collective-permute-done | bytes 16416 | tf_op jit(solution)/shard_map/ppermute | solution.py:573
  64.4 2.5 %collective-permute-start.17 = (f32[32,128]{1,0:T(8,128)S(1)}, f32[32,128]{1,0:T(8,128)S(1)}, u32[]{:S(2)}, u32[]{:S(2)}) collective-permute-start(f32[32,128]{1,0:T(8,128)S(1)} %add.71), channel_id=1, source_target_pairs={{0,3},{1,2},{2,1},{3,0},{4,7},{5,6},{6,5},{7,4},{8,11},{9,10},{10,... | collective-permute-start | bytes 49160 | tf_op jit(solution)/shard_map/ppermute | solution.py:573
  66.9 1.9 %collective-permute-start.15 = (f32[32,128]{1,0:T(8,128)S(1)}, f32[32,128]{1,0:T(8,128)S(1)}, u32[]{:S(2)}, u32[]{:S(2)}) collective-permute-start(f32[32,128]{1,0:T(8,128)S(1)} %add.71), channel_id=1, source_target_pairs={{0,1},{1,0},{2,3},{3,2},{4,5},{5,4},{6,7},{7,6},{8,9},{9,8},{10,11... | collective-permute-start | bytes 49160 | tf_op jit(solution)/shard_map/ppermute | solution.py:573
  71.5 3.0 %norm.1 = (bf16[2048,128]{1,0:T(8,128)(2,1)S(1)}, bf16[2048,128]{1,0:T(8,128)(2,1)S(1)}, bf16[512,128]{1,0:T(8,128)(2,1)S(1)}, bf16[512,128]{1,0:T(8,128)(2,1)S(...) custom-call(s32[128]{0:T(128)S(1)} %fusion.3.refs_0_, s32[3,16]{1,0:T(4,128)S(1)} %pad_add_fusion.refs_1_.refs_0_, ...), custom_call_target="tpu_custom_call" | custom-call | flops 3000000000 | tf_op jit(solution)/shard_map/norm/pallas_call | solution.py:558
  74.6 2.1 %collective-permute-start.18 = (bf16[512,128]{1,0:T(8,128)(2,1)S(1)}, bf16[512,128]{1,0:T(8,128)(2,1)S(1)}, u32[]{:S(2)}, u32[]{:S(2)}) collective-permute-start(bf16[512,128]{1,0:T(8,128)(2,1)S(1)} %get-tuple-element.83), channel_id=1, source_target_pairs={{0,2},{1,3},{2,0},{3,1},{4,6},{5,7},{6,4},{7,5},{8,10},{9,11},{10,... | collective-permute-start | bytes 393224 | tf_op jit(solution)/shard_map/ppermute | solution.py:573
  78.0 5.6 %mix_back.1 = (f32[128,128]{1,0:T(8,128)}, bf16[2,2048,128]{2,1,0:T(8,128)(2,1)S(1)}, bf16[2,512,128]{2,1,0:T(8,128)(2,1)S(1)}, bf16[3,512,128]{2,1,0:T(8,128)(2...) custom-call(s32[128]{0:T(128)S(1)} %fusion.3.refs_0_, ...), custom_call_target="tpu_custom_call" | custom-call | flops 7000000000 | tf_op jit(solution)/shard_map/mix_back/pallas_call | solution.py:558
  84.0 2.3 %collective-permute-start.22 = (bf16[2,512,128]{2,1,0:T(8,128)(2,1)S(1)}, bf16[2,512,128]{2,1,0:T(8,128)(2,1)S(1)}, u32[]{:S(2)}, u32[]{:S(2)}) collective-permute-start(bf16[2,512,128]{2,1,0:T(8,128)(2,1)S(1)} %get-tuple-element.91), channel_id=1, source_target_pairs={{0,3},{1,2},{2,1},{3,0},{4,7},{5,6},{6,5},{7,4},{8,11},{9,10},{10,... | collective-permute-start | bytes 786440 | tf_op jit(solution)/shard_map/ppermute | solution.py:573
  87.2 1.9 %scale_out.1 = bf16[512,512]{1,0:T(8,128)(2,1)} custom-call(s32[3,16]{1,0:T(4,128)S(1)} %pad_add_fusion.refs_1_.refs_0_, s32[1]{0:T(128)} %bitcast.5.refs_2_.refs_0_.refs_1_, f32[32,128]{1,0:T(8,128)S(1)} %add_add_fusion.refs_2_.refs_8_, bf16[528,128]{1,0:T(8,128)(2,1)S(1)} %get-tuple-element.71.refs_3_, ...), custom_call_target="tpu_custom_call" | custom-call | flops 2000000000 | tf_op jit(solution)/shard_map/scale_out/pallas_call | solution.py:558
  89.1 4.0 %collective-permute-done.18.refs_2_ = bf16[512,128]{1,0:T(8,128)(2,1)S(1)} collective-permute-done((bf16[512,128]{1,0:T(8,128)(2,1)S(1)}, bf16[512,128]{1,0:T(8,128)(2,1)S(1)}, u32[]{:S(2)}, u32[]{:S(2)}) %collective-permute-start.18) | collective-permute-done | bytes 131104 | tf_op jit(solution)/shard_map/ppermute | solution.py:573
  93.1 3.6 %tap_grad.1 = (f32[21,128]{1,0:T(8,128)S(1)}, f32[1,128]{1,0:T(1,128)}) custom-call(s32[128]{0:T(128)S(1)} %fusion.3.refs_0_, s32[3,16]{1,0:T(4,128)S(1)} %pad_add_fusion.refs_1_.refs_0_, bf16[2048,128]{1,0:T(8,128)(2,1)S(1)} %get-tuple-element.93.refs_2_, bf16[2,2048,128]{2,1,0:T(8,128)(2,1)S(1)} %get-tuple-element.94.refs_3_, ...), custom_call_target="tpu_custom_call" | custom-call | flops 4000000000 | tf_op jit(solution)/shard_map/tap_grad/pallas_call | solution.py:558
  97.3 7.2 %collective-permute-done.21.refs_6_ = bf16[2,512,128]{2,1,0:T(8,128)(2,1)S(1)} collective-permute-done((bf16[2,512,128]{2,1,0:T(8,128)(2,1)S(1)}, bf16[2,512,128]{2,1,0:T(8,128)(2,1)S(1)}, u32[]{:S(2)}, u32[]{:S(2)}) %collective-permute-start.21) | collective-permute-done | bytes 262176 | tf_op jit(solution)/shard_map/ppermute | solution.py:573
  (75 shorter events, 17.6 us)
Async XLA Ops:
  2.1 31.8 %collective-permute-start.8 = (bf16[2,512,128]{2,1,0:T(8,128)(2,1)S(1)}, bf16[2,512,128]{2,1,0:T(8,128)(2,1)S(1)}, u32[]{:S(2)}, u32[]{:S(2)}) collective-permute-start(bf16[2,512,128]{2,1,0:T(8,128)(2,1)S(1)} %get-tuple-element.116), channel_id=1, source_target_pairs={{0,3},{1,2},{2,1},{3,0},{4,7},{5,6},{6,5},{7,4},{8,11},{9,10},{10,... | collective-permute-start | bytes 786440 | tf_op jit(solution)/shard_map/ppermute | solution.py:573
  7.2 30.3 %collective-permute-start.7 = (bf16[2,512,128]{2,1,0:T(8,128)(2,1)S(1)}, bf16[2,512,128]{2,1,0:T(8,128)(2,1)S(1)}, u32[]{:S(2)}, u32[]{:S(2)}) collective-permute-start(bf16[2,512,128]{2,1,0:T(8,128)(2,1)S(1)} %get-tuple-element.117), channel_id=1, source_target_pairs={{0,2},{1,3},{2,0},{3,1},{4,6},{5,7},{6,4},{7,5},{8,10},{9,11},{10,... | collective-permute-start | bytes 786440 | tf_op jit(solution)/shard_map/ppermute | solution.py:573
  7.2 16.9 %collective-permute-start = (bf16[2,512,128]{2,1,0:T(8,128)(2,1)S(1)}, bf16[2,512,128]{2,1,0:T(8,128)(2,1)S(1)}, u32[]{:S(2)}, u32[]{:S(2)}) collective-permute-start(bf16[2,512,128]{2,1,0:T(8,128)(2,1)S(1)} %get-tuple-element.119), channel_id=1, source_target_pairs={{0,1},{1,0},{2,3},{3,2},{4,5},{5,4},{6,7},{7,6},{8,9},{9,8},{10,11... | collective-permute-start | bytes 786440 | tf_op jit(solution)/shard_map/ppermute | solution.py:573
  7.9 31.0 %copy-start.4 = (bf16[256,256]{1,0:T(8,128)(2,1)S(1)}, bf16[256,256]{1,0:T(8,128)(2,1)}, u32[]{:S(2)}) copy-start(bf16[256,256]{1,0:T(8,128)(2,1)} %constant.65.clone.refs_9_) | copy-start | bytes 393220
  24.1 9.8 %collective-permute-start.1 = (bf16[512,128]{1,0:T(8,128)(2,1)}, bf16[512,128]{1,0:T(8,128)(2,1)S(1)}, u32[]{:S(2)}, u32[]{:S(2)}) collective-permute-start(bf16[512,128]{1,0:T(8,128)(2,1)} %get-tuple-element.52), channel_id=1, source_target_pairs={{0,1},{1,0},{2,3},{3,2},{4,5},{5,4},{6,7},{7,6},{8,9},{9,8},{10,11... | collective-permute-start | bytes 393224 | tf_op jit(solution)/shard_map/ppermute | solution.py:573
  26.7 17.1 %collective-permute-start.5 = (bf16[512,128]{1,0:T(8,128)(2,1)}, bf16[512,128]{1,0:T(8,128)(2,1)S(1)}, u32[]{:S(2)}, u32[]{:S(2)}) collective-permute-start(bf16[512,128]{1,0:T(8,128)(2,1)} %get-tuple-element.59), channel_id=1, source_target_pairs={{0,2},{1,3},{2,0},{3,1},{4,6},{5,7},{6,4},{7,5},{8,10},{9,11},{10,... | collective-permute-start | bytes 393224 | tf_op jit(solution)/shard_map/ppermute | solution.py:573
  26.8 17.0 %collective-permute-start.6 = (bf16[512,128]{1,0:T(8,128)(2,1)S(1)}, bf16[512,128]{1,0:T(8,128)(2,1)S(1)}, u32[]{:S(2)}, u32[]{:S(2)}) collective-permute-start(bf16[512,128]{1,0:T(8,128)(2,1)S(1)} %get-tuple-element.60), channel_id=1, source_target_pairs={{0,3},{1,2},{2,1},{3,0},{4,7},{5,6},{6,5},{7,4},{8,11},{9,10},{10,... | collective-permute-start | bytes 393224 | tf_op jit(solution)/shard_map/ppermute | solution.py:573
  33.9 19.2 %collective-permute-start.2 = (bf16[512,128]{1,0:T(8,128)(2,1)S(1)}, bf16[512,128]{1,0:T(8,128)(2,1)S(1)}, u32[]{:S(2)}, u32[]{:S(2)}) collective-permute-start(bf16[512,128]{1,0:T(8,128)(2,1)S(1)} %get-tuple-element.54), channel_id=1, source_target_pairs={{0,1},{1,0},{2,3},{3,2},{4,5},{5,4},{6,7},{7,6},{8,9},{9,8},{10,11... | collective-permute-start | bytes 393224 | tf_op jit(solution)/shard_map/ppermute | solution.py:573
  33.9 20.6 %collective-permute-start.3 = (bf16[512,128]{1,0:T(8,128)(2,1)S(1)}, bf16[512,128]{1,0:T(8,128)(2,1)S(1)}, u32[]{:S(2)}, u32[]{:S(2)}) collective-permute-start(bf16[512,128]{1,0:T(8,128)(2,1)S(1)} %get-tuple-element.55), channel_id=1, source_target_pairs={{0,2},{1,3},{2,0},{3,1},{4,6},{5,7},{6,4},{7,5},{8,10},{9,11},{10,... | collective-permute-start | bytes 393224 | tf_op jit(solution)/shard_map/ppermute | solution.py:573
  37.5 16.9 %collective-permute-start.4 = (bf16[512,128]{1,0:T(8,128)(2,1)S(1)}, bf16[512,128]{1,0:T(8,128)(2,1)S(1)}, u32[]{:S(2)}, u32[]{:S(2)}) collective-permute-start(bf16[512,128]{1,0:T(8,128)(2,1)S(1)} %get-tuple-element.56), channel_id=1, source_target_pairs={{0,3},{1,2},{2,1},{3,0},{4,7},{5,6},{6,5},{7,4},{8,11},{9,10},{10,... | collective-permute-start | bytes 393224 | tf_op jit(solution)/shard_map/ppermute | solution.py:573
  47.6 16.7 %collective-permute-start.12 = (bf16[528,128]{1,0:T(8,128)(2,1)S(1)}, bf16[528,128]{1,0:T(8,128)(2,1)S(1)}, u32[]{:S(2)}, u32[]{:S(2)}) collective-permute-start(bf16[528,128]{1,0:T(8,128)(2,1)S(1)} %get-tuple-element.67), channel_id=1, source_target_pairs={{0,1},{1,0},{2,3},{3,2},{4,5},{5,4},{6,7},{7,6},{8,9},{9,8},{10,11... | collective-permute-start | bytes 405512 | tf_op jit(solution)/shard_map/ppermute | solution.py:573
  51.3 13.0 %collective-permute-start.13 = (bf16[528,128]{1,0:T(8,128)(2,1)S(1)}, bf16[528,128]{1,0:T(8,128)(2,1)S(1)}, u32[]{:S(2)}, u32[]{:S(2)}) collective-permute-start(bf16[528,128]{1,0:T(8,128)(2,1)S(1)} %get-tuple-element.68), channel_id=1, source_target_pairs={{0,2},{1,3},{2,0},{3,1},{4,6},{5,7},{6,4},{7,5},{8,10},{9,11},{10,... | collective-permute-start | bytes 405512 | tf_op jit(solution)/shard_map/ppermute | solution.py:573
  53.1 11.3 %collective-permute-start.14 = (bf16[528,128]{1,0:T(8,128)(2,1)S(1)}, bf16[528,128]{1,0:T(8,128)(2,1)S(1)}, u32[]{:S(2)}, u32[]{:S(2)}) collective-permute-start(bf16[528,128]{1,0:T(8,128)(2,1)S(1)} %get-tuple-element.69), channel_id=1, source_target_pairs={{0,3},{1,2},{2,1},{3,0},{4,7},{5,6},{6,5},{7,4},{8,11},{9,10},{10,... | collective-permute-start | bytes 405512 | tf_op jit(solution)/shard_map/ppermute | solution.py:573
  55.6 1.2 %collective-permute-start.9 = (f32[32,128]{1,0:T(8,128)S(1)}, f32[32,128]{1,0:T(8,128)S(1)}, u32[]{:S(2)}, u32[]{:S(2)}) collective-permute-start(f32[32,128]{1,0:T(8,128)S(1)} %get-tuple-element.65), channel_id=1, source_target_pairs={{0,4},{4,0},{8,12},{12,8},{16,20},{20,16},{24,28},{28,24},{1,5},{5... | collective-permute-start | bytes 49160 | tf_op jit(solution)/shard_map/ppermute | solution.py:573
  56.8 3.7 %collective-permute-start.10 = (f32[32,128]{1,0:T(8,128)S(1)}, f32[32,128]{1,0:T(8,128)S(1)}, u32[]{:S(2)}, u32[]{:S(2)}) collective-permute-start(f32[32,128]{1,0:T(8,128)S(1)} %add.69), channel_id=1, source_target_pairs={{0,8},{4,12},{8,0},{12,4},{16,24},{20,28},{24,16},{28,20},{1,9},{5... | collective-permute-start | bytes 49160 | tf_op jit(solution)/shard_map/ppermute | solution.py:573
  60.6 3.7 %collective-permute-start.11 = (f32[32,128]{1,0:T(8,128)S(1)}, f32[32,128]{1,0:T(8,128)S(1)}, u32[]{:S(2)}, u32[]{:S(2)}) collective-permute-start(f32[32,128]{1,0:T(8,128)S(1)} %add.70), channel_id=1, source_target_pairs={{0,16},{4,20},{8,24},{12,28},{16,0},{20,4},{24,8},{28,12},{1,17},{... | collective-permute-start | bytes 49160 | tf_op jit(solution)/shard_map/ppermute | solution.py:573
  64.4 5.7 %collective-permute-start.17 = (f32[32,128]{1,0:T(8,128)S(1)}, f32[32,128]{1,0:T(8,128)S(1)}, u32[]{:S(2)}, u32[]{:S(2)}) collective-permute-start(f32[32,128]{1,0:T(8,128)S(1)} %add.71), channel_id=1, source_target_pairs={{0,3},{1,2},{2,1},{3,0},{4,7},{5,6},{6,5},{7,4},{8,11},{9,10},{10,... | collective-permute-start | bytes 49160 | tf_op jit(solution)/shard_map/ppermute | solution.py:573
  66.9 4.6 %collective-permute-start.16 = (f32[32,128]{1,0:T(8,128)S(1)}, f32[32,128]{1,0:T(8,128)S(1)}, u32[]{:S(2)}, u32[]{:S(2)}) collective-permute-start(f32[32,128]{1,0:T(8,128)S(1)} %add.71), channel_id=1, source_target_pairs={{0,2},{1,3},{2,0},{3,1},{4,6},{5,7},{6,4},{7,5},{8,10},{9,11},{10,... | collective-permute-start | bytes 49160 | tf_op jit(solution)/shard_map/ppermute | solution.py:573
  66.9 4.6 %collective-permute-start.15 = (f32[32,128]{1,0:T(8,128)S(1)}, f32[32,128]{1,0:T(8,128)S(1)}, u32[]{:S(2)}, u32[]{:S(2)}) collective-permute-start(f32[32,128]{1,0:T(8,128)S(1)} %add.71), channel_id=1, source_target_pairs={{0,1},{1,0},{2,3},{3,2},{4,5},{5,4},{6,7},{7,6},{8,9},{9,8},{10,11... | collective-permute-start | bytes 49160 | tf_op jit(solution)/shard_map/ppermute | solution.py:573
  74.6 18.5 %collective-permute-start.18 = (bf16[512,128]{1,0:T(8,128)(2,1)S(1)}, bf16[512,128]{1,0:T(8,128)(2,1)S(1)}, u32[]{:S(2)}, u32[]{:S(2)}) collective-permute-start(bf16[512,128]{1,0:T(8,128)(2,1)S(1)} %get-tuple-element.83), channel_id=1, source_target_pairs={{0,2},{1,3},{2,0},{3,1},{4,6},{5,7},{6,4},{7,5},{8,10},{9,11},{10,... | collective-permute-start | bytes 393224 | tf_op jit(solution)/shard_map/ppermute | solution.py:573
  76.7 16.4 %collective-permute-start.19 = (bf16[512,128]{1,0:T(8,128)(2,1)S(1)}, bf16[512,128]{1,0:T(8,128)(2,1)S(1)}, u32[]{:S(2)}, u32[]{:S(2)}) collective-permute-start(bf16[512,128]{1,0:T(8,128)(2,1)S(1)} %get-tuple-element.84), channel_id=1, source_target_pairs={{0,3},{1,2},{2,1},{3,0},{4,7},{5,6},{6,5},{7,4},{8,11},{9,10},{10,... | collective-permute-start | bytes 393224 | tf_op jit(solution)/shard_map/ppermute | solution.py:573
  83.7 20.8 %collective-permute-start.21 = (bf16[2,512,128]{2,1,0:T(8,128)(2,1)S(1)}, bf16[2,512,128]{2,1,0:T(8,128)(2,1)S(1)}, u32[]{:S(2)}, u32[]{:S(2)}) collective-permute-start(bf16[2,512,128]{2,1,0:T(8,128)(2,1)S(1)} %get-tuple-element.90), channel_id=1, source_target_pairs={{0,2},{1,3},{2,0},{3,1},{4,6},{5,7},{6,4},{7,5},{8,10},{9,11},{10,... | collective-permute-start | bytes 786440 | tf_op jit(solution)/shard_map/ppermute | solution.py:573
  84.0 20.5 %collective-permute-start.22 = (bf16[2,512,128]{2,1,0:T(8,128)(2,1)S(1)}, bf16[2,512,128]{2,1,0:T(8,128)(2,1)S(1)}, u32[]{:S(2)}, u32[]{:S(2)}) collective-permute-start(bf16[2,512,128]{2,1,0:T(8,128)(2,1)S(1)} %get-tuple-element.91), channel_id=1, source_target_pairs={{0,3},{1,2},{2,1},{3,0},{4,7},{5,6},{6,5},{7,4},{8,11},{9,10},{10,... | collective-permute-start | bytes 786440 | tf_op jit(solution)/shard_map/ppermute | solution.py:573
  86.3 18.9 %collective-permute-start.20 = (bf16[3,512,128]{2,1,0:T(8,128)(2,1)S(1)}, bf16[3,512,128]{2,1,0:T(8,128)(2,1)S(1)}, u32[]{:S(2)}, u32[]{:S(2)}) collective-permute-start(bf16[3,512,128]{2,1,0:T(8,128)(2,1)S(1)} %get-tuple-element.89), channel_id=1, source_target_pairs={{0,1},{1,0},{2,3},{3,2},{4,5},{5,4},{6,7},{7,6},{8,9},{9,8},{10,11... | collective-permute-start | bytes 1179656 | tf_op jit(solution)/shard_map/ppermute | solution.py:573
  (10 other events, 145.6 us)

commit v3 on v2

--- a/solution.py
+++ b/solution.py
@@ -211,12 +211,12 @@
 
 
 def gate_kernel(shards, rows, *refs):
-    unit_ref, layout_ref, position_ref = refs[:3]
-    pieces = refs[3 : 3 + shards]
-    response_ref, taps_ref, gain_ref = refs[3 + shards : 6 + shards]
-    staged_ref, feature_ref, gated_ref, squares_ref = refs[6 + shards : 10 + shards]
-    leaving = refs[10 + shards : 10 + 2 * shards]
-    extended_ref, sems = refs[10 + 2 * shards :]
+    unit_ref, layout_ref = refs[:2]
+    pieces = refs[2 : 2 + shards]
+    (
+        response_ref, taps_ref, gain_ref, staged_ref, feature_ref, gated_ref, squares_ref,
+        extended_ref, sems,
+    ) = refs[2 + shards :]
     width = staged_ref.shape[1]
     blocks = staged_ref.shape[0] // KM
     arrivals = [
@@ -244,6 +244,11 @@
         squares_ref[pl.ds(block, 1), :] = sum_lanes(gated * gated)
 
     repeat(blocks, 4, gate_block)
+
+
+def pack_kernel(shards, *refs):
+    position_ref, gated_ref = refs[:2]
+    leaving, sems = refs[2 : 2 + shards], refs[2 + shards]
     departures = [
         pltpu.make_async_copy(gated_ref.at[position_ref[0] ^ slot], target, sems.at[slot])
         for slot, target in enumerate(leaving)
@@ -362,8 +367,17 @@
         spread_rows = spread(ahead_ref.at[block + 1], taps_ref, 0)
         store_units(grad_ref, unit_ref, block, spread_rows)
 
-    repeat(blocks, 2, scale_block)
-    repeat(blocks, 2, spread_block)
+    scale_block(blocks - 1, 0)
+    scale_block(blocks - 2, 1)
+
+    def both(index, offset):
+        block = blocks - 3 - index
+        scale_block(block, offset)
+        spread_block(block + 2, offset)
+
+    repeat(blocks - 2, 2, both)
+    spread_block(1, 0)
+    spread_block(0, 1)
     send_slots(grad_ref, leaving, rows, sems)
 
 
@@ -664,21 +678,19 @@
         "respond",
         sems=shards,
     )
-    gate = run_kernel(
+    staged_query, query_feature, gated, squares = run_kernel(
         lambda *refs: gate_kernel(shards, rows, *refs),
-        scalars + (position_word,),
+        scalars,
         [(part, FAR) for part in queries] + [(a, NEAR) for a in (response, taps, gain)],
         (
             (whole, bf16, NEAR), (whole, bf16, NEAR),
             ((shards, rows + UNIT, width), bf16, NEAR), ((blocks, KM), f32, NEAR),
-        ) + (((rows + UNIT, width), bf16, FAR),) * shards,
+        ),
         (((4,) + extended_shape, f32),),
         0.5,
         "gate",
         sems=shards,
     )
-    staged_query, query_feature, gated, squares = gate[:4]
-    gated_back = to_tokens(gate[4:], every_slot)
     cotangent, sums = run_kernel(
         lambda *refs: product_kernel(shards, rows, *refs),
         (position_word,),
@@ -689,20 +701,33 @@
         "product",
         sems=shards,
     )
+    sums, ready_gated = lax.optimization_barrier((sums, gated))
+    gated_pieces = run_kernel(
+        lambda *refs: pack_kernel(shards, *refs),
+        (position_word,),
+        [(ready_gated, NEAR)],
+        (((rows + UNIT, width), bf16, FAR),) * shards,
+        (),
+        1,
+        "pack",
+        sems=shards,
+    )
+    sums = butterfly(sums, "seq", 4)
+    gated_far = to_tokens(gated_pieces[2:], every_slot[2:])
     sums = butterfly(sums, "fsdp", 2)
-    sums, gated_back = lax.optimization_barrier((sums, gated_back))
-    sums = butterfly(sums, "seq", 4)
     norm = run_kernel(
         lambda *refs: norm_kernel(total_channels, shards, rows, *refs),
         scalars,
         [(a, NEAR) for a in (cotangent, response, taps, gain, query_feature, gated, sums)],
         ((whole, bf16, NEAR),) * 2 + (((rows, width), bf16, FAR),) * shards,
         ((whole, bf16), ((blocks + 1,) + extended_shape, f32)),
-        3,
+        0.2,
         "norm",
         sems=shards,
     )
     d_query, d_response = norm[:2]
+    norm, gated_far, near_piece = lax.optimization_barrier((norm, gated_far, gated_pieces[1]))
+    gated_back = to_tokens([gated_pieces[0], near_piece], [0, 1]) + gated_far
     query_back = to_tokens(norm[2:3] + norm[4:], [slot for slot in every_slot if slot != 1])
     back = run_kernel(
         lambda *refs: mix_back_kernel(shards, rows, *refs),
@@ -724,6 +749,7 @@
         "mix_back",
         sems=shards + 1,
     )
+    gated_back[1], back = lax.optimization_barrier((gated_back[1], back))
     mixer_grad, d_others = back[:2]
     others_back = to_tokens(back[2:], every_slot)
     d_others, query_back = lax.optimization_barrier((d_others, query_back))

time: 108 us -> 110 us (1.019); the launches traced: 106 us -> 110 us
  waiting for transfers between devices: 38.6 us -> 44.9 us
  starting transfers between devices: 37 us -> 35.2 us
    ppermute x23, waiting for transfers between devices: 38.6 us -> 44.9 us  [exchange(): lax.ppermute(array, axis, [(i, i ^ bits) for i in range(lax.axis_size(axi...]
    ppermute x23, starting transfers between devices: 37 us -> 35.2 us  [exchange(): lax.ppermute(array, axis, [(i, i ^ bits) for i in range(lax.axis_size(axi...]
    slice x1 -> x2, local copies, waits for them, and re-layouts: 1.12 us -> 0.01 us  [body(): query_parts = lane_parts(streams[0])]
    pallas_call x8 -> x9, Pallas kernels: 25.1 us -> 25 us  [run_kernel(): pl.pallas_call(kernel, out_shape=[jax.ShapeDtypeStruct(s, d) for s, d, _...]
  transfers between devices with their start and end apart: 23 -> 23, of which waited for: 10 -> 9; matrix products, arithmetic and copies ran while one was open for 3% -> 1% of each run, Pallas kernels for 20% -> 21%
where the time goes in v3:
time: 110 us
  waiting for transfers between devices  44.9 us (41%)
  starting transfers between devices  35.2 us (32%)
  Pallas kernels  25 us (23%)
  local copies, waits for them, and re-layouts  3.06 us (3%)
    ppermute x23, waiting for transfers between devices, exchange(): lax.ppermute(array, axis, [(i, i ^ bits) for i in range(lax.axis_size(axi...  44.9 us
    ppermute x23, starting transfers between devices, exchange(): lax.ppermute(array, axis, [(i, i ^ bits) for i in range(lax.axis_size(axi...  35.2 us
    pallas_call x9, Pallas kernels, run_kernel(): pl.pallas_call(kernel, out_shape=[jax.ShapeDtypeStruct(s, d) for s, d, _...  25 us
  transfers between devices with their start and end apart: 23, of which 9 were waited for; matrix products, arithmetic and copies ran while one was open for 1% of the time, Pallas kernels for 21%

profile of v3, /device:TPU:0, one launch (start us, length us, event | category | flops | bytes accessed | tf_op | source)
XLA Modules:
  0.0 109.7 jit_solution(11540880139010437318)
XLA Ops:
  2.9 5.0 %collective-permute-start.8 = (bf16[2,512,128]{2,1,0:T(8,128)(2,1)}, bf16[2,512,128]{2,1,0:T(8,128)(2,1)S(1)}, u32[]{:S(2)}, u32[]{:S(2)}) collective-permute-start(bf16[2,512,128]{2,1,0:T(8,128)(2,1)} %get-tuple-element.138), channel_id=1, source_target_pairs={{0,3},{1,2},{2,1},{3,0},{4,7},{5,6},{6,5},{7,4},{8,11},{9,10},{10,... | collective-permute-start | bytes 786440 | tf_op jit(solution)/shard_map/ppermute | solution.py:587
  9.2 15.9 %collective-permute-done.refs_3_ = bf16[2,512,128]{2,1,0:T(8,128)(2,1)S(1)} collective-permute-done((bf16[2,512,128]{2,1,0:T(8,128)(2,1)}, bf16[2,512,128]{2,1,0:T(8,128)(2,1)S(1)}, u32[]{:S(2)}, u32[]{:S(2)}) %collective-permute-start) | collective-permute-done | bytes 262176 | tf_op jit(solution)/shard_map/ppermute | solution.py:587
  25.1 2.4 %collective-permute-start.1 = (bf16[512,128]{1,0:T(8,128)(2,1)S(1)}, bf16[512,128]{1,0:T(8,128)(2,1)S(1)}, u32[]{:S(2)}, u32[]{:S(2)}) collective-permute-start(bf16[512,128]{1,0:T(8,128)(2,1)S(1)} %get-tuple-element.63), channel_id=1, source_target_pairs={{0,1},{1,0},{2,3},{3,2},{4,5},{5,4},{6,7},{7,6},{8,9},{9,8},{10,11... | collective-permute-start | bytes 393224 | tf_op jit(solution)/shard_map/ppermute | solution.py:587
  27.7 2.4 %collective-permute-start.6 = (bf16[512,128]{1,0:T(8,128)(2,1)S(1)}, bf16[512,128]{1,0:T(8,128)(2,1)S(1)}, u32[]{:S(2)}, u32[]{:S(2)}) collective-permute-start(bf16[512,128]{1,0:T(8,128)(2,1)S(1)} %get-tuple-element.71), channel_id=1, source_target_pairs={{0,3},{1,2},{2,1},{3,0},{4,7},{5,6},{6,5},{7,4},{8,11},{9,10},{10,... | collective-permute-start | bytes 393224 | tf_op jit(solution)/shard_map/ppermute | solution.py:587
  30.1 4.5 %collective-permute-done.1.refs_3_ = bf16[512,128]{1,0:T(8,128)(2,1)S(1)} collective-permute-done((bf16[512,128]{1,0:T(8,128)(2,1)S(1)}, bf16[512,128]{1,0:T(8,128)(2,1)S(1)}, u32[]{:S(2)}, u32[]{:S(2)}) %collective-permute-start.1) | collective-permute-done | bytes 131104 | tf_op jit(solution)/shard_map/ppermute | solution.py:587
  34.6 3.5 %collective-permute-start.3 = (bf16[512,128]{1,0:T(8,128)(2,1)S(1)}, bf16[512,128]{1,0:T(8,128)(2,1)S(1)}, u32[]{:S(2)}, u32[]{:S(2)}) collective-permute-start(bf16[512,128]{1,0:T(8,128)(2,1)S(1)} %get-tuple-element.66), channel_id=1, source_target_pairs={{0,2},{1,3},{2,0},{3,1},{4,6},{5,7},{6,4},{7,5},{8,10},{9,11},{10,... | collective-permute-start | bytes 393224 | tf_op jit(solution)/shard_map/ppermute | solution.py:587
  38.1 1.6 %collective-permute-start.4 = (bf16[512,128]{1,0:T(8,128)(2,1)S(1)}, bf16[512,128]{1,0:T(8,128)(2,1)S(1)}, u32[]{:S(2)}, u32[]{:S(2)}) collective-permute-start(bf16[512,128]{1,0:T(8,128)(2,1)S(1)} %get-tuple-element.67), channel_id=1, source_target_pairs={{0,3},{1,2},{2,1},{3,0},{4,7},{5,6},{6,5},{7,4},{8,11},{9,10},{10,... | collective-permute-start | bytes 393224 | tf_op jit(solution)/shard_map/ppermute | solution.py:587
  39.8 5.0 %respond.1 = (bf16[2,2048,128]{2,1,0:T(8,128)(2,1)S(1)}, bf16[2,2048,128]{2,1,0:T(8,128)(2,1)S(1)}, f32[2048,128]{1,0:T(8,128)S(1)}, f32[256,128]{1,0:T(8,128)S(1)}) custom-call(s32[128]{0:T(128)S(1)} %fusion.3.refs_0_, s32[3,16]{1,0:T(4,128)S(1)} %pad_add_fusion.refs_1_.refs_0_, bf16[2,512,128]{2,1,0:T(8,128)(2,1)S(1)} %get-tuple-element.140.refs_2_, ...), custom_call_target="tpu_custom_call" | custom-call | flops 6000000000 | tf_op jit(solution)/shard_map/respond/pallas_call | solution.py:572
  44.8 2.9 %gate.1 = (bf16[2048,128]{1,0:T(8,128)(2,1)S(1)}, bf16[2048,128]{1,0:T(8,128)(2,1)S(1)}, bf16[4,528,128]{2,1,0:T(8,128)(2,1)S(1)}, f32[16,128]{1,0:T(8,128)S(1)}) custom-call(s32[128]{0:T(128)S(1)} %fusion.3.refs_0_, s32[3,16]{1,0:T(4,128)S(1)} %pad_add_fusion.refs_1_.refs_0_, bf16[512,128]{1,0:T(8,128)(2,1)S(1)} %get-tuple-element.68.refs_2_, ...), custom_call_target="tpu_custom_call" | custom-call | flops 500000000 | tf_op jit(solution)/shard_map/gate/pallas_call | solution.py:572
  47.7 3.1 %collective-permute-done.3.refs_3_ = bf16[512,128]{1,0:T(8,128)(2,1)S(1)} collective-permute-done((bf16[512,128]{1,0:T(8,128)(2,1)S(1)}, bf16[512,128]{1,0:T(8,128)(2,1)S(1)}, u32[]{:S(2)}, u32[]{:S(2)}) %collective-permute-start.3) | collective-permute-done | bytes 131104 | tf_op jit(solution)/shard_map/ppermute | solution.py:587
  51.9 3.1 %collective-permute-start.11 = (f32[32,128]{1,0:T(8,128)S(1)}, f32[32,128]{1,0:T(8,128)S(1)}, u32[]{:S(2)}, u32[]{:S(2)}) collective-permute-start(f32[32,128]{1,0:T(8,128)S(1)} %get-tuple-element.77), channel_id=1, source_target_pairs={{0,3},{1,2},{2,1},{3,0},{4,7},{5,6},{6,5},{7,4},{8,11},{9,10},{10,... | collective-permute-start | bytes 49160 | tf_op jit(solution)/shard_map/ppermute | solution.py:587
  57.1 2.9 %collective-permute-start.15 = (bf16[528,128]{1,0:T(8,128)(2,1)S(1)}, bf16[528,128]{1,0:T(8,128)(2,1)S(1)}, u32[]{:S(2)}, u32[]{:S(2)}) collective-permute-start(bf16[528,128]{1,0:T(8,128)(2,1)S(1)} %get-tuple-element.88), channel_id=1, source_target_pairs={{0,2},{1,3},{2,0},{3,1},{4,6},{5,7},{6,4},{7,5},{8,10},{9,11},{10,... | collective-permute-start | bytes 405512 | tf_op jit(solution)/shard_map/ppermute | solution.py:587
  64.1 2.2 %collective-permute-done.13 = f32[32,128]{1,0:T(8,128)S(1)} collective-permute-done((f32[32,128]{1,0:T(8,128)S(1)}, f32[32,128]{1,0:T(8,128)S(1)}, u32[]{:S(2)}, u32[]{:S(2)}) %collective-permute-start.13) | collective-permute-done | bytes 16416 | tf_op jit(solution)/shard_map/ppermute | solution.py:587
  67.9 2.2 %collective-permute-done.14 = f32[32,128]{1,0:T(8,128)S(1)} collective-permute-done((f32[32,128]{1,0:T(8,128)S(1)}, f32[32,128]{1,0:T(8,128)S(1)}, u32[]{:S(2)}, u32[]{:S(2)}) %collective-permute-start.14) | collective-permute-done | bytes 16416 | tf_op jit(solution)/shard_map/ppermute | solution.py:587
  70.1 3.0 %norm.1 = (bf16[2048,128]{1,0:T(8,128)(2,1)S(1)}, bf16[2048,128]{1,0:T(8,128)(2,1)S(1)}, bf16[512,128]{1,0:T(8,128)(2,1)S(1)}, bf16[512,128]{1,0:T(8,128)(2,1)S(...) custom-call(s32[128]{0:T(128)S(1)} %fusion.3.refs_0_, s32[3,16]{1,0:T(4,128)S(1)} %pad_add_fusion.refs_1_.refs_0_, ...), custom_call_target="tpu_custom_call" | custom-call | flops 200000000 | tf_op jit(solution)/shard_map/norm/pallas_call | solution.py:572
  74.1 1.7 %collective-permute-start.19 = (bf16[512,128]{1,0:T(8,128)(2,1)S(1)}, bf16[512,128]{1,0:T(8,128)(2,1)S(1)}, u32[]{:S(2)}, u32[]{:S(2)}) collective-permute-start(bf16[512,128]{1,0:T(8,128)(2,1)S(1)} %get-tuple-element.107), channel_id=1, source_target_pairs={{0,3},{1,2},{2,1},{3,0},{4,7},{5,6},{6,5},{7,4},{8,11},{9,10},{10,... | collective-permute-start | bytes 393224 | tf_op jit(solution)/shard_map/ppermute | solution.py:587
  76.7 5.7 %mix_back.1 = (f32[128,128]{1,0:T(8,128)}, bf16[2,2048,128]{2,1,0:T(8,128)(2,1)S(1)}, bf16[2,512,128]{2,1,0:T(8,128)(2,1)S(1)}, bf16[3,512,128]{2,1,0:T(8,128)(2...) custom-call(s32[128]{0:T(128)S(1)} %fusion.3.refs_0_, ...), custom_call_target="tpu_custom_call" | custom-call | flops 7000000000 | tf_op jit(solution)/shard_map/mix_back/pallas_call | solution.py:572
  82.3 2.6 %collective-permute-done.17.refs_4_ = bf16[528,128]{1,0:T(8,128)(2,1)S(1)} collective-permute-done((bf16[528,128]{1,0:T(8,128)(2,1)S(1)}, bf16[528,128]{1,0:T(8,128)(2,1)S(1)}, u32[]{:S(2)}, u32[]{:S(2)}) %collective-permute-start.17) | collective-permute-done | bytes 135200 | tf_op jit(solution)/shard_map/ppermute | solution.py:587
  84.9 1.7 %collective-permute-start.21 = (bf16[2,512,128]{2,1,0:T(8,128)(2,1)S(1)}, bf16[2,512,128]{2,1,0:T(8,128)(2,1)S(1)}, u32[]{:S(2)}, u32[]{:S(2)}) collective-permute-start(bf16[2,512,128]{2,1,0:T(8,128)(2,1)S(1)} %get-tuple-element.113), channel_id=1, source_target_pairs={{0,2},{1,3},{2,0},{3,1},{4,6},{5,7},{6,4},{7,5},{8,10},{9,11},{10,... | collective-permute-start | bytes 786440 | tf_op jit(solution)/shard_map/ppermute | solution.py:587
  86.7 2.5 %collective-permute-start.22 = (bf16[2,512,128]{2,1,0:T(8,128)(2,1)S(1)}, bf16[2,512,128]{2,1,0:T(8,128)(2,1)S(1)}, u32[]{:S(2)}, u32[]{:S(2)}) collective-permute-start(bf16[2,512,128]{2,1,0:T(8,128)(2,1)S(1)} %get-tuple-element.114), channel_id=1, source_target_pairs={{0,3},{1,2},{2,1},{3,0},{4,7},{5,6},{6,5},{7,4},{8,11},{9,10},{10,... | collective-permute-start | bytes 786440 | tf_op jit(solution)/shard_map/ppermute | solution.py:587
  89.2 3.7 %tap_grad.1 = (f32[21,128]{1,0:T(8,128)S(1)}, f32[1,128]{1,0:T(1,128)}) custom-call(s32[128]{0:T(128)S(1)} %fusion.3.refs_0_, s32[3,16]{1,0:T(4,128)S(1)} %pad_add_fusion.refs_1_.refs_0_, bf16[2048,128]{1,0:T(8,128)(2,1)S(1)} %get-tuple-element.116.refs_2_, bf16[2,2048,128]{2,1,0:T(8,128)(2,1)S(1)} %get-tuple-element.117.refs_3_, ...), custom_call_target="tpu_custom_call" | custom-call | flops 4000000000 | tf_op jit(solution)/shard_map/tap_grad/pallas_call | solution.py:572
  93.4 1.9 %scale_out.1 = bf16[512,512]{1,0:T(8,128)(2,1)} custom-call(s32[3,16]{1,0:T(4,128)S(1)} %pad_add_fusion.refs_1_.refs_0_, s32[1]{0:T(128)} %bitcast.5.refs_0_.refs_1_, f32[32,128]{1,0:T(8,128)S(1)} %add.74.refs_8_.refs_2_, bf16[528,128]{1,0:T(8,128)(2,1)S(1)} %get-tuple-element.79.refs_3_, bf16[528,128]{1,0:T(8,128)(2,1)S(1)} %collective-permute-done.17.refs_4_, ...), custom_call_target="tpu_custom_call" | custom-call | flops 2000000000 | tf_op jit(solution)/shard_map/scale_out/pallas_call | solution.py:572
  95.3 11.1 %collective-permute-done.21.refs_6_ = bf16[2,512,128]{2,1,0:T(8,128)(2,1)S(1)} collective-permute-done((bf16[2,512,128]{2,1,0:T(8,128)(2,1)S(1)}, bf16[2,512,128]{2,1,0:T(8,128)(2,1)S(1)}, u32[]{:S(2)}, u32[]{:S(2)}) %collective-permute-start.21) | collective-permute-done | bytes 262176 | tf_op jit(solution)/shard_map/ppermute | solution.py:587
  106.4 2.1 %collective-permute-done.20.refs_5_ = bf16[3,512,128]{2,1,0:T(8,128)(2,1)S(1)} collective-permute-done((bf16[3,512,128]{2,1,0:T(8,128)(2,1)S(1)}, bf16[3,512,128]{2,1,0:T(8,128)(2,1)S(1)}, u32[]{:S(2)}, u32[]{:S(2)}) %collective-permute-start.20) | collective-permute-done | bytes 393248 | tf_op jit(solution)/shard_map/ppermute | solution.py:587
  (77 shorter events, 16.1 us)
Async XLA Ops:
  2.9 31.7 %collective-permute-start.8 = (bf16[2,512,128]{2,1,0:T(8,128)(2,1)}, bf16[2,512,128]{2,1,0:T(8,128)(2,1)S(1)}, u32[]{:S(2)}, u32[]{:S(2)}) collective-permute-start(bf16[2,512,128]{2,1,0:T(8,128)(2,1)} %get-tuple-element.138), channel_id=1, source_target_pairs={{0,3},{1,2},{2,1},{3,0},{4,7},{5,6},{6,5},{7,4},{8,11},{9,10},{10,... | collective-permute-start | bytes 786440 | tf_op jit(solution)/shard_map/ppermute | solution.py:587
  7.9 30.2 %collective-permute-start.7 = (bf16[2,512,128]{2,1,0:T(8,128)(2,1)}, bf16[2,512,128]{2,1,0:T(8,128)(2,1)S(1)}, u32[]{:S(2)}, u32[]{:S(2)}) collective-permute-start(bf16[2,512,128]{2,1,0:T(8,128)(2,1)} %get-tuple-element.139), channel_id=1, source_target_pairs={{0,2},{1,3},{2,0},{3,1},{4,6},{5,7},{6,4},{7,5},{8,10},{9,11},{10,... | collective-permute-start | bytes 786440 | tf_op jit(solution)/shard_map/ppermute | solution.py:587
  7.9 17.2 %collective-permute-start = (bf16[2,512,128]{2,1,0:T(8,128)(2,1)}, bf16[2,512,128]{2,1,0:T(8,128)(2,1)S(1)}, u32[]{:S(2)}, u32[]{:S(2)}) collective-permute-start(bf16[2,512,128]{2,1,0:T(8,128)(2,1)} %get-tuple-element.141), channel_id=1, source_target_pairs={{0,1},{1,0},{2,3},{3,2},{4,5},{5,4},{6,7},{7,6},{8,9},{9,8},{10,11... | collective-permute-start | bytes 786440 | tf_op jit(solution)/shard_map/ppermute | solution.py:587
  8.5 31.2 %copy-start.4 = (bf16[256,256]{1,0:T(8,128)(2,1)S(1)}, bf16[256,256]{1,0:T(8,128)(2,1)}, u32[]{:S(2)}) copy-start(bf16[256,256]{1,0:T(8,128)(2,1)} %constant.65.clone.refs_9_) | copy-start | bytes 393220
  25.1 9.5 %collective-permute-start.1 = (bf16[512,128]{1,0:T(8,128)(2,1)S(1)}, bf16[512,128]{1,0:T(8,128)(2,1)S(1)}, u32[]{:S(2)}, u32[]{:S(2)}) collective-permute-start(bf16[512,128]{1,0:T(8,128)(2,1)S(1)} %get-tuple-element.63), channel_id=1, source_target_pairs={{0,1},{1,0},{2,3},{3,2},{4,5},{5,4},{6,7},{7,6},{8,9},{9,8},{10,11... | collective-permute-start | bytes 393224 | tf_op jit(solution)/shard_map/ppermute | solution.py:587
  27.7 17.1 %collective-permute-start.5 = (bf16[512,128]{1,0:T(8,128)(2,1)S(1)}, bf16[512,128]{1,0:T(8,128)(2,1)S(1)}, u32[]{:S(2)}, u32[]{:S(2)}) collective-permute-start(bf16[512,128]{1,0:T(8,128)(2,1)S(1)} %get-tuple-element.70), channel_id=1, source_target_pairs={{0,2},{1,3},{2,0},{3,1},{4,6},{5,7},{6,4},{7,5},{8,10},{9,11},{10,... | collective-permute-start | bytes 393224 | tf_op jit(solution)/shard_map/ppermute | solution.py:587
  27.7 17.0 %collective-permute-start.6 = (bf16[512,128]{1,0:T(8,128)(2,1)S(1)}, bf16[512,128]{1,0:T(8,128)(2,1)S(1)}, u32[]{:S(2)}, u32[]{:S(2)}) collective-permute-start(bf16[512,128]{1,0:T(8,128)(2,1)S(1)} %get-tuple-element.71), channel_id=1, source_target_pairs={{0,3},{1,2},{2,1},{3,0},{4,7},{5,6},{6,5},{7,4},{8,11},{9,10},{10,... | collective-permute-start | bytes 393224 | tf_op jit(solution)/shard_map/ppermute | solution.py:587
  34.6 13.1 %collective-permute-start.2 = (bf16[512,128]{1,0:T(8,128)(2,1)S(1)}, bf16[512,128]{1,0:T(8,128)(2,1)S(1)}, u32[]{:S(2)}, u32[]{:S(2)}) collective-permute-start(bf16[512,128]{1,0:T(8,128)(2,1)S(1)} %get-tuple-element.65), channel_id=1, source_target_pairs={{0,1},{1,0},{2,3},{3,2},{4,5},{5,4},{6,7},{7,6},{8,9},{9,8},{10,11... | collective-permute-start | bytes 393224 | tf_op jit(solution)/shard_map/ppermute | solution.py:587
  34.6 16.2 %collective-permute-start.3 = (bf16[512,128]{1,0:T(8,128)(2,1)S(1)}, bf16[512,128]{1,0:T(8,128)(2,1)S(1)}, u32[]{:S(2)}, u32[]{:S(2)}) collective-permute-start(bf16[512,128]{1,0:T(8,128)(2,1)S(1)} %get-tuple-element.66), channel_id=1, source_target_pairs={{0,2},{1,3},{2,0},{3,1},{4,6},{5,7},{6,4},{7,5},{8,10},{9,11},{10,... | collective-permute-start | bytes 393224 | tf_op jit(solution)/shard_map/ppermute | solution.py:587
  38.1 12.6 %collective-permute-start.4 = (bf16[512,128]{1,0:T(8,128)(2,1)S(1)}, bf16[512,128]{1,0:T(8,128)(2,1)S(1)}, u32[]{:S(2)}, u32[]{:S(2)}) collective-permute-start(bf16[512,128]{1,0:T(8,128)(2,1)S(1)} %get-tuple-element.67), channel_id=1, source_target_pairs={{0,3},{1,2},{2,1},{3,0},{4,7},{5,6},{6,5},{7,4},{8,11},{9,10},{10,... | collective-permute-start | bytes 393224 | tf_op jit(solution)/shard_map/ppermute | solution.py:587
  51.9 9.4 %collective-permute-start.11 = (f32[32,128]{1,0:T(8,128)S(1)}, f32[32,128]{1,0:T(8,128)S(1)}, u32[]{:S(2)}, u32[]{:S(2)}) collective-permute-start(f32[32,128]{1,0:T(8,128)S(1)} %get-tuple-element.77), channel_id=1, source_target_pairs={{0,3},{1,2},{2,1},{3,0},{4,7},{5,6},{6,5},{7,4},{8,11},{9,10},{10,... | collective-permute-start | bytes 49160 | tf_op jit(solution)/shard_map/ppermute | solution.py:587
  55.0 6.3 %collective-permute-start.10 = (f32[32,128]{1,0:T(8,128)S(1)}, f32[32,128]{1,0:T(8,128)S(1)}, u32[]{:S(2)}, u32[]{:S(2)}) collective-permute-start(f32[32,128]{1,0:T(8,128)S(1)} %get-tuple-element.77), channel_id=1, source_target_pairs={{0,2},{1,3},{2,0},{3,1},{4,6},{5,7},{6,4},{7,5},{8,10},{9,11},{10,... | collective-permute-start | bytes 49160 | tf_op jit(solution)/shard_map/ppermute | solution.py:587
  56.1 5.2 %collective-permute-start.9 = (f32[32,128]{1,0:T(8,128)S(1)}, f32[32,128]{1,0:T(8,128)S(1)}, u32[]{:S(2)}, u32[]{:S(2)}) collective-permute-start(f32[32,128]{1,0:T(8,128)S(1)} %get-tuple-element.77), channel_id=1, source_target_pairs={{0,1},{1,0},{2,3},{3,2},{4,5},{5,4},{6,7},{7,6},{8,9},{9,8},{10,11... | collective-permute-start | bytes 49160 | tf_op jit(solution)/shard_map/ppermute | solution.py:587
  57.1 16.0 %collective-permute-start.15 = (bf16[528,128]{1,0:T(8,128)(2,1)S(1)}, bf16[528,128]{1,0:T(8,128)(2,1)S(1)}, u32[]{:S(2)}, u32[]{:S(2)}) collective-permute-start(bf16[528,128]{1,0:T(8,128)(2,1)S(1)} %get-tuple-element.88), channel_id=1, source_target_pairs={{0,2},{1,3},{2,0},{3,1},{4,6},{5,7},{6,4},{7,5},{8,10},{9,11},{10,... | collective-permute-start | bytes 405512 | tf_op jit(solution)/shard_map/ppermute | solution.py:587
  60.0 13.1 %collective-permute-start.16 = (bf16[528,128]{1,0:T(8,128)(2,1)S(1)}, bf16[528,128]{1,0:T(8,128)(2,1)S(1)}, u32[]{:S(2)}, u32[]{:S(2)}) collective-permute-start(bf16[528,128]{1,0:T(8,128)(2,1)S(1)} %get-tuple-element.89), channel_id=1, source_target_pairs={{0,3},{1,2},{2,1},{3,0},{4,7},{5,6},{6,5},{7,4},{8,11},{9,10},{10,... | collective-permute-start | bytes 405512 | tf_op jit(solution)/shard_map/ppermute | solution.py:587
  61.3 1.2 %collective-permute-start.12 = (f32[32,128]{1,0:T(8,128)S(1)}, f32[32,128]{1,0:T(8,128)S(1)}, u32[]{:S(2)}, u32[]{:S(2)}) collective-permute-start(f32[32,128]{1,0:T(8,128)S(1)} %add_add_fusion), channel_id=1, source_target_pairs={{0,4},{4,0},{8,12},{12,8},{16,20},{20,16},{24,28},{28,24},{1,5},{5... | collective-permute-start | bytes 49160 | tf_op jit(solution)/shard_map/ppermute | solution.py:587
  62.6 3.7 %collective-permute-start.13 = (f32[32,128]{1,0:T(8,128)S(1)}, f32[32,128]{1,0:T(8,128)S(1)}, u32[]{:S(2)}, u32[]{:S(2)}) collective-permute-start(f32[32,128]{1,0:T(8,128)S(1)} %add.72), channel_id=1, source_target_pairs={{0,8},{4,12},{8,0},{12,4},{16,24},{20,28},{24,16},{28,20},{1,9},{5... | collective-permute-start | bytes 49160 | tf_op jit(solution)/shard_map/ppermute | solution.py:587
  66.3 3.7 %collective-permute-start.14 = (f32[32,128]{1,0:T(8,128)S(1)}, f32[32,128]{1,0:T(8,128)S(1)}, u32[]{:S(2)}, u32[]{:S(2)}) collective-permute-start(f32[32,128]{1,0:T(8,128)S(1)} %add.73), channel_id=1, source_target_pairs={{0,16},{4,20},{8,24},{12,28},{16,0},{20,4},{24,8},{28,12},{1,17},{... | collective-permute-start | bytes 49160 | tf_op jit(solution)/shard_map/ppermute | solution.py:587
  73.1 11.8 %collective-permute-start.18 = (bf16[512,128]{1,0:T(8,128)(2,1)S(1)}, bf16[512,128]{1,0:T(8,128)(2,1)S(1)}, u32[]{:S(2)}, u32[]{:S(2)}) collective-permute-start(bf16[512,128]{1,0:T(8,128)(2,1)S(1)} %get-tuple-element.106), channel_id=1, source_target_pairs={{0,2},{1,3},{2,0},{3,1},{4,6},{5,7},{6,4},{7,5},{8,10},{9,11},{10,... | collective-permute-start | bytes 393224 | tf_op jit(solution)/shard_map/ppermute | solution.py:587
  74.1 10.9 %collective-permute-start.19 = (bf16[512,128]{1,0:T(8,128)(2,1)S(1)}, bf16[512,128]{1,0:T(8,128)(2,1)S(1)}, u32[]{:S(2)}, u32[]{:S(2)}) collective-permute-start(bf16[512,128]{1,0:T(8,128)(2,1)S(1)} %get-tuple-element.107), channel_id=1, source_target_pairs={{0,3},{1,2},{2,1},{3,0},{4,7},{5,6},{6,5},{7,4},{8,11},{9,10},{10,... | collective-permute-start | bytes 393224 | tf_op jit(solution)/shard_map/ppermute | solution.py:587
  75.8 9.1 %collective-permute-start.17 = (bf16[528,128]{1,0:T(8,128)(2,1)S(1)}, bf16[528,128]{1,0:T(8,128)(2,1)S(1)}, u32[]{:S(2)}, u32[]{:S(2)}) collective-permute-start(bf16[528,128]{1,0:T(8,128)(2,1)S(1)} %get-tuple-element.91), channel_id=1, source_target_pairs={{0,1},{1,0},{2,3},{3,2},{4,5},{5,4},{6,7},{7,6},{8,9},{9,8},{10,11... | collective-permute-start | bytes 405512 | tf_op jit(solution)/shard_map/ppermute | solution.py:587
  84.9 21.4 %collective-permute-start.21 = (bf16[2,512,128]{2,1,0:T(8,128)(2,1)S(1)}, bf16[2,512,128]{2,1,0:T(8,128)(2,1)S(1)}, u32[]{:S(2)}, u32[]{:S(2)}) collective-permute-start(bf16[2,512,128]{2,1,0:T(8,128)(2,1)S(1)} %get-tuple-element.113), channel_id=1, source_target_pairs={{0,2},{1,3},{2,0},{3,1},{4,6},{5,7},{6,4},{7,5},{8,10},{9,11},{10,... | collective-permute-start | bytes 786440 | tf_op jit(solution)/shard_map/ppermute | solution.py:587
  86.7 19.7 %collective-permute-start.22 = (bf16[2,512,128]{2,1,0:T(8,128)(2,1)S(1)}, bf16[2,512,128]{2,1,0:T(8,128)(2,1)S(1)}, u32[]{:S(2)}, u32[]{:S(2)}) collective-permute-start(bf16[2,512,128]{2,1,0:T(8,128)(2,1)S(1)} %get-tuple-element.114), channel_id=1, source_target_pairs={{0,3},{1,2},{2,1},{3,0},{4,7},{5,6},{6,5},{7,4},{8,11},{9,10},{10,... | collective-permute-start | bytes 786440 | tf_op jit(solution)/shard_map/ppermute | solution.py:587
  89.2 19.3 %collective-permute-start.20 = (bf16[3,512,128]{2,1,0:T(8,128)(2,1)S(1)}, bf16[3,512,128]{2,1,0:T(8,128)(2,1)S(1)}, u32[]{:S(2)}, u32[]{:S(2)}) collective-permute-start(bf16[3,512,128]{2,1,0:T(8,128)(2,1)S(1)} %get-tuple-element.112), channel_id=1, source_target_pairs={{0,1},{1,0},{2,3},{3,2},{4,5},{5,4},{6,7},{7,6},{8,9},{9,8},{10,11... | collective-permute-start | bytes 1179656 | tf_op jit(solution)/shard_map/ppermute | solution.py:587
  (11 other events, 165.4 us)

commit v4 on v3

--- a/solution.py
+++ b/solution.py
@@ -749,10 +749,9 @@
         "mix_back",
         sems=shards + 1,
     )
-    gated_back[1], back = lax.optimization_barrier((gated_back[1], back))
-    mixer_grad, d_others = back[:2]
-    others_back = to_tokens(back[2:], every_slot)
-    d_others, query_back = lax.optimization_barrier((d_others, query_back))
+    mixer_grad, d_others, *back_pieces = back
+    gated_back[1], back_pieces[1] = lax.optimization_barrier((gated_back[1], back_pieces[1]))
+    others_back = to_tokens(back_pieces, every_slot)
     taps_grad, gain_grad = run_kernel(
         lambda *refs: tap_grad_kernel(total_channels, *refs),
         scalars,

time: 110 us -> 108 us (0.982)
  waiting for transfers between devices: 44.9 us -> 43.3 us
    ppermute x23, waiting for transfers between devices: 44.9 us -> 43.3 us  [exchange(): lax.ppermute(array, axis, [(i, i ^ bits) for i in range(lax.axis_size(axi...]
  transfers between devices with their start and end apart: 23 -> 23, of which waited for: 9 -> 8; matrix products, arithmetic and copies ran while one was open for 1% -> 1% of each run, Pallas kernels for 21% -> 21%
where the time goes in v4:
time: 108 us; the launch traced here: 107 us
  waiting for transfers between devices  43.3 us (40%)
  starting transfers between devices  34.5 us (32%)
  Pallas kernels  25 us (23%)
  local copies, waits for them, and re-layouts  3.06 us (3%)
    ppermute x23, waiting for transfers between devices, exchange(): lax.ppermute(array, axis, [(i, i ^ bits) for i in range(lax.axis_size(axi...  43.3 us
    ppermute x23, starting transfers between devices, exchange(): lax.ppermute(array, axis, [(i, i ^ bits) for i in range(lax.axis_size(axi...  34.5 us
    pallas_call x9, Pallas kernels, run_kernel(): pl.pallas_call(kernel, out_shape=[jax.ShapeDtypeStruct(s, d) for s, d, _...  25 us
  transfers between devices with their start and end apart: 23, of which 8 were waited for; matrix products, arithmetic and copies ran while one was open for 1% of the time, Pallas kernels for 21%

profile of v4, /device:TPU:0, one launch (start us, length us, event | category | flops | bytes accessed | tf_op | source)
XLA Modules:
  0.0 107.4 jit_solution(17336840422168186601)
XLA Ops:
  2.9 5.0 %collective-permute-start.8 = (bf16[2,512,128]{2,1,0:T(8,128)(2,1)}, bf16[2,512,128]{2,1,0:T(8,128)(2,1)S(1)}, u32[]{:S(2)}, u32[]{:S(2)}) collective-permute-start(bf16[2,512,128]{2,1,0:T(8,128)(2,1)} %get-tuple-element.120), channel_id=1, source_target_pairs={{0,3},{1,2},{2,1},{3,0},{4,7},{5,6},{6,5},{7,4},{8,11},{9,10},{10,... | collective-permute-start | bytes 786440 | tf_op jit(solution)/shard_map/ppermute | solution.py:587
  9.2 15.9 %collective-permute-done.refs_3_ = bf16[2,512,128]{2,1,0:T(8,128)(2,1)S(1)} collective-permute-done((bf16[2,512,128]{2,1,0:T(8,128)(2,1)}, bf16[2,512,128]{2,1,0:T(8,128)(2,1)S(1)}, u32[]{:S(2)}, u32[]{:S(2)}) %collective-permute-start) | collective-permute-done | bytes 262176 | tf_op jit(solution)/shard_map/ppermute | solution.py:587
  25.1 2.4 %collective-permute-start.1 = (bf16[512,128]{1,0:T(8,128)(2,1)S(1)}, bf16[512,128]{1,0:T(8,128)(2,1)S(1)}, u32[]{:S(2)}, u32[]{:S(2)}) collective-permute-start(bf16[512,128]{1,0:T(8,128)(2,1)S(1)} %get-tuple-element.54), channel_id=1, source_target_pairs={{0,1},{1,0},{2,3},{3,2},{4,5},{5,4},{6,7},{7,6},{8,9},{9,8},{10,11... | collective-permute-start | bytes 393224 | tf_op jit(solution)/shard_map/ppermute | solution.py:587
  27.7 2.4 %collective-permute-start.6 = (bf16[512,128]{1,0:T(8,128)(2,1)S(1)}, bf16[512,128]{1,0:T(8,128)(2,1)S(1)}, u32[]{:S(2)}, u32[]{:S(2)}) collective-permute-start(bf16[512,128]{1,0:T(8,128)(2,1)S(1)} %get-tuple-element.62), channel_id=1, source_target_pairs={{0,3},{1,2},{2,1},{3,0},{4,7},{5,6},{6,5},{7,4},{8,11},{9,10},{10,... | collective-permute-start | bytes 393224 | tf_op jit(solution)/shard_map/ppermute | solution.py:587
  30.1 4.5 %collective-permute-done.1.refs_3_ = bf16[512,128]{1,0:T(8,128)(2,1)S(1)} collective-permute-done((bf16[512,128]{1,0:T(8,128)(2,1)S(1)}, bf16[512,128]{1,0:T(8,128)(2,1)S(1)}, u32[]{:S(2)}, u32[]{:S(2)}) %collective-permute-start.1) | collective-permute-done | bytes 131104 | tf_op jit(solution)/shard_map/ppermute | solution.py:587
  34.6 3.5 %collective-permute-start.3 = (bf16[512,128]{1,0:T(8,128)(2,1)S(1)}, bf16[512,128]{1,0:T(8,128)(2,1)S(1)}, u32[]{:S(2)}, u32[]{:S(2)}) collective-permute-start(bf16[512,128]{1,0:T(8,128)(2,1)S(1)} %get-tuple-element.57), channel_id=1, source_target_pairs={{0,2},{1,3},{2,0},{3,1},{4,6},{5,7},{6,4},{7,5},{8,10},{9,11},{10,... | collective-permute-start | bytes 393224 | tf_op jit(solution)/shard_map/ppermute | solution.py:587
  38.1 1.6 %collective-permute-start.4 = (bf16[512,128]{1,0:T(8,128)(2,1)S(1)}, bf16[512,128]{1,0:T(8,128)(2,1)S(1)}, u32[]{:S(2)}, u32[]{:S(2)}) collective-permute-start(bf16[512,128]{1,0:T(8,128)(2,1)S(1)} %get-tuple-element.58), channel_id=1, source_target_pairs={{0,3},{1,2},{2,1},{3,0},{4,7},{5,6},{6,5},{7,4},{8,11},{9,10},{10,... | collective-permute-start | bytes 393224 | tf_op jit(solution)/shard_map/ppermute | solution.py:587
  39.8 5.0 %respond.1 = (bf16[2,2048,128]{2,1,0:T(8,128)(2,1)S(1)}, bf16[2,2048,128]{2,1,0:T(8,128)(2,1)S(1)}, f32[2048,128]{1,0:T(8,128)S(1)}, f32[256,128]{1,0:T(8,128)S(1)}) custom-call(s32[128]{0:T(128)S(1)} %fusion.3.refs_0_, s32[3,16]{1,0:T(4,128)S(1)} %pad_add_fusion.refs_1_.refs_0_, bf16[2,512,128]{2,1,0:T(8,128)(2,1)S(1)} %get-tuple-element.122.refs_2_, ...), custom_call_target="tpu_custom_call" | custom-call | flops 6000000000 | tf_op jit(solution)/shard_map/respond/pallas_call | solution.py:572
  44.8 2.9 %gate.1 = (bf16[2048,128]{1,0:T(8,128)(2,1)S(1)}, bf16[2048,128]{1,0:T(8,128)(2,1)S(1)}, bf16[4,528,128]{2,1,0:T(8,128)(2,1)S(1)}, f32[16,128]{1,0:T(8,128)S(1)}) custom-call(s32[128]{0:T(128)S(1)} %fusion.3.refs_0_, s32[3,16]{1,0:T(4,128)S(1)} %pad_add_fusion.refs_1_.refs_0_, bf16[512,128]{1,0:T(8,128)(2,1)S(1)} %get-tuple-element.59.refs_2_, ...), custom_call_target="tpu_custom_call" | custom-call | flops 500000000 | tf_op jit(solution)/shard_map/gate/pallas_call | solution.py:572
  47.7 3.1 %collective-permute-done.3.refs_3_ = bf16[512,128]{1,0:T(8,128)(2,1)S(1)} collective-permute-done((bf16[512,128]{1,0:T(8,128)(2,1)S(1)}, bf16[512,128]{1,0:T(8,128)(2,1)S(1)}, u32[]{:S(2)}, u32[]{:S(2)}) %collective-permute-start.3) | collective-permute-done | bytes 131104 | tf_op jit(solution)/shard_map/ppermute | solution.py:587
  51.9 3.1 %collective-permute-start.11 = (f32[32,128]{1,0:T(8,128)S(1)}, f32[32,128]{1,0:T(8,128)S(1)}, u32[]{:S(2)}, u32[]{:S(2)}) collective-permute-start(f32[32,128]{1,0:T(8,128)S(1)} %get-tuple-element.68), channel_id=1, source_target_pairs={{0,3},{1,2},{2,1},{3,0},{4,7},{5,6},{6,5},{7,4},{8,11},{9,10},{10,... | collective-permute-start | bytes 49160 | tf_op jit(solution)/shard_map/ppermute | solution.py:587
  57.1 2.9 %collective-permute-start.15 = (bf16[528,128]{1,0:T(8,128)(2,1)S(1)}, bf16[528,128]{1,0:T(8,128)(2,1)S(1)}, u32[]{:S(2)}, u32[]{:S(2)}) collective-permute-start(bf16[528,128]{1,0:T(8,128)(2,1)S(1)} %get-tuple-element.79), channel_id=1, source_target_pairs={{0,2},{1,3},{2,0},{3,1},{4,6},{5,7},{6,4},{7,5},{8,10},{9,11},{10,... | collective-permute-start | bytes 405512 | tf_op jit(solution)/shard_map/ppermute | solution.py:587
  64.1 2.2 %collective-permute-done.13 = f32[32,128]{1,0:T(8,128)S(1)} collective-permute-done((f32[32,128]{1,0:T(8,128)S(1)}, f32[32,128]{1,0:T(8,128)S(1)}, u32[]{:S(2)}, u32[]{:S(2)}) %collective-permute-start.13) | collective-permute-done | bytes 16416 | tf_op jit(solution)/shard_map/ppermute | solution.py:587
  66.3 1.5 %collective-permute-start.14 = (f32[32,128]{1,0:T(8,128)S(1)}, f32[32,128]{1,0:T(8,128)S(1)}, u32[]{:S(2)}, u32[]{:S(2)}) collective-permute-start(f32[32,128]{1,0:T(8,128)S(1)} %add.73), channel_id=1, source_target_pairs={{0,16},{4,20},{8,24},{12,28},{16,0},{20,4},{24,8},{28,12},{1,17},{... | collective-permute-start | bytes 49160 | tf_op jit(solution)/shard_map/ppermute | solution.py:587
  67.9 2.2 %collective-permute-done.14 = f32[32,128]{1,0:T(8,128)S(1)} collective-permute-done((f32[32,128]{1,0:T(8,128)S(1)}, f32[32,128]{1,0:T(8,128)S(1)}, u32[]{:S(2)}, u32[]{:S(2)}) %collective-permute-start.14) | collective-permute-done | bytes 16416 | tf_op jit(solution)/shard_map/ppermute | solution.py:587
  70.1 3.0 %norm.1 = (bf16[2048,128]{1,0:T(8,128)(2,1)S(1)}, bf16[2048,128]{1,0:T(8,128)(2,1)S(1)}, bf16[512,128]{1,0:T(8,128)(2,1)S(1)}, bf16[512,128]{1,0:T(8,128)(2,1)S(...) custom-call(s32[128]{0:T(128)S(1)} %fusion.3.refs_0_, s32[3,16]{1,0:T(4,128)S(1)} %pad_add_fusion.refs_1_.refs_0_, ...), custom_call_target="tpu_custom_call" | custom-call | flops 200000000 | tf_op jit(solution)/shard_map/norm/pallas_call | solution.py:572
  74.1 1.7 %collective-permute-start.19 = (bf16[512,128]{1,0:T(8,128)(2,1)S(1)}, bf16[512,128]{1,0:T(8,128)(2,1)S(1)}, u32[]{:S(2)}, u32[]{:S(2)}) collective-permute-start(bf16[512,128]{1,0:T(8,128)(2,1)S(1)} %get-tuple-element.92), channel_id=1, source_target_pairs={{0,3},{1,2},{2,1},{3,0},{4,7},{5,6},{6,5},{7,4},{8,11},{9,10},{10,... | collective-permute-start | bytes 393224 | tf_op jit(solution)/shard_map/ppermute | solution.py:587
  76.7 5.7 %mix_back.1 = (f32[128,128]{1,0:T(8,128)}, bf16[2,2048,128]{2,1,0:T(8,128)(2,1)S(1)}, bf16[2,512,128]{2,1,0:T(8,128)(2,1)S(1)}, bf16[3,512,128]{2,1,0:T(8,128)(2...) custom-call(s32[128]{0:T(128)S(1)} %fusion.3.refs_0_, ...), custom_call_target="tpu_custom_call" | custom-call | flops 7000000000 | tf_op jit(solution)/shard_map/mix_back/pallas_call | solution.py:572
  82.4 1.8 %collective-permute-start.21 = (bf16[2,512,128]{2,1,0:T(8,128)(2,1)S(1)}, bf16[2,512,128]{2,1,0:T(8,128)(2,1)S(1)}, u32[]{:S(2)}, u32[]{:S(2)}) collective-permute-start(bf16[2,512,128]{2,1,0:T(8,128)(2,1)S(1)} %get-tuple-element.95), channel_id=1, source_target_pairs={{0,2},{1,3},{2,0},{3,1},{4,6},{5,7},{6,4},{7,5},{8,10},{9,11},{10,... | collective-permute-start | bytes 786440 | tf_op jit(solution)/shard_map/ppermute | solution.py:587
  84.2 1.7 %collective-permute-start.22 = (bf16[2,512,128]{2,1,0:T(8,128)(2,1)S(1)}, bf16[2,512,128]{2,1,0:T(8,128)(2,1)S(1)}, u32[]{:S(2)}, u32[]{:S(2)}) collective-permute-start(bf16[2,512,128]{2,1,0:T(8,128)(2,1)S(1)} %get-tuple-element.96), channel_id=1, source_target_pairs={{0,3},{1,2},{2,1},{3,0},{4,7},{5,6},{6,5},{7,4},{8,11},{9,10},{10,... | collective-permute-start | bytes 786440 | tf_op jit(solution)/shard_map/ppermute | solution.py:587
  85.9 3.7 %tap_grad.1 = (f32[21,128]{1,0:T(8,128)S(1)}, f32[1,128]{1,0:T(1,128)}) custom-call(s32[128]{0:T(128)S(1)} %fusion.3.refs_0_, s32[3,16]{1,0:T(4,128)S(1)} %pad_add_fusion.refs_1_.refs_0_, bf16[2048,128]{1,0:T(8,128)(2,1)S(1)} %get-tuple-element.98.refs_2_, bf16[2,2048,128]{2,1,0:T(8,128)(2,1)S(1)} %get-tuple-element.99.refs_3_, ...), custom_call_target="tpu_custom_call" | custom-call | flops 4000000000 | tf_op jit(solution)/shard_map/tap_grad/pallas_call | solution.py:572
  90.2 1.9 %scale_out.1 = bf16[512,512]{1,0:T(8,128)(2,1)} custom-call(s32[3,16]{1,0:T(4,128)S(1)} %pad_add_fusion.refs_1_.refs_0_, s32[1]{0:T(128)} %bitcast.5.refs_0_.refs_1_, f32[32,128]{1,0:T(8,128)S(1)} %add.74.refs_8_.refs_2_, bf16[528,128]{1,0:T(8,128)(2,1)S(1)} %get-tuple-element.70.refs_3_, bf16[528,128]{1,0:T(8,128)(2,1)S(1)} %collective-permute-done.17.refs_4_, ...), custom_call_target="tpu_custom_call" | custom-call | flops 2000000000 | tf_op jit(solution)/shard_map/scale_out/pallas_call | solution.py:572
  92.1 11.1 %collective-permute-done.21.refs_6_ = bf16[2,512,128]{2,1,0:T(8,128)(2,1)S(1)} collective-permute-done((bf16[2,512,128]{2,1,0:T(8,128)(2,1)S(1)}, bf16[2,512,128]{2,1,0:T(8,128)(2,1)S(1)}, u32[]{:S(2)}, u32[]{:S(2)}) %collective-permute-start.21) | collective-permute-done | bytes 262176 | tf_op jit(solution)/shard_map/ppermute | solution.py:587
  103.2 3.0 %collective-permute-done.20.refs_5_ = bf16[3,512,128]{2,1,0:T(8,128)(2,1)S(1)} collective-permute-done((bf16[3,512,128]{2,1,0:T(8,128)(2,1)S(1)}, bf16[3,512,128]{2,1,0:T(8,128)(2,1)S(1)}, u32[]{:S(2)}, u32[]{:S(2)}) %collective-permute-start.20) | collective-permute-done | bytes 393248 | tf_op jit(solution)/shard_map/ppermute | solution.py:587
  (77 shorter events, 14.6 us)
Async XLA Ops:
  2.9 31.7 %collective-permute-start.8 = (bf16[2,512,128]{2,1,0:T(8,128)(2,1)}, bf16[2,512,128]{2,1,0:T(8,128)(2,1)S(1)}, u32[]{:S(2)}, u32[]{:S(2)}) collective-permute-start(bf16[2,512,128]{2,1,0:T(8,128)(2,1)} %get-tuple-element.120), channel_id=1, source_target_pairs={{0,3},{1,2},{2,1},{3,0},{4,7},{5,6},{6,5},{7,4},{8,11},{9,10},{10,... | collective-permute-start | bytes 786440 | tf_op jit(solution)/shard_map/ppermute | solution.py:587
  7.9 30.2 %collective-permute-start.7 = (bf16[2,512,128]{2,1,0:T(8,128)(2,1)}, bf16[2,512,128]{2,1,0:T(8,128)(2,1)S(1)}, u32[]{:S(2)}, u32[]{:S(2)}) collective-permute-start(bf16[2,512,128]{2,1,0:T(8,128)(2,1)} %get-tuple-element.121), channel_id=1, source_target_pairs={{0,2},{1,3},{2,0},{3,1},{4,6},{5,7},{6,4},{7,5},{8,10},{9,11},{10,... | collective-permute-start | bytes 786440 | tf_op jit(solution)/shard_map/ppermute | solution.py:587
  7.9 17.2 %collective-permute-start = (bf16[2,512,128]{2,1,0:T(8,128)(2,1)}, bf16[2,512,128]{2,1,0:T(8,128)(2,1)S(1)}, u32[]{:S(2)}, u32[]{:S(2)}) collective-permute-start(bf16[2,512,128]{2,1,0:T(8,128)(2,1)} %get-tuple-element.123), channel_id=1, source_target_pairs={{0,1},{1,0},{2,3},{3,2},{4,5},{5,4},{6,7},{7,6},{8,9},{9,8},{10,11... | collective-permute-start | bytes 786440 | tf_op jit(solution)/shard_map/ppermute | solution.py:587
  8.5 31.2 %copy-start.4 = (bf16[256,256]{1,0:T(8,128)(2,1)S(1)}, bf16[256,256]{1,0:T(8,128)(2,1)}, u32[]{:S(2)}) copy-start(bf16[256,256]{1,0:T(8,128)(2,1)} %constant.65.clone.refs_9_) | copy-start | bytes 393220
  25.1 9.5 %collective-permute-start.1 = (bf16[512,128]{1,0:T(8,128)(2,1)S(1)}, bf16[512,128]{1,0:T(8,128)(2,1)S(1)}, u32[]{:S(2)}, u32[]{:S(2)}) collective-permute-start(bf16[512,128]{1,0:T(8,128)(2,1)S(1)} %get-tuple-element.54), channel_id=1, source_target_pairs={{0,1},{1,0},{2,3},{3,2},{4,5},{5,4},{6,7},{7,6},{8,9},{9,8},{10,11... | collective-permute-start | bytes 393224 | tf_op jit(solution)/shard_map/ppermute | solution.py:587
  27.7 17.1 %collective-permute-start.5 = (bf16[512,128]{1,0:T(8,128)(2,1)S(1)}, bf16[512,128]{1,0:T(8,128)(2,1)S(1)}, u32[]{:S(2)}, u32[]{:S(2)}) collective-permute-start(bf16[512,128]{1,0:T(8,128)(2,1)S(1)} %get-tuple-element.61), channel_id=1, source_target_pairs={{0,2},{1,3},{2,0},{3,1},{4,6},{5,7},{6,4},{7,5},{8,10},{9,11},{10,... | collective-permute-start | bytes 393224 | tf_op jit(solution)/shard_map/ppermute | solution.py:587
  27.7 17.0 %collective-permute-start.6 = (bf16[512,128]{1,0:T(8,128)(2,1)S(1)}, bf16[512,128]{1,0:T(8,128)(2,1)S(1)}, u32[]{:S(2)}, u32[]{:S(2)}) collective-permute-start(bf16[512,128]{1,0:T(8,128)(2,1)S(1)} %get-tuple-element.62), channel_id=1, source_target_pairs={{0,3},{1,2},{2,1},{3,0},{4,7},{5,6},{6,5},{7,4},{8,11},{9,10},{10,... | collective-permute-start | bytes 393224 | tf_op jit(solution)/shard_map/ppermute | solution.py:587
  34.6 13.1 %collective-permute-start.2 = (bf16[512,128]{1,0:T(8,128)(2,1)S(1)}, bf16[512,128]{1,0:T(8,128)(2,1)S(1)}, u32[]{:S(2)}, u32[]{:S(2)}) collective-permute-start(bf16[512,128]{1,0:T(8,128)(2,1)S(1)} %get-tuple-element.56), channel_id=1, source_target_pairs={{0,1},{1,0},{2,3},{3,2},{4,5},{5,4},{6,7},{7,6},{8,9},{9,8},{10,11... | collective-permute-start | bytes 393224 | tf_op jit(solution)/shard_map/ppermute | solution.py:587
  34.6 16.2 %collective-permute-start.3 = (bf16[512,128]{1,0:T(8,128)(2,1)S(1)}, bf16[512,128]{1,0:T(8,128)(2,1)S(1)}, u32[]{:S(2)}, u32[]{:S(2)}) collective-permute-start(bf16[512,128]{1,0:T(8,128)(2,1)S(1)} %get-tuple-element.57), channel_id=1, source_target_pairs={{0,2},{1,3},{2,0},{3,1},{4,6},{5,7},{6,4},{7,5},{8,10},{9,11},{10,... | collective-permute-start | bytes 393224 | tf_op jit(solution)/shard_map/ppermute | solution.py:587
  38.1 12.6 %collective-permute-start.4 = (bf16[512,128]{1,0:T(8,128)(2,1)S(1)}, bf16[512,128]{1,0:T(8,128)(2,1)S(1)}, u32[]{:S(2)}, u32[]{:S(2)}) collective-permute-start(bf16[512,128]{1,0:T(8,128)(2,1)S(1)} %get-tuple-element.58), channel_id=1, source_target_pairs={{0,3},{1,2},{2,1},{3,0},{4,7},{5,6},{6,5},{7,4},{8,11},{9,10},{10,... | collective-permute-start | bytes 393224 | tf_op jit(solution)/shard_map/ppermute | solution.py:587
  51.9 9.4 %collective-permute-start.11 = (f32[32,128]{1,0:T(8,128)S(1)}, f32[32,128]{1,0:T(8,128)S(1)}, u32[]{:S(2)}, u32[]{:S(2)}) collective-permute-start(f32[32,128]{1,0:T(8,128)S(1)} %get-tuple-element.68), channel_id=1, source_target_pairs={{0,3},{1,2},{2,1},{3,0},{4,7},{5,6},{6,5},{7,4},{8,11},{9,10},{10,... | collective-permute-start | bytes 49160 | tf_op jit(solution)/shard_map/ppermute | solution.py:587
  55.0 6.3 %collective-permute-start.10 = (f32[32,128]{1,0:T(8,128)S(1)}, f32[32,128]{1,0:T(8,128)S(1)}, u32[]{:S(2)}, u32[]{:S(2)}) collective-permute-start(f32[32,128]{1,0:T(8,128)S(1)} %get-tuple-element.68), channel_id=1, source_target_pairs={{0,2},{1,3},{2,0},{3,1},{4,6},{5,7},{6,4},{7,5},{8,10},{9,11},{10,... | collective-permute-start | bytes 49160 | tf_op jit(solution)/shard_map/ppermute | solution.py:587
  56.1 5.2 %collective-permute-start.9 = (f32[32,128]{1,0:T(8,128)S(1)}, f32[32,128]{1,0:T(8,128)S(1)}, u32[]{:S(2)}, u32[]{:S(2)}) collective-permute-start(f32[32,128]{1,0:T(8,128)S(1)} %get-tuple-element.68), channel_id=1, source_target_pairs={{0,1},{1,0},{2,3},{3,2},{4,5},{5,4},{6,7},{7,6},{8,9},{9,8},{10,11... | collective-permute-start | bytes 49160 | tf_op jit(solution)/shard_map/ppermute | solution.py:587
  57.1 16.0 %collective-permute-start.15 = (bf16[528,128]{1,0:T(8,128)(2,1)S(1)}, bf16[528,128]{1,0:T(8,128)(2,1)S(1)}, u32[]{:S(2)}, u32[]{:S(2)}) collective-permute-start(bf16[528,128]{1,0:T(8,128)(2,1)S(1)} %get-tuple-element.79), channel_id=1, source_target_pairs={{0,2},{1,3},{2,0},{3,1},{4,6},{5,7},{6,4},{7,5},{8,10},{9,11},{10,... | collective-permute-start | bytes 405512 | tf_op jit(solution)/shard_map/ppermute | solution.py:587
  60.0 13.1 %collective-permute-start.16 = (bf16[528,128]{1,0:T(8,128)(2,1)S(1)}, bf16[528,128]{1,0:T(8,128)(2,1)S(1)}, u32[]{:S(2)}, u32[]{:S(2)}) collective-permute-start(bf16[528,128]{1,0:T(8,128)(2,1)S(1)} %get-tuple-element.80), channel_id=1, source_target_pairs={{0,3},{1,2},{2,1},{3,0},{4,7},{5,6},{6,5},{7,4},{8,11},{9,10},{10,... | collective-permute-start | bytes 405512 | tf_op jit(solution)/shard_map/ppermute | solution.py:587
  61.3 1.2 %collective-permute-start.12 = (f32[32,128]{1,0:T(8,128)S(1)}, f32[32,128]{1,0:T(8,128)S(1)}, u32[]{:S(2)}, u32[]{:S(2)}) collective-permute-start(f32[32,128]{1,0:T(8,128)S(1)} %add_add_fusion), channel_id=1, source_target_pairs={{0,4},{4,0},{8,12},{12,8},{16,20},{20,16},{24,28},{28,24},{1,5},{5... | collective-permute-start | bytes 49160 | tf_op jit(solution)/shard_map/ppermute | solution.py:587
  62.6 3.7 %collective-permute-start.13 = (f32[32,128]{1,0:T(8,128)S(1)}, f32[32,128]{1,0:T(8,128)S(1)}, u32[]{:S(2)}, u32[]{:S(2)}) collective-permute-start(f32[32,128]{1,0:T(8,128)S(1)} %add.72), channel_id=1, source_target_pairs={{0,8},{4,12},{8,0},{12,4},{16,24},{20,28},{24,16},{28,20},{1,9},{5... | collective-permute-start | bytes 49160 | tf_op jit(solution)/shard_map/ppermute | solution.py:587
  66.3 3.7 %collective-permute-start.14 = (f32[32,128]{1,0:T(8,128)S(1)}, f32[32,128]{1,0:T(8,128)S(1)}, u32[]{:S(2)}, u32[]{:S(2)}) collective-permute-start(f32[32,128]{1,0:T(8,128)S(1)} %add.73), channel_id=1, source_target_pairs={{0,16},{4,20},{8,24},{12,28},{16,0},{20,4},{24,8},{28,12},{1,17},{... | collective-permute-start | bytes 49160 | tf_op jit(solution)/shard_map/ppermute | solution.py:587
  73.1 18.9 %collective-permute-start.18 = (bf16[512,128]{1,0:T(8,128)(2,1)S(1)}, bf16[512,128]{1,0:T(8,128)(2,1)S(1)}, u32[]{:S(2)}, u32[]{:S(2)}) collective-permute-start(bf16[512,128]{1,0:T(8,128)(2,1)S(1)} %get-tuple-element.91), channel_id=1, source_target_pairs={{0,2},{1,3},{2,0},{3,1},{4,6},{5,7},{6,4},{7,5},{8,10},{9,11},{10,... | collective-permute-start | bytes 393224 | tf_op jit(solution)/shard_map/ppermute | solution.py:587
  74.1 18.0 %collective-permute-start.19 = (bf16[512,128]{1,0:T(8,128)(2,1)S(1)}, bf16[512,128]{1,0:T(8,128)(2,1)S(1)}, u32[]{:S(2)}, u32[]{:S(2)}) collective-permute-start(bf16[512,128]{1,0:T(8,128)(2,1)S(1)} %get-tuple-element.92), channel_id=1, source_target_pairs={{0,3},{1,2},{2,1},{3,0},{4,7},{5,6},{6,5},{7,4},{8,11},{9,10},{10,... | collective-permute-start | bytes 393224 | tf_op jit(solution)/shard_map/ppermute | solution.py:587
  75.8 10.1 %collective-permute-start.17 = (bf16[528,128]{1,0:T(8,128)(2,1)S(1)}, bf16[528,128]{1,0:T(8,128)(2,1)S(1)}, u32[]{:S(2)}, u32[]{:S(2)}) collective-permute-start(bf16[528,128]{1,0:T(8,128)(2,1)S(1)} %get-tuple-element.82), channel_id=1, source_target_pairs={{0,1},{1,0},{2,3},{3,2},{4,5},{5,4},{6,7},{7,6},{8,9},{9,8},{10,11... | collective-permute-start | bytes 405512 | tf_op jit(solution)/shard_map/ppermute | solution.py:587
  82.4 20.8 %collective-permute-start.21 = (bf16[2,512,128]{2,1,0:T(8,128)(2,1)S(1)}, bf16[2,512,128]{2,1,0:T(8,128)(2,1)S(1)}, u32[]{:S(2)}, u32[]{:S(2)}) collective-permute-start(bf16[2,512,128]{2,1,0:T(8,128)(2,1)S(1)} %get-tuple-element.95), channel_id=1, source_target_pairs={{0,2},{1,3},{2,0},{3,1},{4,6},{5,7},{6,4},{7,5},{8,10},{9,11},{10,... | collective-permute-start | bytes 786440 | tf_op jit(solution)/shard_map/ppermute | solution.py:587
  84.2 19.0 %collective-permute-start.22 = (bf16[2,512,128]{2,1,0:T(8,128)(2,1)S(1)}, bf16[2,512,128]{2,1,0:T(8,128)(2,1)S(1)}, u32[]{:S(2)}, u32[]{:S(2)}) collective-permute-start(bf16[2,512,128]{2,1,0:T(8,128)(2,1)S(1)} %get-tuple-element.96), channel_id=1, source_target_pairs={{0,3},{1,2},{2,1},{3,0},{4,7},{5,6},{6,5},{7,4},{8,11},{9,10},{10,... | collective-permute-start | bytes 786440 | tf_op jit(solution)/shard_map/ppermute | solution.py:587
  85.9 20.3 %collective-permute-start.20 = (bf16[3,512,128]{2,1,0:T(8,128)(2,1)S(1)}, bf16[3,512,128]{2,1,0:T(8,128)(2,1)S(1)}, u32[]{:S(2)}, u32[]{:S(2)}) collective-permute-start(bf16[3,512,128]{2,1,0:T(8,128)(2,1)S(1)} %get-tuple-element.94), channel_id=1, source_target_pairs={{0,1},{1,0},{2,3},{3,2},{4,5},{5,4},{6,7},{7,6},{8,9},{9,8},{10,11... | collective-permute-start | bytes 1179656 | tf_op jit(solution)/shard_map/ppermute | solution.py:587
  (11 other events, 165.4 us)

commit v5 on v4

--- a/solution.py
+++ b/solution.py
@@ -618,9 +618,11 @@
             return array
         return jnp.pad(array, ((0, 0),) * (array.ndim - 1) + ((0, width - narrow),))
 
-    def lane_parts(array):
+    def lane_parts(array, start=(), counts=()):
+        starts = start + (0,) * (array.ndim - 1 - len(start))
+        sizes = counts + array.shape[len(counts) : -1] + (narrow,)
         return [
-            lax.dynamic_slice_in_dim(array, (position ^ slot) * narrow, narrow, array.ndim - 1)
+            lax.dynamic_slice(array, starts + ((position ^ slot) * narrow,), sizes)
             for slot in range(shards)
         ]
 
@@ -652,8 +654,8 @@
     gain = widen(own_gain)
     mixer = widen(mixer_filter)
 
-    others = exchange_parts(lane_parts(streams[1:]))
-    query_parts = lane_parts(streams[0])
+    others = exchange_parts(lane_parts(streams, (1,), (2,)))
+    query_parts = [part[0] for part in lane_parts(streams, (0,), (1,))]
     others[1], query_parts = lax.optimization_barrier((others[1], query_parts))
     queries = exchange_parts(query_parts)
     grad_parts = lane_parts(out_grad)
@@ -725,8 +727,11 @@
         "norm",
         sems=shards,
     )
+    norm = list(norm)
+    first_piece = norm[4]
+    norm, gated_far, near_piece = lax.optimization_barrier((norm, gated_far, gated_pieces[1]))
+    norm[4] = first_piece
     d_query, d_response = norm[:2]
-    norm, gated_far, near_piece = lax.optimization_barrier((norm, gated_far, gated_pieces[1]))
     gated_back = to_tokens([gated_pieces[0], near_piece], [0, 1]) + gated_far
     query_back = to_tokens(norm[2:3] + norm[4:], [slot for slot in every_slot if slot != 1])
     back = run_kernel(

time: 108 us -> 107 us (level)
  starting transfers between devices: 34.5 us -> 33 us
    ppermute x23, starting transfers between devices: 34.5 us -> 33 us  [exchange(): lax.ppermute(array, axis, [(i, i ^ bits) for i in range(lax.axis_size(axi...]
    slice x4 -> x0, local copies, waits for them, and re-layouts: 1.2 us -> none  [the longest x2 1.2 us: body(): others = exchange_parts(lane_parts(streams[1:]))]
    squeeze x0 -> x1, local copies, waits for them, and re-layouts: none -> 1.15 us  [body(): query_parts = [part[0] for part in lane_parts(streams, (0,), (1,))]]
  transfers between devices with their start and end apart: 23 -> 23, of which waited for: 8 -> 10; matrix products, arithmetic and copies ran while one was open for 1% -> 2% of each run, Pallas kernels for 21% -> 21%
where the time goes in v5:
time: 107 us; the launch traced here: 106 us
  waiting for transfers between devices  43.6 us (41%)
  starting transfers between devices  33 us (31%)
  Pallas kernels  25 us (23%)
  local copies, waits for them, and re-layouts  3.29 us (3%)
    ppermute x23, waiting for transfers between devices, exchange(): lax.ppermute(array, axis, [(i, i ^ bits) for i in range(lax.axis_size(axi...  43.6 us
    ppermute x23, starting transfers between devices, exchange(): lax.ppermute(array, axis, [(i, i ^ bits) for i in range(lax.axis_size(axi...  33 us
    pallas_call x9, Pallas kernels, run_kernel(): pl.pallas_call(kernel, out_shape=[jax.ShapeDtypeStruct(s, d) for s, d, _...  25 us
  transfers between devices with their start and end apart: 23, of which 10 were waited for; matrix products, arithmetic and copies ran while one was open for 2% of the time, Pallas kernels for 21%

profile of v5, /device:TPU:0, one launch (start us, length us, event | category | flops | bytes accessed | tf_op | source)
XLA Modules:
  0.0 106.4 jit_solution(4294673034592479971)
XLA Ops:
  2.1 5.1 %collective-permute-start.8 = (bf16[2,512,128]{2,1,0:T(8,128)(2,1)S(1)}, bf16[2,512,128]{2,1,0:T(8,128)(2,1)S(1)}, u32[]{:S(2)}, u32[]{:S(2)}) collective-permute-start(bf16[2,512,128]{2,1,0:T(8,128)(2,1)S(1)} %get-tuple-element.122), channel_id=1, source_target_pairs={{0,3},{1,2},{2,1},{3,0},{4,7},{5,6},{6,5},{7,4},{8,11},{9,10},{10,... | collective-permute-start | bytes 786440 | tf_op jit(solution)/shard_map/ppermute | solution.py:587
  9.6 10.7 %collective-permute-done.refs_3_ = bf16[2,512,128]{2,1,0:T(8,128)(2,1)S(1)} collective-permute-done((bf16[2,512,128]{2,1,0:T(8,128)(2,1)S(1)}, bf16[2,512,128]{2,1,0:T(8,128)(2,1)S(1)}, u32[]{:S(2)}, u32[]{:S(2)}) %collective-permute-start) | collective-permute-done | bytes 262176 | tf_op jit(solution)/shard_map/ppermute | solution.py:587
  20.3 1.8 %collective-permute-start.1 = (bf16[512,128]{1,0:T(8,128)(2,1)S(1)}, bf16[512,128]{1,0:T(8,128)(2,1)S(1)}, u32[]{:S(2)}, u32[]{:S(2)}) collective-permute-start(bf16[512,128]{1,0:T(8,128)(2,1)S(1)} %get-tuple-element.55), channel_id=1, source_target_pairs={{0,1},{1,0},{2,3},{3,2},{4,5},{5,4},{6,7},{7,6},{8,9},{9,8},{10,11... | collective-permute-start | bytes 393224 | tf_op jit(solution)/shard_map/ppermute | solution.py:587
  22.9 2.0 %collective-permute-start.6 = (bf16[512,128]{1,0:T(8,128)(2,1)S(1)}, bf16[512,128]{1,0:T(8,128)(2,1)S(1)}, u32[]{:S(2)}, u32[]{:S(2)}) collective-permute-start(bf16[512,128]{1,0:T(8,128)(2,1)S(1)} %get-tuple-element.63), channel_id=1, source_target_pairs={{0,3},{1,2},{2,1},{3,0},{4,7},{5,6},{6,5},{7,4},{8,11},{9,10},{10,... | collective-permute-start | bytes 393224 | tf_op jit(solution)/shard_map/ppermute | solution.py:587
  24.9 3.2 %collective-permute-done.1.refs_3_ = bf16[512,128]{1,0:T(8,128)(2,1)S(1)} collective-permute-done((bf16[512,128]{1,0:T(8,128)(2,1)S(1)}, bf16[512,128]{1,0:T(8,128)(2,1)S(1)}, u32[]{:S(2)}, u32[]{:S(2)}) %collective-permute-start.1) | collective-permute-done | bytes 131104 | tf_op jit(solution)/shard_map/ppermute | solution.py:587
  28.1 2.4 %collective-permute-start.2 = (bf16[512,128]{1,0:T(8,128)(2,1)S(1)}, bf16[512,128]{1,0:T(8,128)(2,1)S(1)}, u32[]{:S(2)}, u32[]{:S(2)}) collective-permute-start(bf16[512,128]{1,0:T(8,128)(2,1)S(1)} %get-tuple-element.57), channel_id=1, source_target_pairs={{0,1},{1,0},{2,3},{3,2},{4,5},{5,4},{6,7},{7,6},{8,9},{9,8},{10,11... | collective-permute-start | bytes 393224 | tf_op jit(solution)/shard_map/ppermute | solution.py:587
  30.5 6.5 %collective-permute-done.7.refs_4_ = bf16[2,512,128]{2,1,0:T(8,128)(2,1)S(1)} collective-permute-done((bf16[2,512,128]{2,1,0:T(8,128)(2,1)S(1)}, bf16[2,512,128]{2,1,0:T(8,128)(2,1)S(1)}, u32[]{:S(2)}, u32[]{:S(2)}) %collective-permute-start.7) | collective-permute-done | bytes 262176 | tf_op jit(solution)/shard_map/ppermute | solution.py:587
  37.0 1.9 %collective-permute-start.4 = (bf16[512,128]{1,0:T(8,128)(2,1)S(1)}, bf16[512,128]{1,0:T(8,128)(2,1)S(1)}, u32[]{:S(2)}, u32[]{:S(2)}) collective-permute-start(bf16[512,128]{1,0:T(8,128)(2,1)S(1)} %get-tuple-element.59), channel_id=1, source_target_pairs={{0,3},{1,2},{2,1},{3,0},{4,7},{5,6},{6,5},{7,4},{8,11},{9,10},{10,... | collective-permute-start | bytes 393224 | tf_op jit(solution)/shard_map/ppermute | solution.py:587
  39.0 5.0 %respond.1 = (bf16[2,2048,128]{2,1,0:T(8,128)(2,1)S(1)}, bf16[2,2048,128]{2,1,0:T(8,128)(2,1)S(1)}, f32[2048,128]{1,0:T(8,128)S(1)}, f32[256,128]{1,0:T(8,128)S(1)}) custom-call(s32[128]{0:T(128)S(1)} %fusion.3.refs_0_, s32[3,16]{1,0:T(4,128)S(1)} %pad_add_fusion.refs_1_.refs_0_, bf16[2,512,128]{2,1,0:T(8,128)(2,1)S(1)} %get-tuple-element.123.refs_2_, ...), custom_call_target="tpu_custom_call" | custom-call | flops 6000000000 | tf_op jit(solution)/shard_map/respond/pallas_call | solution.py:572
  44.6 2.9 %gate.1 = (bf16[2048,128]{1,0:T(8,128)(2,1)S(1)}, bf16[2048,128]{1,0:T(8,128)(2,1)S(1)}, bf16[4,528,128]{2,1,0:T(8,128)(2,1)S(1)}, f32[16,128]{1,0:T(8,128)S(1)}) custom-call(s32[128]{0:T(128)S(1)} %fusion.3.refs_0_, s32[3,16]{1,0:T(4,128)S(1)} %pad_add_fusion.refs_1_.refs_0_, bf16[512,128]{1,0:T(8,128)(2,1)S(1)} %get-tuple-element.60.refs_2_, ...), custom_call_target="tpu_custom_call" | custom-call | flops 500000000 | tf_op jit(solution)/shard_map/gate/pallas_call | solution.py:572
  47.5 2.7 %collective-permute-done.3.refs_3_ = bf16[512,128]{1,0:T(8,128)(2,1)S(1)} collective-permute-done((bf16[512,128]{1,0:T(8,128)(2,1)S(1)}, bf16[512,128]{1,0:T(8,128)(2,1)S(1)}, u32[]{:S(2)}, u32[]{:S(2)}) %collective-permute-start.3) | collective-permute-done | bytes 131104 | tf_op jit(solution)/shard_map/ppermute | solution.py:587
  51.3 2.6 %collective-permute-start.11 = (f32[32,128]{1,0:T(8,128)S(1)}, f32[32,128]{1,0:T(8,128)S(1)}, u32[]{:S(2)}, u32[]{:S(2)}) collective-permute-start(f32[32,128]{1,0:T(8,128)S(1)} %get-tuple-element.69), channel_id=1, source_target_pairs={{0,3},{1,2},{2,1},{3,0},{4,7},{5,6},{6,5},{7,4},{8,11},{9,10},{10,... | collective-permute-start | bytes 49160 | tf_op jit(solution)/shard_map/ppermute | solution.py:587
  56.5 2.5 %collective-permute-start.15 = (bf16[528,128]{1,0:T(8,128)(2,1)S(1)}, bf16[528,128]{1,0:T(8,128)(2,1)S(1)}, u32[]{:S(2)}, u32[]{:S(2)}) collective-permute-start(bf16[528,128]{1,0:T(8,128)(2,1)S(1)} %get-tuple-element.80), channel_id=1, source_target_pairs={{0,2},{1,3},{2,0},{3,1},{4,6},{5,7},{6,4},{7,5},{8,10},{9,11},{10,... | collective-permute-start | bytes 405512 | tf_op jit(solution)/shard_map/ppermute | solution.py:587
  63.2 2.3 %collective-permute-done.13 = f32[32,128]{1,0:T(8,128)S(1)} collective-permute-done((f32[32,128]{1,0:T(8,128)S(1)}, f32[32,128]{1,0:T(8,128)S(1)}, u32[]{:S(2)}, u32[]{:S(2)}) %collective-permute-start.13) | collective-permute-done | bytes 16416 | tf_op jit(solution)/shard_map/ppermute | solution.py:587
  67.0 2.3 %collective-permute-done.14 = f32[32,128]{1,0:T(8,128)S(1)} collective-permute-done((f32[32,128]{1,0:T(8,128)S(1)}, f32[32,128]{1,0:T(8,128)S(1)}, u32[]{:S(2)}, u32[]{:S(2)}) %collective-permute-start.14) | collective-permute-done | bytes 16416 | tf_op jit(solution)/shard_map/ppermute | solution.py:587
  69.2 3.0 %norm.1 = (bf16[2048,128]{1,0:T(8,128)(2,1)S(1)}, bf16[2048,128]{1,0:T(8,128)(2,1)S(1)}, bf16[512,128]{1,0:T(8,128)(2,1)S(1)}, bf16[512,128]{1,0:T(8,128)(2,1)S(...) custom-call(s32[128]{0:T(128)S(1)} %fusion.3.refs_0_, s32[3,16]{1,0:T(4,128)S(1)} %pad_add_fusion.refs_1_.refs_0_, ...), custom_call_target="tpu_custom_call" | custom-call | flops 200000000 | tf_op jit(solution)/shard_map/norm/pallas_call | solution.py:572
  73.0 1.7 %collective-permute-start.19 = (bf16[512,128]{1,0:T(8,128)(2,1)S(1)}, bf16[512,128]{1,0:T(8,128)(2,1)S(1)}, u32[]{:S(2)}, u32[]{:S(2)}) collective-permute-start(bf16[512,128]{1,0:T(8,128)(2,1)S(1)} %get-tuple-element.93), channel_id=1, source_target_pairs={{0,3},{1,2},{2,1},{3,0},{4,7},{5,6},{6,5},{7,4},{8,11},{9,10},{10,... | collective-permute-start | bytes 393224 | tf_op jit(solution)/shard_map/ppermute | solution.py:587
  75.8 5.7 %mix_back.1 = (f32[128,128]{1,0:T(8,128)}, bf16[2,2048,128]{2,1,0:T(8,128)(2,1)S(1)}, bf16[2,512,128]{2,1,0:T(8,128)(2,1)S(1)}, bf16[3,512,128]{2,1,0:T(8,128)(2...) custom-call(s32[128]{0:T(128)S(1)} %fusion.3.refs_0_, ...), custom_call_target="tpu_custom_call" | custom-call | flops 7000000000 | tf_op jit(solution)/shard_map/mix_back/pallas_call | solution.py:572
  81.5 1.7 %collective-permute-start.21 = (bf16[2,512,128]{2,1,0:T(8,128)(2,1)S(1)}, bf16[2,512,128]{2,1,0:T(8,128)(2,1)S(1)}, u32[]{:S(2)}, u32[]{:S(2)}) collective-permute-start(bf16[2,512,128]{2,1,0:T(8,128)(2,1)S(1)} %get-tuple-element.96), channel_id=1, source_target_pairs={{0,2},{1,3},{2,0},{3,1},{4,6},{5,7},{6,4},{7,5},{8,10},{9,11},{10,... | collective-permute-start | bytes 786440 | tf_op jit(solution)/shard_map/ppermute | solution.py:587
  83.2 1.7 %collective-permute-start.22 = (bf16[2,512,128]{2,1,0:T(8,128)(2,1)S(1)}, bf16[2,512,128]{2,1,0:T(8,128)(2,1)S(1)}, u32[]{:S(2)}, u32[]{:S(2)}) collective-permute-start(bf16[2,512,128]{2,1,0:T(8,128)(2,1)S(1)} %get-tuple-element.97), channel_id=1, source_target_pairs={{0,3},{1,2},{2,1},{3,0},{4,7},{5,6},{6,5},{7,4},{8,11},{9,10},{10,... | collective-permute-start | bytes 786440 | tf_op jit(solution)/shard_map/ppermute | solution.py:587
  85.0 3.7 %tap_grad.1 = (f32[21,128]{1,0:T(8,128)S(1)}, f32[1,128]{1,0:T(1,128)}) custom-call(s32[128]{0:T(128)S(1)} %fusion.3.refs_0_, s32[3,16]{1,0:T(4,128)S(1)} %pad_add_fusion.refs_1_.refs_0_, bf16[2048,128]{1,0:T(8,128)(2,1)S(1)} %get-tuple-element.99.refs_2_, bf16[2,2048,128]{2,1,0:T(8,128)(2,1)S(1)} %get-tuple-element.100.refs_3_, ...), custom_call_target="tpu_custom_call" | custom-call | flops 4000000000 | tf_op jit(solution)/shard_map/tap_grad/pallas_call | solution.py:572
  89.3 1.9 %scale_out.1 = bf16[512,512]{1,0:T(8,128)(2,1)} custom-call(s32[3,16]{1,0:T(4,128)S(1)} %pad_add_fusion.refs_1_.refs_0_, s32[1]{0:T(128)} %bitcast.5.refs_0_.refs_1_, f32[32,128]{1,0:T(8,128)S(1)} %add.74.refs_8_.refs_2_, bf16[528,128]{1,0:T(8,128)(2,1)S(1)} %get-tuple-element.71.refs_3_, bf16[528,128]{1,0:T(8,128)(2,1)S(1)} %collective-permute-done.17.refs_4_, ...), custom_call_target="tpu_custom_call" | custom-call | flops 2000000000 | tf_op jit(solution)/shard_map/scale_out/pallas_call | solution.py:572
  91.2 11.0 %collective-permute-done.21.refs_6_ = bf16[2,512,128]{2,1,0:T(8,128)(2,1)S(1)} collective-permute-done((bf16[2,512,128]{2,1,0:T(8,128)(2,1)S(1)}, bf16[2,512,128]{2,1,0:T(8,128)(2,1)S(1)}, u32[]{:S(2)}, u32[]{:S(2)}) %collective-permute-start.21) | collective-permute-done | bytes 262176 | tf_op jit(solution)/shard_map/ppermute | solution.py:587
  102.2 3.0 %collective-permute-done.20.refs_5_ = bf16[3,512,128]{2,1,0:T(8,128)(2,1)S(1)} collective-permute-done((bf16[3,512,128]{2,1,0:T(8,128)(2,1)S(1)}, bf16[3,512,128]{2,1,0:T(8,128)(2,1)S(1)}, u32[]{:S(2)}, u32[]{:S(2)}) %collective-permute-start.20) | collective-permute-done | bytes 393248 | tf_op jit(solution)/shard_map/ppermute | solution.py:587
  (73 shorter events, 18.2 us)
Async XLA Ops:
  2.1 36.9 %copy-start.1 = (f32[128,128]{1,0:T(8,128)S(1)}, f32[128,128]{1,0:T(8,128)}, u32[]{:S(2)}) copy-start(f32[128,128]{1,0:T(8,128)} %refs_7_.1) | copy-start | bytes 196612
  2.1 28.4 %collective-permute-start.8 = (bf16[2,512,128]{2,1,0:T(8,128)(2,1)S(1)}, bf16[2,512,128]{2,1,0:T(8,128)(2,1)S(1)}, u32[]{:S(2)}, u32[]{:S(2)}) collective-permute-start(bf16[2,512,128]{2,1,0:T(8,128)(2,1)S(1)} %get-tuple-element.122), channel_id=1, source_target_pairs={{0,3},{1,2},{2,1},{3,0},{4,7},{5,6},{6,5},{7,4},{8,11},{9,10},{10,... | collective-permute-start | bytes 786440 | tf_op jit(solution)/shard_map/ppermute | solution.py:587
  7.2 13.1 %collective-permute-start = (bf16[2,512,128]{2,1,0:T(8,128)(2,1)S(1)}, bf16[2,512,128]{2,1,0:T(8,128)(2,1)S(1)}, u32[]{:S(2)}, u32[]{:S(2)}) collective-permute-start(bf16[2,512,128]{2,1,0:T(8,128)(2,1)S(1)} %get-tuple-element.124), channel_id=1, source_target_pairs={{0,1},{1,0},{2,3},{3,2},{4,5},{5,4},{6,7},{7,6},{8,9},{9,8},{10,11... | collective-permute-start | bytes 786440 | tf_op jit(solution)/shard_map/ppermute | solution.py:587
  7.2 29.8 %collective-permute-start.7 = (bf16[2,512,128]{2,1,0:T(8,128)(2,1)S(1)}, bf16[2,512,128]{2,1,0:T(8,128)(2,1)S(1)}, u32[]{:S(2)}, u32[]{:S(2)}) collective-permute-start(bf16[2,512,128]{2,1,0:T(8,128)(2,1)S(1)} %get-tuple-element.125), channel_id=1, source_target_pairs={{0,2},{1,3},{2,0},{3,1},{4,6},{5,7},{6,4},{7,5},{8,10},{9,11},{10,... | collective-permute-start | bytes 786440 | tf_op jit(solution)/shard_map/ppermute | solution.py:587
  20.3 7.9 %collective-permute-start.1 = (bf16[512,128]{1,0:T(8,128)(2,1)S(1)}, bf16[512,128]{1,0:T(8,128)(2,1)S(1)}, u32[]{:S(2)}, u32[]{:S(2)}) collective-permute-start(bf16[512,128]{1,0:T(8,128)(2,1)S(1)} %get-tuple-element.55), channel_id=1, source_target_pairs={{0,1},{1,0},{2,3},{3,2},{4,5},{5,4},{6,7},{7,6},{8,9},{9,8},{10,11... | collective-permute-start | bytes 393224 | tf_op jit(solution)/shard_map/ppermute | solution.py:587
  22.2 22.4 %collective-permute-start.5 = (bf16[512,128]{1,0:T(8,128)(2,1)S(1)}, bf16[512,128]{1,0:T(8,128)(2,1)S(1)}, u32[]{:S(2)}, u32[]{:S(2)}) collective-permute-start(bf16[512,128]{1,0:T(8,128)(2,1)S(1)} %get-tuple-element.62), channel_id=1, source_target_pairs={{0,2},{1,3},{2,0},{3,1},{4,6},{5,7},{6,4},{7,5},{8,10},{9,11},{10,... | collective-permute-start | bytes 393224 | tf_op jit(solution)/shard_map/ppermute | solution.py:587
  22.9 21.8 %collective-permute-start.6 = (bf16[512,128]{1,0:T(8,128)(2,1)S(1)}, bf16[512,128]{1,0:T(8,128)(2,1)S(1)}, u32[]{:S(2)}, u32[]{:S(2)}) collective-permute-start(bf16[512,128]{1,0:T(8,128)(2,1)S(1)} %get-tuple-element.63), channel_id=1, source_target_pairs={{0,3},{1,2},{2,1},{3,0},{4,7},{5,6},{6,5},{7,4},{8,11},{9,10},{10,... | collective-permute-start | bytes 393224 | tf_op jit(solution)/shard_map/ppermute | solution.py:587
  28.1 19.4 %collective-permute-start.2 = (bf16[512,128]{1,0:T(8,128)(2,1)S(1)}, bf16[512,128]{1,0:T(8,128)(2,1)S(1)}, u32[]{:S(2)}, u32[]{:S(2)}) collective-permute-start(bf16[512,128]{1,0:T(8,128)(2,1)S(1)} %get-tuple-element.57), channel_id=1, source_target_pairs={{0,1},{1,0},{2,3},{3,2},{4,5},{5,4},{6,7},{7,6},{8,9},{9,8},{10,11... | collective-permute-start | bytes 393224 | tf_op jit(solution)/shard_map/ppermute | solution.py:587
  30.5 19.7 %collective-permute-start.3 = (bf16[512,128]{1,0:T(8,128)(2,1)S(1)}, bf16[512,128]{1,0:T(8,128)(2,1)S(1)}, u32[]{:S(2)}, u32[]{:S(2)}) collective-permute-start(bf16[512,128]{1,0:T(8,128)(2,1)S(1)} %get-tuple-element.58), channel_id=1, source_target_pairs={{0,2},{1,3},{2,0},{3,1},{4,6},{5,7},{6,4},{7,5},{8,10},{9,11},{10,... | collective-permute-start | bytes 393224 | tf_op jit(solution)/shard_map/ppermute | solution.py:587
  37.0 13.2 %collective-permute-start.4 = (bf16[512,128]{1,0:T(8,128)(2,1)S(1)}, bf16[512,128]{1,0:T(8,128)(2,1)S(1)}, u32[]{:S(2)}, u32[]{:S(2)}) collective-permute-start(bf16[512,128]{1,0:T(8,128)(2,1)S(1)} %get-tuple-element.59), channel_id=1, source_target_pairs={{0,3},{1,2},{2,1},{3,0},{4,7},{5,6},{6,5},{7,4},{8,11},{9,10},{10,... | collective-permute-start | bytes 393224 | tf_op jit(solution)/shard_map/ppermute | solution.py:587
  51.3 9.1 %collective-permute-start.11 = (f32[32,128]{1,0:T(8,128)S(1)}, f32[32,128]{1,0:T(8,128)S(1)}, u32[]{:S(2)}, u32[]{:S(2)}) collective-permute-start(f32[32,128]{1,0:T(8,128)S(1)} %get-tuple-element.69), channel_id=1, source_target_pairs={{0,3},{1,2},{2,1},{3,0},{4,7},{5,6},{6,5},{7,4},{8,11},{9,10},{10,... | collective-permute-start | bytes 49160 | tf_op jit(solution)/shard_map/ppermute | solution.py:587
  54.0 6.5 %collective-permute-start.10 = (f32[32,128]{1,0:T(8,128)S(1)}, f32[32,128]{1,0:T(8,128)S(1)}, u32[]{:S(2)}, u32[]{:S(2)}) collective-permute-start(f32[32,128]{1,0:T(8,128)S(1)} %get-tuple-element.69), channel_id=1, source_target_pairs={{0,2},{1,3},{2,0},{3,1},{4,6},{5,7},{6,4},{7,5},{8,10},{9,11},{10,... | collective-permute-start | bytes 49160 | tf_op jit(solution)/shard_map/ppermute | solution.py:587
  55.3 5.2 %collective-permute-start.9 = (f32[32,128]{1,0:T(8,128)S(1)}, f32[32,128]{1,0:T(8,128)S(1)}, u32[]{:S(2)}, u32[]{:S(2)}) collective-permute-start(f32[32,128]{1,0:T(8,128)S(1)} %get-tuple-element.69), channel_id=1, source_target_pairs={{0,1},{1,0},{2,3},{3,2},{4,5},{5,4},{6,7},{7,6},{8,9},{9,8},{10,11... | collective-permute-start | bytes 49160 | tf_op jit(solution)/shard_map/ppermute | solution.py:587
  56.5 16.5 %collective-permute-start.15 = (bf16[528,128]{1,0:T(8,128)(2,1)S(1)}, bf16[528,128]{1,0:T(8,128)(2,1)S(1)}, u32[]{:S(2)}, u32[]{:S(2)}) collective-permute-start(bf16[528,128]{1,0:T(8,128)(2,1)S(1)} %get-tuple-element.80), channel_id=1, source_target_pairs={{0,2},{1,3},{2,0},{3,1},{4,6},{5,7},{6,4},{7,5},{8,10},{9,11},{10,... | collective-permute-start | bytes 405512 | tf_op jit(solution)/shard_map/ppermute | solution.py:587
  59.0 14.0 %collective-permute-start.16 = (bf16[528,128]{1,0:T(8,128)(2,1)S(1)}, bf16[528,128]{1,0:T(8,128)(2,1)S(1)}, u32[]{:S(2)}, u32[]{:S(2)}) collective-permute-start(bf16[528,128]{1,0:T(8,128)(2,1)S(1)} %get-tuple-element.81), channel_id=1, source_target_pairs={{0,3},{1,2},{2,1},{3,0},{4,7},{5,6},{6,5},{7,4},{8,11},{9,10},{10,... | collective-permute-start | bytes 405512 | tf_op jit(solution)/shard_map/ppermute | solution.py:587
  60.5 1.2 %collective-permute-start.12 = (f32[32,128]{1,0:T(8,128)S(1)}, f32[32,128]{1,0:T(8,128)S(1)}, u32[]{:S(2)}, u32[]{:S(2)}) collective-permute-start(f32[32,128]{1,0:T(8,128)S(1)} %add_add_fusion), channel_id=1, source_target_pairs={{0,4},{4,0},{8,12},{12,8},{16,20},{20,16},{24,28},{28,24},{1,5},{5... | collective-permute-start | bytes 49160 | tf_op jit(solution)/shard_map/ppermute | solution.py:587
  61.7 3.7 %collective-permute-start.13 = (f32[32,128]{1,0:T(8,128)S(1)}, f32[32,128]{1,0:T(8,128)S(1)}, u32[]{:S(2)}, u32[]{:S(2)}) collective-permute-start(f32[32,128]{1,0:T(8,128)S(1)} %add.72), channel_id=1, source_target_pairs={{0,8},{4,12},{8,0},{12,4},{16,24},{20,28},{24,16},{28,20},{1,9},{5... | collective-permute-start | bytes 49160 | tf_op jit(solution)/shard_map/ppermute | solution.py:587
  65.5 3.7 %collective-permute-start.14 = (f32[32,128]{1,0:T(8,128)S(1)}, f32[32,128]{1,0:T(8,128)S(1)}, u32[]{:S(2)}, u32[]{:S(2)}) collective-permute-start(f32[32,128]{1,0:T(8,128)S(1)} %add.73), channel_id=1, source_target_pairs={{0,16},{4,20},{8,24},{12,28},{16,0},{20,4},{24,8},{28,12},{1,17},{... | collective-permute-start | bytes 49160 | tf_op jit(solution)/shard_map/ppermute | solution.py:587
  72.2 18.9 %collective-permute-start.18 = (bf16[512,128]{1,0:T(8,128)(2,1)S(1)}, bf16[512,128]{1,0:T(8,128)(2,1)S(1)}, u32[]{:S(2)}, u32[]{:S(2)}) collective-permute-start(bf16[512,128]{1,0:T(8,128)(2,1)S(1)} %get-tuple-element.78), channel_id=1, source_target_pairs={{0,2},{1,3},{2,0},{3,1},{4,6},{5,7},{6,4},{7,5},{8,10},{9,11},{10,... | collective-permute-start | bytes 393224 | tf_op jit(solution)/shard_map/ppermute | solution.py:587
  73.0 18.1 %collective-permute-start.19 = (bf16[512,128]{1,0:T(8,128)(2,1)S(1)}, bf16[512,128]{1,0:T(8,128)(2,1)S(1)}, u32[]{:S(2)}, u32[]{:S(2)}) collective-permute-start(bf16[512,128]{1,0:T(8,128)(2,1)S(1)} %get-tuple-element.93), channel_id=1, source_target_pairs={{0,3},{1,2},{2,1},{3,0},{4,7},{5,6},{6,5},{7,4},{8,11},{9,10},{10,... | collective-permute-start | bytes 393224 | tf_op jit(solution)/shard_map/ppermute | solution.py:587
  74.8 10.1 %collective-permute-start.17 = (bf16[528,128]{1,0:T(8,128)(2,1)S(1)}, bf16[528,128]{1,0:T(8,128)(2,1)S(1)}, u32[]{:S(2)}, u32[]{:S(2)}) collective-permute-start(bf16[528,128]{1,0:T(8,128)(2,1)S(1)} %get-tuple-element.83), channel_id=1, source_target_pairs={{0,1},{1,0},{2,3},{3,2},{4,5},{5,4},{6,7},{7,6},{8,9},{9,8},{10,11... | collective-permute-start | bytes 405512 | tf_op jit(solution)/shard_map/ppermute | solution.py:587
  81.5 20.7 %collective-permute-start.21 = (bf16[2,512,128]{2,1,0:T(8,128)(2,1)S(1)}, bf16[2,512,128]{2,1,0:T(8,128)(2,1)S(1)}, u32[]{:S(2)}, u32[]{:S(2)}) collective-permute-start(bf16[2,512,128]{2,1,0:T(8,128)(2,1)S(1)} %get-tuple-element.96), channel_id=1, source_target_pairs={{0,2},{1,3},{2,0},{3,1},{4,6},{5,7},{6,4},{7,5},{8,10},{9,11},{10,... | collective-permute-start | bytes 786440 | tf_op jit(solution)/shard_map/ppermute | solution.py:587
  83.2 19.0 %collective-permute-start.22 = (bf16[2,512,128]{2,1,0:T(8,128)(2,1)S(1)}, bf16[2,512,128]{2,1,0:T(8,128)(2,1)S(1)}, u32[]{:S(2)}, u32[]{:S(2)}) collective-permute-start(bf16[2,512,128]{2,1,0:T(8,128)(2,1)S(1)} %get-tuple-element.97), channel_id=1, source_target_pairs={{0,3},{1,2},{2,1},{3,0},{4,7},{5,6},{6,5},{7,4},{8,11},{9,10},{10,... | collective-permute-start | bytes 786440 | tf_op jit(solution)/shard_map/ppermute | solution.py:587
  84.9 20.3 %collective-permute-start.20 = (bf16[3,512,128]{2,1,0:T(8,128)(2,1)S(1)}, bf16[3,512,128]{2,1,0:T(8,128)(2,1)S(1)}, u32[]{:S(2)}, u32[]{:S(2)}) collective-permute-start(bf16[3,512,128]{2,1,0:T(8,128)(2,1)S(1)} %get-tuple-element.95), channel_id=1, source_target_pairs={{0,1},{1,0},{2,3},{3,2},{4,5},{5,4},{6,7},{7,6},{8,9},{9,8},{10,11... | collective-permute-start | bytes 1179656 | tf_op jit(solution)/shard_map/ppermute | solution.py:587
  (9 other events, 163.6 us)

commit v6 on v5

--- a/solution.py
+++ b/solution.py
@@ -367,17 +367,17 @@
         spread_rows = spread(ahead_ref.at[block + 1], taps_ref, 0)
         store_units(grad_ref, unit_ref, block, spread_rows)
 
-    scale_block(blocks - 1, 0)
-    scale_block(blocks - 2, 1)
+    for offset in range(4):
+        scale_block(blocks - 1 - offset, offset)
 
     def both(index, offset):
-        block = blocks - 3 - index
+        block = blocks - 5 - index
         scale_block(block, offset)
-        spread_block(block + 2, offset)
-
-    repeat(blocks - 2, 2, both)
-    spread_block(1, 0)
-    spread_block(0, 1)
+        spread_block(block + 4, offset)
+
+    repeat(blocks - 4, 4, both)
+    for offset in range(4):
+        spread_block(3 - offset, offset)
     send_slots(grad_ref, leaving, rows, sems)
 
 
@@ -587,14 +587,14 @@
     return lax.ppermute(array, axis, [(i, i ^ bits) for i in range(lax.axis_size(axis))])
 
 
-def butterfly(sums, axis, radix):
-    step = 1
-    while step < lax.axis_size(axis):
-        radix = min(radix, lax.axis_size(axis) // step)
+def butterfly(sums, axis, radices):
+    length, step, radix = lax.axis_size(axis), 1, radices[0]
+    while step < length:
         others = [exchange(sums, axis, step * k) for k in range(1, radix)]
         for other in others:
             sums = sums + other
         step *= radix
+        radix = min(radices[1], max(length // step, 1))
     return sums
 
 
@@ -714,9 +714,9 @@
         "pack",
         sems=shards,
     )
-    sums = butterfly(sums, "seq", 4)
+    sums = butterfly(sums, "seq", (4, 4))
     gated_far = to_tokens(gated_pieces[2:], every_slot[2:])
-    sums = butterfly(sums, "fsdp", 2)
+    sums = butterfly(sums, "fsdp", (2, 2))
     norm = run_kernel(
         lambda *refs: norm_kernel(total_channels, shards, rows, *refs),
         scalars,

time: 107 us -> 107 us (level)
  no operation moved by 1% of the time
where the time goes in v6:
time: 107 us; the launch traced here: 106 us
  waiting for transfers between devices  43.6 us (41%)
  starting transfers between devices  33 us (31%)
  Pallas kernels  24.8 us (23%)
  local copies, waits for them, and re-layouts  3.29 us (3%)
    ppermute x23, waiting for transfers between devices, exchange(): lax.ppermute(array, axis, [(i, i ^ bits) for i in range(lax.axis_size(axi...  43.6 us
    ppermute x23, starting transfers between devices, exchange(): lax.ppermute(array, axis, [(i, i ^ bits) for i in range(lax.axis_size(axi...  33 us
    pallas_call x9, Pallas kernels, run_kernel(): pl.pallas_call(kernel, out_shape=[jax.ShapeDtypeStruct(s, d) for s, d, _...  24.8 us
  transfers between devices with their start and end apart: 23, of which 10 were waited for; matrix products, arithmetic and copies ran while one was open for 2% of the time, Pallas kernels for 21%

profile of v6, /device:TPU:0, one launch (start us, length us, event | category | flops | bytes accessed | tf_op | source)
XLA Modules:
  0.0 106.2 jit_solution(11321950947210279979)
XLA Ops:
  2.1 5.1 %collective-permute-start.8 = (bf16[2,512,128]{2,1,0:T(8,128)(2,1)S(1)}, bf16[2,512,128]{2,1,0:T(8,128)(2,1)S(1)}, u32[]{:S(2)}, u32[]{:S(2)}) collective-permute-start(bf16[2,512,128]{2,1,0:T(8,128)(2,1)S(1)} %get-tuple-element.122), channel_id=1, source_target_pairs={{0,3},{1,2},{2,1},{3,0},{4,7},{5,6},{6,5},{7,4},{8,11},{9,10},{10,... | collective-permute-start | bytes 786440 | tf_op jit(solution)/shard_map/ppermute | solution.py:587
  9.6 10.7 %collective-permute-done.refs_3_ = bf16[2,512,128]{2,1,0:T(8,128)(2,1)S(1)} collective-permute-done((bf16[2,512,128]{2,1,0:T(8,128)(2,1)S(1)}, bf16[2,512,128]{2,1,0:T(8,128)(2,1)S(1)}, u32[]{:S(2)}, u32[]{:S(2)}) %collective-permute-start) | collective-permute-done | bytes 262176 | tf_op jit(solution)/shard_map/ppermute | solution.py:587
  20.3 1.8 %collective-permute-start.1 = (bf16[512,128]{1,0:T(8,128)(2,1)S(1)}, bf16[512,128]{1,0:T(8,128)(2,1)S(1)}, u32[]{:S(2)}, u32[]{:S(2)}) collective-permute-start(bf16[512,128]{1,0:T(8,128)(2,1)S(1)} %get-tuple-element.55), channel_id=1, source_target_pairs={{0,1},{1,0},{2,3},{3,2},{4,5},{5,4},{6,7},{7,6},{8,9},{9,8},{10,11... | collective-permute-start | bytes 393224 | tf_op jit(solution)/shard_map/ppermute | solution.py:587
  22.9 2.0 %collective-permute-start.6 = (bf16[512,128]{1,0:T(8,128)(2,1)S(1)}, bf16[512,128]{1,0:T(8,128)(2,1)S(1)}, u32[]{:S(2)}, u32[]{:S(2)}) collective-permute-start(bf16[512,128]{1,0:T(8,128)(2,1)S(1)} %get-tuple-element.63), channel_id=1, source_target_pairs={{0,3},{1,2},{2,1},{3,0},{4,7},{5,6},{6,5},{7,4},{8,11},{9,10},{10,... | collective-permute-start | bytes 393224 | tf_op jit(solution)/shard_map/ppermute | solution.py:587
  24.9 3.2 %collective-permute-done.1.refs_3_ = bf16[512,128]{1,0:T(8,128)(2,1)S(1)} collective-permute-done((bf16[512,128]{1,0:T(8,128)(2,1)S(1)}, bf16[512,128]{1,0:T(8,128)(2,1)S(1)}, u32[]{:S(2)}, u32[]{:S(2)}) %collective-permute-start.1) | collective-permute-done | bytes 131104 | tf_op jit(solution)/shard_map/ppermute | solution.py:587
  28.1 2.4 %collective-permute-start.2 = (bf16[512,128]{1,0:T(8,128)(2,1)S(1)}, bf16[512,128]{1,0:T(8,128)(2,1)S(1)}, u32[]{:S(2)}, u32[]{:S(2)}) collective-permute-start(bf16[512,128]{1,0:T(8,128)(2,1)S(1)} %get-tuple-element.57), channel_id=1, source_target_pairs={{0,1},{1,0},{2,3},{3,2},{4,5},{5,4},{6,7},{7,6},{8,9},{9,8},{10,11... | collective-permute-start | bytes 393224 | tf_op jit(solution)/shard_map/ppermute | solution.py:587
  30.5 6.5 %collective-permute-done.7.refs_4_ = bf16[2,512,128]{2,1,0:T(8,128)(2,1)S(1)} collective-permute-done((bf16[2,512,128]{2,1,0:T(8,128)(2,1)S(1)}, bf16[2,512,128]{2,1,0:T(8,128)(2,1)S(1)}, u32[]{:S(2)}, u32[]{:S(2)}) %collective-permute-start.7) | collective-permute-done | bytes 262176 | tf_op jit(solution)/shard_map/ppermute | solution.py:587
  37.0 1.9 %collective-permute-start.4 = (bf16[512,128]{1,0:T(8,128)(2,1)S(1)}, bf16[512,128]{1,0:T(8,128)(2,1)S(1)}, u32[]{:S(2)}, u32[]{:S(2)}) collective-permute-start(bf16[512,128]{1,0:T(8,128)(2,1)S(1)} %get-tuple-element.59), channel_id=1, source_target_pairs={{0,3},{1,2},{2,1},{3,0},{4,7},{5,6},{6,5},{7,4},{8,11},{9,10},{10,... | collective-permute-start | bytes 393224 | tf_op jit(solution)/shard_map/ppermute | solution.py:587
  39.0 5.0 %respond.1 = (bf16[2,2048,128]{2,1,0:T(8,128)(2,1)S(1)}, bf16[2,2048,128]{2,1,0:T(8,128)(2,1)S(1)}, f32[2048,128]{1,0:T(8,128)S(1)}, f32[256,128]{1,0:T(8,128)S(1)}) custom-call(s32[128]{0:T(128)S(1)} %fusion.3.refs_0_, s32[3,16]{1,0:T(4,128)S(1)} %pad_add_fusion.refs_1_.refs_0_, bf16[2,512,128]{2,1,0:T(8,128)(2,1)S(1)} %get-tuple-element.123.refs_2_, ...), custom_call_target="tpu_custom_call" | custom-call | flops 6000000000 | tf_op jit(solution)/shard_map/respond/pallas_call | solution.py:572
  44.6 2.9 %gate.1 = (bf16[2048,128]{1,0:T(8,128)(2,1)S(1)}, bf16[2048,128]{1,0:T(8,128)(2,1)S(1)}, bf16[4,528,128]{2,1,0:T(8,128)(2,1)S(1)}, f32[16,128]{1,0:T(8,128)S(1)}) custom-call(s32[128]{0:T(128)S(1)} %fusion.3.refs_0_, s32[3,16]{1,0:T(4,128)S(1)} %pad_add_fusion.refs_1_.refs_0_, bf16[512,128]{1,0:T(8,128)(2,1)S(1)} %get-tuple-element.60.refs_2_, ...), custom_call_target="tpu_custom_call" | custom-call | flops 500000000 | tf_op jit(solution)/shard_map/gate/pallas_call | solution.py:572
  47.5 2.7 %collective-permute-done.3.refs_3_ = bf16[512,128]{1,0:T(8,128)(2,1)S(1)} collective-permute-done((bf16[512,128]{1,0:T(8,128)(2,1)S(1)}, bf16[512,128]{1,0:T(8,128)(2,1)S(1)}, u32[]{:S(2)}, u32[]{:S(2)}) %collective-permute-start.3) | collective-permute-done | bytes 131104 | tf_op jit(solution)/shard_map/ppermute | solution.py:587
  51.3 2.6 %collective-permute-start.11 = (f32[32,128]{1,0:T(8,128)S(1)}, f32[32,128]{1,0:T(8,128)S(1)}, u32[]{:S(2)}, u32[]{:S(2)}) collective-permute-start(f32[32,128]{1,0:T(8,128)S(1)} %get-tuple-element.69), channel_id=1, source_target_pairs={{0,3},{1,2},{2,1},{3,0},{4,7},{5,6},{6,5},{7,4},{8,11},{9,10},{10,... | collective-permute-start | bytes 49160 | tf_op jit(solution)/shard_map/ppermute | solution.py:587
  56.5 2.5 %collective-permute-start.15 = (bf16[528,128]{1,0:T(8,128)(2,1)S(1)}, bf16[528,128]{1,0:T(8,128)(2,1)S(1)}, u32[]{:S(2)}, u32[]{:S(2)}) collective-permute-start(bf16[528,128]{1,0:T(8,128)(2,1)S(1)} %get-tuple-element.80), channel_id=1, source_target_pairs={{0,2},{1,3},{2,0},{3,1},{4,6},{5,7},{6,4},{7,5},{8,10},{9,11},{10,... | collective-permute-start | bytes 405512 | tf_op jit(solution)/shard_map/ppermute | solution.py:587
  63.2 2.3 %collective-permute-done.13 = f32[32,128]{1,0:T(8,128)S(1)} collective-permute-done((f32[32,128]{1,0:T(8,128)S(1)}, f32[32,128]{1,0:T(8,128)S(1)}, u32[]{:S(2)}, u32[]{:S(2)}) %collective-permute-start.13) | collective-permute-done | bytes 16416 | tf_op jit(solution)/shard_map/ppermute | solution.py:587
  67.0 2.3 %collective-permute-done.14 = f32[32,128]{1,0:T(8,128)S(1)} collective-permute-done((f32[32,128]{1,0:T(8,128)S(1)}, f32[32,128]{1,0:T(8,128)S(1)}, u32[]{:S(2)}, u32[]{:S(2)}) %collective-permute-start.14) | collective-permute-done | bytes 16416 | tf_op jit(solution)/shard_map/ppermute | solution.py:587
  69.2 2.8 %norm.1 = (bf16[2048,128]{1,0:T(8,128)(2,1)S(1)}, bf16[2048,128]{1,0:T(8,128)(2,1)S(1)}, bf16[512,128]{1,0:T(8,128)(2,1)S(1)}, bf16[512,128]{1,0:T(8,128)(2,1)S(...) custom-call(s32[128]{0:T(128)S(1)} %fusion.3.refs_0_, s32[3,16]{1,0:T(4,128)S(1)} %pad_add_fusion.refs_1_.refs_0_, ...), custom_call_target="tpu_custom_call" | custom-call | flops 200000000 | tf_op jit(solution)/shard_map/norm/pallas_call | solution.py:572
  72.9 1.7 %collective-permute-start.19 = (bf16[512,128]{1,0:T(8,128)(2,1)S(1)}, bf16[512,128]{1,0:T(8,128)(2,1)S(1)}, u32[]{:S(2)}, u32[]{:S(2)}) collective-permute-start(bf16[512,128]{1,0:T(8,128)(2,1)S(1)} %get-tuple-element.93), channel_id=1, source_target_pairs={{0,3},{1,2},{2,1},{3,0},{4,7},{5,6},{6,5},{7,4},{8,11},{9,10},{10,... | collective-permute-start | bytes 393224 | tf_op jit(solution)/shard_map/ppermute | solution.py:587
  75.6 5.7 %mix_back.1 = (f32[128,128]{1,0:T(8,128)}, bf16[2,2048,128]{2,1,0:T(8,128)(2,1)S(1)}, bf16[2,512,128]{2,1,0:T(8,128)(2,1)S(1)}, bf16[3,512,128]{2,1,0:T(8,128)(2...) custom-call(s32[128]{0:T(128)S(1)} %fusion.3.refs_0_, ...), custom_call_target="tpu_custom_call" | custom-call | flops 7000000000 | tf_op jit(solution)/shard_map/mix_back/pallas_call | solution.py:572
  81.3 1.7 %collective-permute-start.21 = (bf16[2,512,128]{2,1,0:T(8,128)(2,1)S(1)}, bf16[2,512,128]{2,1,0:T(8,128)(2,1)S(1)}, u32[]{:S(2)}, u32[]{:S(2)}) collective-permute-start(bf16[2,512,128]{2,1,0:T(8,128)(2,1)S(1)} %get-tuple-element.96), channel_id=1, source_target_pairs={{0,2},{1,3},{2,0},{3,1},{4,6},{5,7},{6,4},{7,5},{8,10},{9,11},{10,... | collective-permute-start | bytes 786440 | tf_op jit(solution)/shard_map/ppermute | solution.py:587
  83.0 1.7 %collective-permute-start.22 = (bf16[2,512,128]{2,1,0:T(8,128)(2,1)S(1)}, bf16[2,512,128]{2,1,0:T(8,128)(2,1)S(1)}, u32[]{:S(2)}, u32[]{:S(2)}) collective-permute-start(bf16[2,512,128]{2,1,0:T(8,128)(2,1)S(1)} %get-tuple-element.97), channel_id=1, source_target_pairs={{0,3},{1,2},{2,1},{3,0},{4,7},{5,6},{6,5},{7,4},{8,11},{9,10},{10,... | collective-permute-start | bytes 786440 | tf_op jit(solution)/shard_map/ppermute | solution.py:587
  84.9 3.7 %tap_grad.1 = (f32[21,128]{1,0:T(8,128)S(1)}, f32[1,128]{1,0:T(1,128)}) custom-call(s32[128]{0:T(128)S(1)} %fusion.3.refs_0_, s32[3,16]{1,0:T(4,128)S(1)} %pad_add_fusion.refs_1_.refs_0_, bf16[2048,128]{1,0:T(8,128)(2,1)S(1)} %get-tuple-element.99.refs_2_, bf16[2,2048,128]{2,1,0:T(8,128)(2,1)S(1)} %get-tuple-element.100.refs_3_, ...), custom_call_target="tpu_custom_call" | custom-call | flops 4000000000 | tf_op jit(solution)/shard_map/tap_grad/pallas_call | solution.py:572
  89.1 1.9 %scale_out.1 = bf16[512,512]{1,0:T(8,128)(2,1)} custom-call(s32[3,16]{1,0:T(4,128)S(1)} %pad_add_fusion.refs_1_.refs_0_, s32[1]{0:T(128)} %bitcast.5.refs_0_.refs_1_, f32[32,128]{1,0:T(8,128)S(1)} %add.74.refs_8_.refs_2_, bf16[528,128]{1,0:T(8,128)(2,1)S(1)} %get-tuple-element.71.refs_3_, bf16[528,128]{1,0:T(8,128)(2,1)S(1)} %collective-permute-done.17.refs_4_, ...), custom_call_target="tpu_custom_call" | custom-call | flops 2000000000 | tf_op jit(solution)/shard_map/scale_out/pallas_call | solution.py:572
  91.0 11.0 %collective-permute-done.21.refs_6_ = bf16[2,512,128]{2,1,0:T(8,128)(2,1)S(1)} collective-permute-done((bf16[2,512,128]{2,1,0:T(8,128)(2,1)S(1)}, bf16[2,512,128]{2,1,0:T(8,128)(2,1)S(1)}, u32[]{:S(2)}, u32[]{:S(2)}) %collective-permute-start.21) | collective-permute-done | bytes 262176 | tf_op jit(solution)/shard_map/ppermute | solution.py:587
  102.0 3.0 %collective-permute-done.20.refs_5_ = bf16[3,512,128]{2,1,0:T(8,128)(2,1)S(1)} collective-permute-done((bf16[3,512,128]{2,1,0:T(8,128)(2,1)S(1)}, bf16[3,512,128]{2,1,0:T(8,128)(2,1)S(1)}, u32[]{:S(2)}, u32[]{:S(2)}) %collective-permute-start.20) | collective-permute-done | bytes 393248 | tf_op jit(solution)/shard_map/ppermute | solution.py:587
  (73 shorter events, 18.2 us)
Async XLA Ops:
  2.1 36.9 %copy-start.1 = (f32[128,128]{1,0:T(8,128)S(1)}, f32[128,128]{1,0:T(8,128)}, u32[]{:S(2)}) copy-start(f32[128,128]{1,0:T(8,128)} %refs_7_.1) | copy-start | bytes 196612
  2.1 28.4 %collective-permute-start.8 = (bf16[2,512,128]{2,1,0:T(8,128)(2,1)S(1)}, bf16[2,512,128]{2,1,0:T(8,128)(2,1)S(1)}, u32[]{:S(2)}, u32[]{:S(2)}) collective-permute-start(bf16[2,512,128]{2,1,0:T(8,128)(2,1)S(1)} %get-tuple-element.122), channel_id=1, source_target_pairs={{0,3},{1,2},{2,1},{3,0},{4,7},{5,6},{6,5},{7,4},{8,11},{9,10},{10,... | collective-permute-start | bytes 786440 | tf_op jit(solution)/shard_map/ppermute | solution.py:587
  7.2 13.1 %collective-permute-start = (bf16[2,512,128]{2,1,0:T(8,128)(2,1)S(1)}, bf16[2,512,128]{2,1,0:T(8,128)(2,1)S(1)}, u32[]{:S(2)}, u32[]{:S(2)}) collective-permute-start(bf16[2,512,128]{2,1,0:T(8,128)(2,1)S(1)} %get-tuple-element.124), channel_id=1, source_target_pairs={{0,1},{1,0},{2,3},{3,2},{4,5},{5,4},{6,7},{7,6},{8,9},{9,8},{10,11... | collective-permute-start | bytes 786440 | tf_op jit(solution)/shard_map/ppermute | solution.py:587
  7.2 29.8 %collective-permute-start.7 = (bf16[2,512,128]{2,1,0:T(8,128)(2,1)S(1)}, bf16[2,512,128]{2,1,0:T(8,128)(2,1)S(1)}, u32[]{:S(2)}, u32[]{:S(2)}) collective-permute-start(bf16[2,512,128]{2,1,0:T(8,128)(2,1)S(1)} %get-tuple-element.125), channel_id=1, source_target_pairs={{0,2},{1,3},{2,0},{3,1},{4,6},{5,7},{6,4},{7,5},{8,10},{9,11},{10,... | collective-permute-start | bytes 786440 | tf_op jit(solution)/shard_map/ppermute | solution.py:587
  20.3 7.9 %collective-permute-start.1 = (bf16[512,128]{1,0:T(8,128)(2,1)S(1)}, bf16[512,128]{1,0:T(8,128)(2,1)S(1)}, u32[]{:S(2)}, u32[]{:S(2)}) collective-permute-start(bf16[512,128]{1,0:T(8,128)(2,1)S(1)} %get-tuple-element.55), channel_id=1, source_target_pairs={{0,1},{1,0},{2,3},{3,2},{4,5},{5,4},{6,7},{7,6},{8,9},{9,8},{10,11... | collective-permute-start | bytes 393224 | tf_op jit(solution)/shard_map/ppermute | solution.py:587
  22.2 22.4 %collective-permute-start.5 = (bf16[512,128]{1,0:T(8,128)(2,1)S(1)}, bf16[512,128]{1,0:T(8,128)(2,1)S(1)}, u32[]{:S(2)}, u32[]{:S(2)}) collective-permute-start(bf16[512,128]{1,0:T(8,128)(2,1)S(1)} %get-tuple-element.62), channel_id=1, source_target_pairs={{0,2},{1,3},{2,0},{3,1},{4,6},{5,7},{6,4},{7,5},{8,10},{9,11},{10,... | collective-permute-start | bytes 393224 | tf_op jit(solution)/shard_map/ppermute | solution.py:587
  22.9 21.8 %collective-permute-start.6 = (bf16[512,128]{1,0:T(8,128)(2,1)S(1)}, bf16[512,128]{1,0:T(8,128)(2,1)S(1)}, u32[]{:S(2)}, u32[]{:S(2)}) collective-permute-start(bf16[512,128]{1,0:T(8,128)(2,1)S(1)} %get-tuple-element.63), channel_id=1, source_target_pairs={{0,3},{1,2},{2,1},{3,0},{4,7},{5,6},{6,5},{7,4},{8,11},{9,10},{10,... | collective-permute-start | bytes 393224 | tf_op jit(solution)/shard_map/ppermute | solution.py:587
  28.1 19.4 %collective-permute-start.2 = (bf16[512,128]{1,0:T(8,128)(2,1)S(1)}, bf16[512,128]{1,0:T(8,128)(2,1)S(1)}, u32[]{:S(2)}, u32[]{:S(2)}) collective-permute-start(bf16[512,128]{1,0:T(8,128)(2,1)S(1)} %get-tuple-element.57), channel_id=1, source_target_pairs={{0,1},{1,0},{2,3},{3,2},{4,5},{5,4},{6,7},{7,6},{8,9},{9,8},{10,11... | collective-permute-start | bytes 393224 | tf_op jit(solution)/shard_map/ppermute | solution.py:587
  30.5 19.7 %collective-permute-start.3 = (bf16[512,128]{1,0:T(8,128)(2,1)S(1)}, bf16[512,128]{1,0:T(8,128)(2,1)S(1)}, u32[]{:S(2)}, u32[]{:S(2)}) collective-permute-start(bf16[512,128]{1,0:T(8,128)(2,1)S(1)} %get-tuple-element.58), channel_id=1, source_target_pairs={{0,2},{1,3},{2,0},{3,1},{4,6},{5,7},{6,4},{7,5},{8,10},{9,11},{10,... | collective-permute-start | bytes 393224 | tf_op jit(solution)/shard_map/ppermute | solution.py:587
  37.0 13.2 %collective-permute-start.4 = (bf16[512,128]{1,0:T(8,128)(2,1)S(1)}, bf16[512,128]{1,0:T(8,128)(2,1)S(1)}, u32[]{:S(2)}, u32[]{:S(2)}) collective-permute-start(bf16[512,128]{1,0:T(8,128)(2,1)S(1)} %get-tuple-element.59), channel_id=1, source_target_pairs={{0,3},{1,2},{2,1},{3,0},{4,7},{5,6},{6,5},{7,4},{8,11},{9,10},{10,... | collective-permute-start | bytes 393224 | tf_op jit(solution)/shard_map/ppermute | solution.py:587
  51.3 9.1 %collective-permute-start.11 = (f32[32,128]{1,0:T(8,128)S(1)}, f32[32,128]{1,0:T(8,128)S(1)}, u32[]{:S(2)}, u32[]{:S(2)}) collective-permute-start(f32[32,128]{1,0:T(8,128)S(1)} %get-tuple-element.69), channel_id=1, source_target_pairs={{0,3},{1,2},{2,1},{3,0},{4,7},{5,6},{6,5},{7,4},{8,11},{9,10},{10,... | collective-permute-start | bytes 49160 | tf_op jit(solution)/shard_map/ppermute | solution.py:587
  54.0 6.5 %collective-permute-start.10 = (f32[32,128]{1,0:T(8,128)S(1)}, f32[32,128]{1,0:T(8,128)S(1)}, u32[]{:S(2)}, u32[]{:S(2)}) collective-permute-start(f32[32,128]{1,0:T(8,128)S(1)} %get-tuple-element.69), channel_id=1, source_target_pairs={{0,2},{1,3},{2,0},{3,1},{4,6},{5,7},{6,4},{7,5},{8,10},{9,11},{10,... | collective-permute-start | bytes 49160 | tf_op jit(solution)/shard_map/ppermute | solution.py:587
  55.3 5.2 %collective-permute-start.9 = (f32[32,128]{1,0:T(8,128)S(1)}, f32[32,128]{1,0:T(8,128)S(1)}, u32[]{:S(2)}, u32[]{:S(2)}) collective-permute-start(f32[32,128]{1,0:T(8,128)S(1)} %get-tuple-element.69), channel_id=1, source_target_pairs={{0,1},{1,0},{2,3},{3,2},{4,5},{5,4},{6,7},{7,6},{8,9},{9,8},{10,11... | collective-permute-start | bytes 49160 | tf_op jit(solution)/shard_map/ppermute | solution.py:587
  56.5 16.3 %collective-permute-start.15 = (bf16[528,128]{1,0:T(8,128)(2,1)S(1)}, bf16[528,128]{1,0:T(8,128)(2,1)S(1)}, u32[]{:S(2)}, u32[]{:S(2)}) collective-permute-start(bf16[528,128]{1,0:T(8,128)(2,1)S(1)} %get-tuple-element.80), channel_id=1, source_target_pairs={{0,2},{1,3},{2,0},{3,1},{4,6},{5,7},{6,4},{7,5},{8,10},{9,11},{10,... | collective-permute-start | bytes 405512 | tf_op jit(solution)/shard_map/ppermute | solution.py:587
  59.0 13.8 %collective-permute-start.16 = (bf16[528,128]{1,0:T(8,128)(2,1)S(1)}, bf16[528,128]{1,0:T(8,128)(2,1)S(1)}, u32[]{:S(2)}, u32[]{:S(2)}) collective-permute-start(bf16[528,128]{1,0:T(8,128)(2,1)S(1)} %get-tuple-element.81), channel_id=1, source_target_pairs={{0,3},{1,2},{2,1},{3,0},{4,7},{5,6},{6,5},{7,4},{8,11},{9,10},{10,... | collective-permute-start | bytes 405512 | tf_op jit(solution)/shard_map/ppermute | solution.py:587
  60.5 1.2 %collective-permute-start.12 = (f32[32,128]{1,0:T(8,128)S(1)}, f32[32,128]{1,0:T(8,128)S(1)}, u32[]{:S(2)}, u32[]{:S(2)}) collective-permute-start(f32[32,128]{1,0:T(8,128)S(1)} %add_add_fusion), channel_id=1, source_target_pairs={{0,4},{4,0},{8,12},{12,8},{16,20},{20,16},{24,28},{28,24},{1,5},{5... | collective-permute-start | bytes 49160 | tf_op jit(solution)/shard_map/ppermute | solution.py:587
  61.7 3.7 %collective-permute-start.13 = (f32[32,128]{1,0:T(8,128)S(1)}, f32[32,128]{1,0:T(8,128)S(1)}, u32[]{:S(2)}, u32[]{:S(2)}) collective-permute-start(f32[32,128]{1,0:T(8,128)S(1)} %add.72), channel_id=1, source_target_pairs={{0,8},{4,12},{8,0},{12,4},{16,24},{20,28},{24,16},{28,20},{1,9},{5... | collective-permute-start | bytes 49160 | tf_op jit(solution)/shard_map/ppermute | solution.py:587
  65.5 3.7 %collective-permute-start.14 = (f32[32,128]{1,0:T(8,128)S(1)}, f32[32,128]{1,0:T(8,128)S(1)}, u32[]{:S(2)}, u32[]{:S(2)}) collective-permute-start(f32[32,128]{1,0:T(8,128)S(1)} %add.73), channel_id=1, source_target_pairs={{0,16},{4,20},{8,24},{12,28},{16,0},{20,4},{24,8},{28,12},{1,17},{... | collective-permute-start | bytes 49160 | tf_op jit(solution)/shard_map/ppermute | solution.py:587
  72.0 18.9 %collective-permute-start.18 = (bf16[512,128]{1,0:T(8,128)(2,1)S(1)}, bf16[512,128]{1,0:T(8,128)(2,1)S(1)}, u32[]{:S(2)}, u32[]{:S(2)}) collective-permute-start(bf16[512,128]{1,0:T(8,128)(2,1)S(1)} %get-tuple-element.78), channel_id=1, source_target_pairs={{0,2},{1,3},{2,0},{3,1},{4,6},{5,7},{6,4},{7,5},{8,10},{9,11},{10,... | collective-permute-start | bytes 393224 | tf_op jit(solution)/shard_map/ppermute | solution.py:587
  72.9 18.1 %collective-permute-start.19 = (bf16[512,128]{1,0:T(8,128)(2,1)S(1)}, bf16[512,128]{1,0:T(8,128)(2,1)S(1)}, u32[]{:S(2)}, u32[]{:S(2)}) collective-permute-start(bf16[512,128]{1,0:T(8,128)(2,1)S(1)} %get-tuple-element.93), channel_id=1, source_target_pairs={{0,3},{1,2},{2,1},{3,0},{4,7},{5,6},{6,5},{7,4},{8,11},{9,10},{10,... | collective-permute-start | bytes 393224 | tf_op jit(solution)/shard_map/ppermute | solution.py:587
  74.6 10.1 %collective-permute-start.17 = (bf16[528,128]{1,0:T(8,128)(2,1)S(1)}, bf16[528,128]{1,0:T(8,128)(2,1)S(1)}, u32[]{:S(2)}, u32[]{:S(2)}) collective-permute-start(bf16[528,128]{1,0:T(8,128)(2,1)S(1)} %get-tuple-element.83), channel_id=1, source_target_pairs={{0,1},{1,0},{2,3},{3,2},{4,5},{5,4},{6,7},{7,6},{8,9},{9,8},{10,11... | collective-permute-start | bytes 405512 | tf_op jit(solution)/shard_map/ppermute | solution.py:587
  81.3 20.7 %collective-permute-start.21 = (bf16[2,512,128]{2,1,0:T(8,128)(2,1)S(1)}, bf16[2,512,128]{2,1,0:T(8,128)(2,1)S(1)}, u32[]{:S(2)}, u32[]{:S(2)}) collective-permute-start(bf16[2,512,128]{2,1,0:T(8,128)(2,1)S(1)} %get-tuple-element.96), channel_id=1, source_target_pairs={{0,2},{1,3},{2,0},{3,1},{4,6},{5,7},{6,4},{7,5},{8,10},{9,11},{10,... | collective-permute-start | bytes 786440 | tf_op jit(solution)/shard_map/ppermute | solution.py:587
  83.0 19.0 %collective-permute-start.22 = (bf16[2,512,128]{2,1,0:T(8,128)(2,1)S(1)}, bf16[2,512,128]{2,1,0:T(8,128)(2,1)S(1)}, u32[]{:S(2)}, u32[]{:S(2)}) collective-permute-start(bf16[2,512,128]{2,1,0:T(8,128)(2,1)S(1)} %get-tuple-element.97), channel_id=1, source_target_pairs={{0,3},{1,2},{2,1},{3,0},{4,7},{5,6},{6,5},{7,4},{8,11},{9,10},{10,... | collective-permute-start | bytes 786440 | tf_op jit(solution)/shard_map/ppermute | solution.py:587
  84.7 20.3 %collective-permute-start.20 = (bf16[3,512,128]{2,1,0:T(8,128)(2,1)S(1)}, bf16[3,512,128]{2,1,0:T(8,128)(2,1)S(1)}, u32[]{:S(2)}, u32[]{:S(2)}) collective-permute-start(bf16[3,512,128]{2,1,0:T(8,128)(2,1)S(1)} %get-tuple-element.95), channel_id=1, source_target_pairs={{0,1},{1,0},{2,3},{3,2},{4,5},{5,4},{6,7},{7,6},{8,9},{9,8},{10,11... | collective-permute-start | bytes 1179656 | tf_op jit(solution)/shard_map/ppermute | solution.py:587
  (9 other events, 163.4 us)
